TPU v7x, 32 devices: a whole 2x2x4 slice. The times are simulated.
32 devices in a mesh: section: 2 (over core), dp: 4 (over z), seq: 4 (over y, x).
Axes of the slice: x: 2, y: 2, z: 4, core: 2. Of those that a mesh axis runs over, the one named last changes fastest.
Arguments:
- ends: bfloat16 [2, 2, 4, 1024, 1024], P('section', None, 'dp', 'seq'), may hold values from -6 to 6
- mixer_input_weight: bfloat16 [2, 1024, 3072], P('section', 'dp'), may hold values from -0.1875 to 0.1875
- forget_first_map: bfloat16 [2, 1024, 16], P('section', 'dp'), may hold values from -0.1875 to 0.1875
- forget_second_map: bfloat16 [2, 16, 512], P('section'), may hold values from -1.5 to 1.5
- forget_logit_bias: float32 [2, 512], P('section'), may hold values from -2 to 6
- mixer_output_weight: bfloat16 [2, 1024, 1024], P('section', 'dp'), may hold values from -0.1875 to 0.1875
- feedforward_input_weight: bfloat16 [2, 1024, 5632], P('section', 'dp'), may hold values from -0.1875 to 0.1875
- feedforward_output_weight: bfloat16 [2, 2816, 1024], P('section', 'dp'), may hold values from -0.109375 to 0.109375
- adapter_model_first: bfloat16 [2, 1024, 768], P('section'), may hold values from -0.1875 to 0.1875
- adapter_hidden_first: bfloat16 [2, 3840, 128], P('section'), may hold values from -0.125 to 0.125
- adapter_second_maps: bfloat16 [2, 128, 10752], P('section'), may hold values from -0.75 to 0.75
- lengths: int32 [2, 4], P(None, 'dp'), may hold values from 256 to 1024, as said below
- dealt_block_order: int32 [2, 4, 16], P(None, 'dp'), may hold values from 0 to 15, each once within a row
- adapter_choice_per_seq: int32 [2, 4], P(None, 'dp'), may hold values from 0 to 7
Outputs:
- results: bfloat16 [2, 2, 4, 1024, 1024], P('section', None, 'dp', 'seq')
- grad_lora_model: float32 [2, 1024, 768], P('section', None, ('dp', 'seq'))
- grad_lora_hidden: float32 [2, 3840, 128], P('section', None, ('dp', 'seq'))
- grad_lora_up: float32 [2, 128, 10752], P('section', None, ('dp', 'seq'))
Inputs may be any that keep to these rules, and one draw needn't show every extreme that they name: `lengths`: in every micro-batch some sequence has 1024 live positions. `dealt_block_order`: each row is a permutation of the block numbers.
All inputs are finite; a program needn't handle non-finite values.
Results may differ from a plain program's by a relative error of at most 0.025.
Values may be sent and summed in bfloat16 or wider, within the bound.
A program may use at most 384 MiB of HBM per device.

v0:
```python
import jax
import jax.numpy as jnp
from jax import lax
from jax.sharding import PartitionSpec as P

MODEL_WIDTH = 1024
HEADS = 4
KEY = 512
VALUE_WIDTH = 1024
HIDDEN_UNITS = 2816
GROUP = 64
ADAPTER_RANK = 16
ADAPTERS = 8
ADAPTER_COLUMNS = 128


def as_sent(x):
    return jax.tree.map(lambda a: a.astype(jnp.bfloat16) if a.dtype == jnp.float32 else a, x)


def passed_along(block, axis, distance):
    devices = range(lax.axis_size(axis))
    route = [(i - distance, i) for i in devices if i - distance in devices]
    return lax.ppermute(block, axis, route)


def matrix_product(left, right):
    return jnp.dot(left, right, preferred_element_type=jnp.float32)


def times_trans(left, right):
    return lax.dot_general(
        left, right, (((1,), (1,)), ((), ())), preferred_element_type=jnp.float32
    )


def trans_times(left, right):
    return lax.dot_general(
        left, right, (((0,), (0,)), ((), ())), preferred_element_type=jnp.float32
    )


def rms_norm(values, epsilon):
    return values * lax.rsqrt(jnp.mean(values * values, axis=-1, keepdims=True) + epsilon)


def rms_back(values, grad):
    _, pullback = jax.vjp(lambda tensor: rms_norm(tensor, 1e-06), values)
    return pullback(grad)[0]


def all_spans():
    frozen_base = 2 * KEY + 2 * VALUE_WIDTH
    mixer_column_ranges = (
        (0, KEY),
        (KEY, KEY),
        (2 * KEY, VALUE_WIDTH),
        (2 * KEY + VALUE_WIDTH, VALUE_WIDTH),
    )
    feedforward_ranges = ((frozen_base, HIDDEN_UNITS), (frozen_base + HIDDEN_UNITS, HIDDEN_UNITS))
    return (
        mixer_column_ranges,
        feedforward_ranges,
        ((frozen_base + 2 * HIDDEN_UNITS, MODEL_WIDTH),),
        ((frozen_base + 2 * HIDDEN_UNITS + MODEL_WIDTH, MODEL_WIDTH),),
    )


def describe(seq_length, order_row, adapter_pick):
    group_count = order_row.shape[0]
    offsets = jnp.arange(GROUP, dtype=jnp.int32)
    positions = jnp.arange(group_count, dtype=jnp.int32)
    dealt_tokens = (order_row[:, None] * GROUP + offsets[None, :]).reshape(-1)
    inverse = jnp.sum(
        positions[:, None] * (order_row[:, None] == positions[None, :]).astype(jnp.int32), axis=0
    )
    source_tokens = (inverse[:, None] * GROUP + offsets[None, :]).reshape(-1)
    live = (jnp.arange(group_count * GROUP, dtype=jnp.int32) < seq_length).astype(jnp.float32)
    adapter_select_mask = (
        jnp.arange(ADAPTERS * ADAPTER_RANK, dtype=jnp.int32) // ADAPTER_RANK == adapter_pick
    ).astype(jnp.float32)
    return (adapter_select_mask, source_tokens, dealt_tokens, live)


def sequence_info(lengths, dealt_block_order, adapter_choice_per_seq, micro_index):
    return describe(
        lengths[micro_index, 0],
        dealt_block_order[micro_index, 0],
        adapter_choice_per_seq[micro_index, 0],
    )


def head_mix(queries, keys, values, forget, source_tokens, dealt_tokens, live):
    key_dim = KEY // HEADS
    value_dim = VALUE_WIDTH // HEADS
    seq_total = queries.shape[0]
    head_count = queries.shape[1] // key_dim
    block_count = seq_total // GROUP
    highest = lax.Precision.HIGHEST
    queries = jnp.take(queries, source_tokens, axis=0) * key_dim ** (-0.5)
    keys = jnp.take(keys, source_tokens, axis=0) * live[:, None]
    values = jnp.take(values, source_tokens, axis=0)
    forget = jnp.take(forget, source_tokens, axis=0)
    queries = queries.reshape(block_count, GROUP, head_count, key_dim)
    keys = keys.reshape(block_count, GROUP, head_count, key_dim)
    values = values.reshape(block_count, GROUP, head_count, value_dim)
    forget = forget.reshape(block_count, GROUP, head_count, key_dim)
    summed = jnp.cumsum(forget, axis=1)
    middle = summed[:, GROUP // 2 : GROUP // 2 + 1]
    block_total = summed[:, -1]
    scores = jnp.einsum(
        "nihk,njhk->nhij",
        queries * jnp.exp(summed - middle),
        keys * jnp.exp(middle - summed),
        precision=highest,
    )
    causal = (
        jnp.arange(GROUP, dtype=jnp.int32)[:, None] >= jnp.arange(GROUP, dtype=jnp.int32)[None, :]
    ).astype(jnp.float32)
    inner = jnp.einsum("nhij,njhv->nihv", scores * causal, values, precision=highest)
    update = jnp.einsum(
        "njhk,njhv->nhkv", keys * jnp.exp(block_total[:, None] - summed), values, precision=highest
    )

    def advance(state, inputs_now):
        decay, addend = inputs_now
        return (decay[..., None] * state + addend, state)

    _, states = lax.scan(
        advance,
        jnp.zeros((head_count, key_dim, value_dim), jnp.float32),
        (jnp.exp(block_total), update),
    )
    cross = jnp.einsum("nihk,nhkv->nihv", queries * jnp.exp(summed), states, precision=highest)
    layer_result = (inner + cross).reshape(seq_total, head_count, value_dim)
    layer_result = layer_result * lax.rsqrt(
        jnp.mean(layer_result * layer_result, axis=-1, keepdims=True) + 1.0
    )
    return jnp.take(layer_result.reshape(seq_total, head_count * value_dim), dealt_tokens, axis=0)


def adapter_forward(values, down, up, spans, adapter_select_mask):
    rank_block = down.shape[1] // len(spans)
    adapted = (matrix_product(values, down) * jnp.tile(adapter_select_mask, len(spans))).astype(
        jnp.bfloat16
    )
    pieces = []
    for block_index, (col_start, col_width) in enumerate(spans):
        pieces.append(
            matrix_product(
                adapted[:, block_index * rank_block : (block_index + 1) * rank_block],
                up[:, col_start : col_start + col_width],
            )
        )
    return (jnp.concatenate(pieces, axis=1), adapted)


def low_rank_back(grad, values, adapted, down, up, spans, adapter_select_mask):
    rank_block = down.shape[1] // len(spans)
    back_parts = []
    up_parts = []
    offset = 0
    for block_index, (col_start, col_width) in enumerate(spans):
        grad_block = grad[:, offset : offset + col_width]
        back_parts.append(times_trans(grad_block, up[:, col_start : col_start + col_width]))
        up_parts.append(
            trans_times(
                adapted[:, block_index * rank_block : (block_index + 1) * rank_block], grad_block
            )
        )
        offset = offset + col_width
    grad_adapted = jnp.concatenate(back_parts, axis=1).astype(jnp.bfloat16) * jnp.tile(
        adapter_select_mask, len(spans)
    ).astype(jnp.bfloat16)
    return (
        times_trans(grad_adapted, down),
        trans_times(values, grad_adapted),
        jnp.concatenate(up_parts, axis=1),
    )


def layer_forward_pass(
    residual_stream, weight_tree, rank_features, adapter_params, sequence_details
):
    (
        mixer_input_weight,
        forget_first_map,
        mixer_output_weight,
        feedforward_input_weight,
        feedforward_output_weight,
    ) = weight_tree
    forget_second_map, forget_logit_bias = rank_features
    adapter_model_first, adapter_hidden_first, adapter_second_maps = adapter_params
    adapter_select_mask, source_tokens, dealt_tokens, live = sequence_details
    mixer_column_ranges, feedforward_ranges, output_column_range, down_column_range = all_spans()
    normalized_input = rms_norm(residual_stream, 1e-06).astype(jnp.bfloat16)
    extra_mix, adapt_mix = adapter_forward(
        normalized_input,
        adapter_model_first[:, : 4 * ADAPTER_COLUMNS],
        adapter_second_maps,
        mixer_column_ranges,
        adapter_select_mask,
    )
    projected_features = matrix_product(normalized_input, mixer_input_weight) + extra_mix
    out_gate = projected_features[:, 2 * KEY + VALUE_WIDTH :]
    gate_low = matrix_product(normalized_input, forget_first_map).astype(jnp.bfloat16)
    gate_logit = matrix_product(gate_low, forget_second_map) + forget_logit_bias
    forget = jax.nn.log_sigmoid(gate_logit) / 16.0
    outgoing = (
        projected_features[:, :KEY].astype(jnp.bfloat16),
        projected_features[:, KEY : 2 * KEY].astype(jnp.bfloat16),
        projected_features[:, 2 * KEY : 2 * KEY + VALUE_WIDTH].astype(jnp.bfloat16),
        forget.astype(jnp.bfloat16),
    )
    head_inputs = (
        lax.all_to_all(outgoing[0], "seq", split_axis=1, concat_axis=0, tiled=True),
        lax.all_to_all(outgoing[1], "seq", split_axis=1, concat_axis=0, tiled=True),
        lax.all_to_all(outgoing[2], "seq", split_axis=1, concat_axis=0, tiled=True),
        lax.all_to_all(outgoing[3], "seq", split_axis=1, concat_axis=0, tiled=True),
    )
    mixed_head = head_mix(
        *[tensor.astype(jnp.float32) for tensor in head_inputs], source_tokens, dealt_tokens, live
    )
    mixed_tok = lax.all_to_all(
        mixed_head.astype(jnp.bfloat16), "seq", split_axis=0, concat_axis=1, tiled=True
    )
    gated_output = (mixed_tok.astype(jnp.float32) * jax.nn.silu(out_gate)).astype(jnp.bfloat16)
    output_adapter_extra, adapter_output_proj = adapter_forward(
        gated_output,
        adapter_hidden_first[:VALUE_WIDTH],
        adapter_second_maps,
        output_column_range,
        adapter_select_mask,
    )
    resid_mid = (
        residual_stream + matrix_product(gated_output, mixer_output_weight) + output_adapter_extra
    )
    normalized_middle = rms_norm(resid_mid, 1e-06).astype(jnp.bfloat16)
    extra_ffn, adapt_ffn = adapter_forward(
        normalized_middle,
        adapter_model_first[:, 4 * ADAPTER_COLUMNS :],
        adapter_second_maps,
        feedforward_ranges,
        adapter_select_mask,
    )
    gate_and_up = matrix_product(normalized_middle, feedforward_input_weight) + extra_ffn
    hidden_features = (
        jax.nn.silu(gate_and_up[:, :HIDDEN_UNITS]) * gate_and_up[:, HIDDEN_UNITS:]
    ).astype(jnp.bfloat16)
    down_adapter_extra, adapter_down_proj = adapter_forward(
        hidden_features,
        adapter_hidden_first[VALUE_WIDTH:],
        adapter_second_maps,
        down_column_range,
        adapter_select_mask,
    )
    layer_result = (
        resid_mid + matrix_product(hidden_features, feedforward_output_weight) + down_adapter_extra
    )
    saved_record = (
        residual_stream,
        normalized_input,
        adapt_mix,
        out_gate,
        gate_logit,
        head_inputs,
        mixed_tok,
        gated_output,
        adapter_output_proj,
        resid_mid,
        normalized_middle,
        adapt_ffn,
        gate_and_up,
        hidden_features,
        adapter_down_proj,
    )
    return (layer_result, saved_record)


def layer_backward_pass(
    output_gradient, saved_record, weight_tree, rank_features, adapter_params, sequence_details
):
    (
        mixer_input_weight,
        forget_first_map,
        mixer_output_weight,
        feedforward_input_weight,
        feedforward_output_weight,
    ) = weight_tree
    forget_second_map, forget_logit_bias = rank_features
    adapter_model_first, adapter_hidden_first, adapter_second_maps = adapter_params
    adapter_select_mask, source_tokens, dealt_tokens, live = sequence_details
    mixer_column_ranges, feedforward_ranges, output_column_range, down_column_range = all_spans()
    (
        residual_stream,
        normalized_input,
        adapt_mix,
        out_gate,
        gate_logit,
        head_inputs,
        mixed_tok,
        gated_output,
        adapter_output_proj,
        resid_mid,
        normalized_middle,
        adapt_ffn,
        gate_and_up,
        hidden_features,
        adapter_down_proj,
    ) = saved_record
    branch_gradient = output_gradient.astype(jnp.bfloat16)
    back_down = low_rank_back(
        branch_gradient,
        hidden_features,
        adapter_down_proj,
        adapter_hidden_first[VALUE_WIDTH:],
        adapter_second_maps,
        down_column_range,
        adapter_select_mask,
    )
    grad_hidden = times_trans(branch_gradient, feedforward_output_weight) + back_down[0]
    gate_part = gate_and_up[:, :HIDDEN_UNITS]
    up_part = gate_and_up[:, HIDDEN_UNITS:]
    sigma = jax.nn.sigmoid(gate_part)
    grad_gate_up = jnp.concatenate(
        [
            grad_hidden * up_part * sigma * (1.0 + gate_part * (1.0 - sigma)),
            grad_hidden * gate_part * sigma,
        ],
        axis=1,
    ).astype(jnp.bfloat16)
    back_ffn = low_rank_back(
        grad_gate_up,
        normalized_middle,
        adapt_ffn,
        adapter_model_first[:, 4 * ADAPTER_COLUMNS :],
        adapter_second_maps,
        feedforward_ranges,
        adapter_select_mask,
    )
    grad_mid = output_gradient + rms_back(
        resid_mid, times_trans(grad_gate_up, feedforward_input_weight) + back_ffn[0]
    )
    attention_gradient = grad_mid.astype(jnp.bfloat16)
    back_out = low_rank_back(
        attention_gradient,
        gated_output,
        adapter_output_proj,
        adapter_hidden_first[:VALUE_WIDTH],
        adapter_second_maps,
        output_column_range,
        adapter_select_mask,
    )
    grad_gated = times_trans(attention_gradient, mixer_output_weight) + back_out[0]
    sig_gate = jax.nn.sigmoid(out_gate)
    grad_mixed = (grad_gated * out_gate * sig_gate).astype(jnp.bfloat16)
    grad_out_gate = (
        grad_gated * mixed_tok.astype(jnp.float32) * sig_gate * (1.0 + out_gate * (1.0 - sig_gate))
    ).astype(jnp.bfloat16)
    grad_heads = lax.all_to_all(grad_mixed, "seq", split_axis=1, concat_axis=0, tiled=True)

    def local_mix(queries, keys, values, forget):
        return head_mix(queries, keys, values, forget, source_tokens, dealt_tokens, live)

    _, pullback = jax.vjp(local_mix, *[tensor.astype(jnp.float32) for tensor in head_inputs])
    head_grads = pullback(grad_heads.astype(jnp.float32))
    token_grads = lax.all_to_all(
        as_sent(tuple((tensor.astype(jnp.bfloat16) for tensor in head_grads))),
        "seq",
        split_axis=0,
        concat_axis=1,
        tiled=True,
    )
    grad_queries, grad_keys, grad_values, grad_forget = token_grads
    grad_logit = (grad_forget.astype(jnp.float32) * jax.nn.sigmoid(-gate_logit) / 16.0).astype(
        jnp.bfloat16
    )
    grad_low = times_trans(grad_logit, forget_second_map).astype(jnp.bfloat16)
    grad_proj = jnp.concatenate([grad_queries, grad_keys, grad_values, grad_out_gate], axis=1)
    back_mix = low_rank_back(
        grad_proj,
        normalized_input,
        adapt_mix,
        adapter_model_first[:, : 4 * ADAPTER_COLUMNS],
        adapter_second_maps,
        mixer_column_ranges,
        adapter_select_mask,
    )
    grad_normed = (
        times_trans(grad_proj, mixer_input_weight)
        + times_trans(grad_low, forget_first_map)
        + back_mix[0]
    )
    entry_gradient = grad_mid + rms_back(residual_stream, grad_normed)
    gradient_tree = (
        jnp.concatenate([back_mix[1], back_ffn[1]], axis=1),
        jnp.concatenate([back_out[1], back_down[1]], axis=0),
        jnp.concatenate([back_mix[2], back_ffn[2], back_out[2], back_down[2]], axis=1),
    )
    return (entry_gradient, gradient_tree)


def local(
    ends,
    mixer_input_weight,
    forget_first_map,
    forget_second_map,
    forget_logit_bias,
    mixer_output_weight,
    feedforward_input_weight,
    feedforward_output_weight,
    adapter_model_first,
    adapter_hidden_first,
    adapter_second_maps,
    lengths,
    dealt_block_order,
    adapter_choice_per_seq,
):
    section_index = lax.axis_index("section")
    first_section = section_index == 0
    micro_count = ends.shape[1]
    boundary = ends[0, :, 0]
    collected_rows = (
        lax.all_gather(mixer_input_weight[0], "dp", axis=0, tiled=True),
        lax.all_gather(forget_first_map[0], "dp", axis=0, tiled=True),
        lax.all_gather(mixer_output_weight[0], "dp", axis=0, tiled=True),
        lax.all_gather(feedforward_input_weight[0], "dp", axis=0, tiled=True),
        lax.all_gather(feedforward_output_weight[0], "dp", axis=0, tiled=True),
    )
    rank_features = (forget_second_map[0], forget_logit_bias[0])
    adapter_params = (adapter_model_first[0], adapter_hidden_first[0], adapter_second_maps[0])
    records = []
    outputs = []
    incoming = jnp.zeros(boundary.shape[1:], jnp.bfloat16)
    for turn in range(micro_count + 1):
        micro_index = jnp.clip(turn - section_index, 0, micro_count - 1)
        source_rows = jnp.where(
            first_section, boundary[min(turn, micro_count - 1)], incoming
        ).astype(jnp.float32)
        sequence_details = sequence_info(
            lengths, dealt_block_order, adapter_choice_per_seq, micro_index
        )
        layer_result, saved_record = layer_forward_pass(
            source_rows, collected_rows, rank_features, adapter_params, sequence_details
        )
        outgoing = layer_result.astype(jnp.bfloat16)
        incoming = passed_along(outgoing, "section", 1)
        records.append(saved_record)
        outputs.append(outgoing)
    recomputed_again = (
        lax.all_gather(mixer_input_weight[0], "dp", axis=0, tiled=True),
        lax.all_gather(forget_first_map[0], "dp", axis=0, tiled=True),
        lax.all_gather(mixer_output_weight[0], "dp", axis=0, tiled=True),
        lax.all_gather(feedforward_input_weight[0], "dp", axis=0, tiled=True),
        lax.all_gather(feedforward_output_weight[0], "dp", axis=0, tiled=True),
    )
    grad_sums = (
        jnp.zeros(adapter_params[0].shape, jnp.float32),
        jnp.zeros(adapter_params[1].shape, jnp.float32),
        jnp.zeros(adapter_params[2].shape, jnp.float32),
    )
    entry_grads = []
    incoming = jnp.zeros(boundary.shape[1:], jnp.bfloat16)
    for turn in range(micro_count + 1):
        micro_index = jnp.clip(turn - 1 + section_index, 0, micro_count - 1)
        later_rec = records[min(turn + 1, micro_count)]
        early_rec = records[max(turn - 1, 0)]
        saved_record = jax.tree.map(
            lambda early, later: jnp.where(first_section, early, later), early_rec, later_rec
        )
        sequence_details = sequence_info(
            lengths, dealt_block_order, adapter_choice_per_seq, micro_index
        )
        input_gradient = jnp.where(
            first_section, incoming, boundary[min(turn, micro_count - 1)]
        ).astype(jnp.float32)
        entry_gradient, gradient_tree = layer_backward_pass(
            input_gradient,
            saved_record,
            recomputed_again,
            rank_features,
            adapter_params,
            sequence_details,
        )
        valid_flag = jnp.where(first_section, turn >= 1, turn < micro_count).astype(jnp.float32)
        grad_sums = tuple(
            (total + valid_flag * addend for total, addend in zip(grad_sums, gradient_tree))
        )
        outgoing = entry_gradient.astype(jnp.bfloat16)
        incoming = passed_along(outgoing, "section", -1)
        entry_grads.append(outgoing)
    results = jnp.stack(
        [
            jnp.where(first_section, entry_grads[index_mb + 1], outputs[index_mb + 1])
            for index_mb in range(micro_count)
        ]
    )
    reduced = (
        lax.psum_scatter(grad_sums[0], ("dp", "seq"), scatter_dimension=1, tiled=True),
        lax.psum_scatter(grad_sums[1], ("dp", "seq"), scatter_dimension=1, tiled=True),
        lax.psum_scatter(grad_sums[2], ("dp", "seq"), scatter_dimension=1, tiled=True),
    )
    return (results[None, :, None], reduced[0][None], reduced[1][None], reduced[2][None])


def solution(mesh):
    return jax.shard_map(
        local,
        mesh=mesh,
        in_specs=(
            P("section", None, "dp", "seq", None),
            P("section", "dp", None),
            P("section", "dp", None),
            P("section", None, None),
            P("section", None),
            P("section", "dp", None),
            P("section", "dp", None),
            P("section", "dp", None),
            P("section", None, None),
            P("section", None, None),
            P("section", None, None),
            P(None, "dp"),
            P(None, "dp", None),
            P(None, "dp"),
        ),
        out_specs=(
            P("section", None, "dp", "seq", None),
            P("section", None, ("dp", "seq")),
            P("section", None, ("dp", "seq")),
            P("section", None, ("dp", "seq")),
        ),
        check_vma=False,
    )
```

profile of v0, /device:TPU:0, one launch (start us, length us, event | category | flops | bytes accessed | tf_op | source)
XLA Modules:
  0.0 2045.0 jit_solution(13662887748484104636)
XLA Ops:
  9.5 14.9 all-gather.2
  66.3 61.4 %all-gather.12.cloned.1.call-done = bf16[1,1024,3072]{2,1,0:T(8,128)(2,1)} async-done(((bf16[1,256,3072]{2,1,0:T(8,128)(2,1)}), bf16[1,1024,3072]{2,1,0:T(8,128)(2,1)}) %all-gather.12.cloned.1.call-update) | async-done | bytes 6291472 | tf_op jit(solution)/shard_map/all_gather | solution.py:424
  127.7 6.7 fusion.761
  178.6 17.3 while.141
  228.5 146.3 %all-gather.16.cloned.1.call-done = bf16[1,1024,5632]{2,1,0:T(8,128)(2,1)} async-done(((bf16[1,256,5632]{2,1,0:T(8,128)(2,1)}), bf16[1,1024,5632]{2,1,0:T(8,128)(2,1)}) %all-gather.16.cloned.1.call-update) | async-done | bytes 11534352 | tf_op jit(solution)/shard_map/all_gather | solution.py:427
  374.9 8.6 fusion.24
  388.4 92.8 %all-gather.10.cloned.1.call-done = bf16[1,2816,1024]{2,1,0:T(8,128)(2,1)} async-done(((bf16[1,704,1024]{2,1,0:T(8,128)(2,1)}), bf16[1,2816,1024]{2,1,0:T(8,128)(2,1)}) %all-gather.10.cloned.1.call-update) | async-done | bytes 5767184 | tf_op jit(solution)/shard_map/all_gather | solution.py:455
  496.8 7.3 fusion.762
  553.8 17.0 while.142
  628.6 7.4 fusion.763
  756.0 37.0 %while.145 = (s32[]{:T(128)}, f32[1,128,256]{2,1,0:T(8,128)S(1)}, f32[16,1,128,256]{3,2,1,0:T(8,128)}, f32[16,1,128]{2,1,0:T(1,128)}, f32[16,1,128,256]{3,2,1,0:T(8,128)}, /*index=5*/s32[]{:T(128)}, s32[]{:T(128)}) while((s32[]{:T(128)}, f32[1,128,256]{2,1,0:T(8,128)S(1)}, f32[16,1,128,256]{3,2,1,0:T(8,128)}, ...), condition=%wide.region_40.45_spmd.clone, body=%wide.region_39.44_spmd.clone.sunk | while | flops 131075 | bytes 657004 | solution.py:129
  825.7 55.9 %while.143 = (s32[]{:T(128)}, f32[1,128,256]{2,1,0:T(8,128)S(1)}, f32[16,1,128,256]{3,2,1,0:T(8,128)}, f32[16,1,128,1]{2,3,1,0:T(1,128)}, f32[16,1,128]{2,1,0:T(...) while((s32[]{:T(128)}, f32[1,128,256]{2,1,0:T(8,128)S(1)}, ...), condition=%wide.region_20.25_spmd.clone, body=%wide.region_19.24_spmd.clone.sunk | while | flops 131075 | bytes 658040 | solution.py:129
  900.0 55.7 %while.146 = (s32[]{:T(128)}, f32[1,128,256]{2,1,0:T(8,128)S(1)}, f32[16,1,128,256]{3,2,1,0:T(8,128)}, f32[16,1,128,1]{2,3,1,0:T(1,128)}, f32[16,1,128]{2,1,0:T(...) while((s32[]{:T(128)}, f32[1,128,256]{2,1,0:T(8,128)S(1)}, ...), condition=%wide.region_49.54_spmd.clone, body=%wide.region_48.53_spmd.clone.sunk | while | flops 131075 | bytes 658040 | solution.py:129
  973.5 55.8 %while.148 = (s32[]{:T(128)}, f32[1,128,256]{2,1,0:T(8,128)S(1)}, f32[16,1,128,256]{3,2,1,0:T(8,128)}, f32[16,1,128,1]{2,3,1,0:T(1,128)}, f32[16,1,128]{2,1,0:T(...) while((s32[]{:T(128)}, f32[1,128,256]{2,1,0:T(8,128)S(1)}, ...), condition=%wide.region_71.76_spmd.clone, body=%wide.region_70.75_spmd.clone.sunk | while | flops 131075 | bytes 658040 | solution.py:129
  1050.4 17.1 broadcast_select_fusion
  1110.2 7.9 scatter_custom_fusion
  1134.0 71.0 %while.144 = (s32[]{:T(128)}, f32[1,128,256]{2,1,0:T(8,128)S(1)}, f32[16,1,128]{2,1,0:T(1,128)}, f32[16,1,128,256]{3,2,1,0:T(8,128)}, f32[16,1,128,256]{2,3,0,1:...) while((s32[]{:T(128)}, f32[1,128,256]{2,1,0:T(8,128)S(1)}, ...), condition=%wide.region_26.31_spmd.clone, body=%wide.region_24.30_spmd.clone.sunk | while | flops 196484 | bytes 1313944 | solution.py:129
  1210.4 7.5 scatter_custom_fusion.3
  1306.3 8.8 fusion.80
  1348.6 7.5 scatter_custom_fusion.5
  1370.8 71.3 %while.147 = (s32[]{:T(128)}, f32[1,128,256]{2,1,0:T(8,128)S(1)}, f32[16,1,128]{2,1,0:T(1,128)}, f32[16,1,128,256]{3,2,1,0:T(8,128)}, f32[16,1,128,256]{2,3,0,1:...) while((s32[]{:T(128)}, f32[1,128,256]{2,1,0:T(8,128)S(1)}, ...), condition=%wide.region_55.60_spmd.clone, body=%wide.region_53.59_spmd.clone.sunk | while | flops 196484 | bytes 1313944 | solution.py:129
  1447.3 7.6 scatter_custom_fusion.8
  1464.7 6.7 scatter_custom_fusion.7
  1475.5 6.5 scatter_custom_fusion.6
  1544.7 8.1 fusion.77
  1608.3 70.7 %while.149 = (s32[]{:T(128)}, f32[1,128,256]{2,1,0:T(8,128)S(1)}, f32[16,1,128]{2,1,0:T(1,128)}, f32[16,1,128,256]{3,2,1,0:T(8,128)}, f32[16,1,128,256]{2,3,0,1:...) while((s32[]{:T(128)}, f32[1,128,256]{2,1,0:T(8,128)S(1)}, ...), condition=%wide.region_77.82_spmd.clone, body=%wide.region_75.81_spmd.clone.sunk | while | flops 196484 | bytes 1313944 | solution.py:129
  1699.5 6.5 scatter_custom_fusion.11
  1718.5 6.8 scatter_custom_fusion.13
  1747.2 9.2 multiply_add_fusion
  1785.5 6.5 scatter_custom_fusion.14
  1813.5 88.2 %reduce-scatter.12.cloned.1.call-done = f32[672,128]{1,0:T(8,128)} async-done(((f32[10752,128]{1,0:T(8,128)}), f32[672,128]{1,0:T(8,128)}) %reduce-scatter.12.cloned.1.call-update) | async-done | bytes 344080
  1903.8 134.1 %reduce-scatter.8.cloned.1.call-done = f32[1024,48]{0,1:T(8,128)} async-done(((f32[1024,768]{0,1:T(8,128)}), f32[1024,48]{0,1:T(8,128)}) %reduce-scatter.8.cloned.1.call-update) | async-done | bytes 196624 | tf_op jit(solution)/shard_map/reduce_scatter | solution.py:499
  (1978 shorter events, 1347.0 us)
Async XLA Ops:
  7.2 120.5 %all-gather.12.cloned.1.call-start = ((), (), s32[]{:S(2)}) async-start(), calls=%async_computation.35 | async-start | bytes 7864320 | tf_op jit(solution)/shard_map/all_gather | solution.py:424
  7.9 211.6 %all-gather.14.cloned.1.call-start = ((), (), s32[]{:S(2)}) async-start(), calls=%async_computation.36 | async-start | bytes 2621440 | tf_op jit(solution)/shard_map/all_gather | solution.py:426
  8.7 366.2 %all-gather.16.cloned.1.call-start = ((), (), s32[]{:S(2)}) async-start(), calls=%async_computation.37 | async-start | bytes 14417920 | tf_op jit(solution)/shard_map/all_gather | solution.py:427
  28.2 108.1 %all-to-all-start.2 = ((bf16[256,4,128]{2,0,1:T(8,128)(2,1)}), bf16[256,4,128]{2,0,1:T(8,128)(2,1)S(1)}, u32[]{:S(2)}, u32[]{:S(2)}) async-start(bf16[256,4,128]{2,0,1:T(8,128)(2,1)} %copy_bitcast_fusion.19), calls=%async_computation.2 | async-start | bytes 524288 | tf_op jit(solution)/shard_map/all_to_all | solution.py:219
  32.0 449.2 %all-gather.10.cloned.1.call-start = ((), (), s32[]{:S(2)}) async-start(), calls=%async_computation.34 | async-start | bytes 7208960 | tf_op jit(solution)/shard_map/all_gather | solution.py:455
  145.6 11.6 all-to-all-start.3
  157.2 14.1 all-to-all-start
  204.8 10.9 all-to-all-start.4
  523.3 11.7 all-to-all-start.8
  534.9 11.6 all-to-all-start.5
  581.9 11.0 all-to-all-start.9
  655.1 10.3 all-to-all-start.18
  665.4 73.6 %all-to-all-start.15 = ((bf16[256,4,256]{2,0,1:T(8,128)(2,1)}), bf16[256,4,256]{2,0,1:T(8,128)(2,1)}, u32[]{:S(2)}, u32[]{:S(2)}) async-start(bf16[256,4,256]{2,0,1:T(8,128)(2,1)} %bitcast.1627), calls=%async_computation.15 | async-start | bytes 1048576 | tf_op jit(solution)/shard_map/all_to_all | solution.py:218
  808.3 226.9 %all-to-all-start.19 = ((bf16[4,256,256]{2,1,0:T(8,128)(2,1)}), bf16[4,256,256]{2,1,0:T(8,128)(2,1)}, u32[]{:S(2)}, u32[]{:S(2)}) async-start(bf16[4,256,256]{2,1,0:T(8,128)(2,1)} %bitcast.1625), calls=%async_computation.19 | async-start | bytes 1048576 | tf_op jit(solution)/shard_map/all_to_all | solution.py:224
  1097.0 12.2 all-to-all-start.10
  1235.7 19.4 all-to-all-start.12
  1255.1 11.1 all-to-all-start.11
  1266.2 11.2 all-to-all-start.13
  1277.4 13.1 all-to-all-start.14
  1333.8 13.6 all-to-all-start.20
  1472.1 18.6 all-to-all-start.22
  1490.8 9.5 all-to-all-start.21
  1500.3 10.4 all-to-all-start.23
  1510.7 13.1 all-to-all-start.24
  1572.6 13.0 all-to-all-start.25
  1576.7 234.1 %reduce-scatter.10.cloned.1.call-start = ((), (), s32[]{:S(2)}) async-start(), calls=%async_computation.38 | async-start | bytes 2088960
  1696.1 14.8 all-to-all-start.27
  1710.8 15.4 all-to-all-start.26
  1726.2 12.1 all-to-all-start.28
  1730.5 171.2 %reduce-scatter.12.cloned.1.call-start = ((), (), s32[]{:S(2)}) async-start(), calls=%async_computation.39 | async-start | bytes 5849088
  1762.6 275.4 %reduce-scatter.8.cloned.1.call-start = ((), (), s32[]{:S(2)}) async-start(), calls=%async_computation.33 | async-start | bytes 3342336 | tf_op jit(solution)/shard_map/reduce_scatter | solution.py:499
  1792.8 11.9 all-to-all-start.29
  (393 other events, 4422.2 us)
Sparse Core Ops, SparseCore 0:
  9.6 118.0 all-gather.11
  129.3 44.1 all-gather.13
  175.0 199.7 all-gather.15
  376.3 104.8 all-gather.9
  1582.1 126.6 reduce-scatter.9
  1762.7 139.0 reduce-scatter.11
  1908.1 129.8 reduce-scatter.7
where the time goes:
time: 2060 us; the launch traced here: 2050 us
  waiting for transfers between devices  581 us (28%)
  other arithmetic  460 us (22%)
  matrix products  422 us (20%)
  local copies, waits for them, and re-layouts  417 us (20%)
  starting transfers between devices  126 us (6%)
    all_gather x1, waiting for transfers between devices, local(): lax.all_gather(feedforward_input_weight[0], 'dp', axis=0, tiled=True)  146 us
    reduce_scatter x1, waiting for transfers between devices, local(): lax.psum_scatter(grad_sums[0], ('dp', 'seq'), scatter_dimension=1, tiled=...  134 us
    dot_general x51, matrix products, times_trans(): lax.dot_general(left, right, (((1,), (1,)), ((), ())), preferred_element_...  128 us
    dot_general x51, matrix products, matrix_product(): return jnp.dot(left, right, preferred_element_type=jnp.float32)  118 us
    mul x144, local copies, waits for them, and re-layouts, advance(): return (decay[..., None] * state + addend, state)  97.8 us
    add x96, other arithmetic, advance(): return (decay[..., None] * state + addend, state)  95.8 us
    all_gather x1, waiting for transfers between devices, local(): lax.all_gather(feedforward_output_weight[0], 'dp', axis=0, tiled=True)  92.8 us
    unnamed x9, waiting for transfers between devices  90.9 us
  transfers between devices with their start and end apart: 41, of which 19 were waited for; matrix products, arithmetic and copies ran while one was open for 36% of the time, Pallas kernels for 0%

commit v1 on v0

v1 whole, which is shorter than its diff:
```python
import functools
import jax
import jax.numpy as jnp
from jax import lax
from jax.experimental import pallas as pl
from jax.experimental.pallas import tpu as pltpu

from jax.sharding import PartitionSpec as P

MODEL_WIDTH = 1024
HEADS = 4
KEY = 512
VALUE_WIDTH = 1024
HIDDEN_UNITS = 2816
FGATE_RANK = 16
GROUP = 64
ADAPTER_RANK = 16
ADAPTERS = 8
ADAPTER_COLUMNS = 128
VMEM_LIMIT = 60 << 20

MESH = pl.DeviceIdType.MESH
ANY = pl.BlockSpec(memory_space=pl.ANY)


def gather_kernel(*refs):
    n_w, n_s = 4, 6
    shards = refs[:n_w]
    f1_ref, ends_ref = refs[n_w : n_w + 2]
    small = refs[n_w + 2 : n_w + 2 + n_s - 1]
    at = n_w + 2 + len(small)
    outs = refs[at : at + n_w]
    f1_out, x_out, c_out = refs[at + n_w : at + n_w + 3]
    small_out = refs[at + n_w + 3 : at + n_w + 3 + len(small)]
    at += n_w + 3 + len(small)
    held, held_small, held_ends, held_f1 = refs[at : at + n_w], refs[at + n_w : at + n_w + len(small)], refs[-23], refs[-22]
    ins = refs[-21]
    (zs, zr, xs, xr, ys, yr, fxs, fxr, fys, fyr, cs, cr, own, ms, mr, es, er, f1s, f1r, f1c) = refs[-20:]
    core, z, s = lax.axis_index("section"), lax.axis_index("dp"), lax.axis_index("seq")
    other = 1 - core
    n_z = 4
    fetch = [pltpu.make_async_copy(shards[w].at[0], held[w], ins.at[w]) for w in range(n_w)]
    fetch += [pltpu.make_async_copy(a.at[0], b, ins.at[n_w + i]) for i, (a, b) in enumerate(zip(small, held_small))]
    fetch.append(pltpu.make_async_copy(ends_ref.at[0, :, 0], held_ends, ins.at[n_w + len(small)]))
    fetch.append(pltpu.make_async_copy(f1_ref, held_f1, ins.at[n_w + len(small) + 1]))
    for f in fetch:
        f.start()
    barrier = pltpu.get_barrier_semaphore()

    def greet(**where):
        pl.semaphore_signal(barrier, inc=1, device_id=where, device_id_type=MESH)

    greet(section=other)
    greet(seq=s ^ 1)
    greet(seq=s ^ 2)
    for gap in range(1, n_z):
        greet(dp=lax.rem(z + gap, n_z))
    pl.semaphore_wait(barrier, 3 + n_z - 1)

    finals = []

    def remote(src, dst, ssem, rsem, **where):
        return pltpu.make_async_remote_copy(
            src_ref=src, dst_ref=dst, send_sem=ssem, recv_sem=rsem, device_id=where, device_id_type=MESH
        )

    def rows_of(w, j):
        return shards[w].shape[1] * j

    def piece(w, j, q):
        r = shards[w].shape[1]
        return outs[w].at[core, pl.ds(pl.multiple_of(j * r + q * (r // 4), 16), r // 4)]

    def half(w, j, q, low):
        r = shards[w].shape[1]
        cut = (r // 8 + 15) // 16 * 16
        start, size = (0, cut) if low else (cut, r // 4 - cut)
        return outs[w].at[core, pl.ds(pl.multiple_of(j * r + q * (r // 4) + start, 16), size)]

    def block(w, j):
        r = shards[w].shape[1]
        return outs[w].at[core, pl.ds(pl.multiple_of(j * r, 16), r)]

    def own_shard(w):
        return held[w]

    def own_piece(w):
        r = shards[w].shape[1]
        return held[w].at[pl.ds(pl.multiple_of(s * (r // 4), 16), r // 4)]

    def step(d):
        return 1 if d == 0 else -1

    def can_send(d, t):
        has_next = (z < n_z - 1) if d == 0 else (z > 0)
        origin = z - step(d) * (t - 1)
        return jnp.logical_and(has_next, jnp.logical_and(origin >= 0, origin < n_z))

    def gets(d, t):
        origin = z - step(d) * t
        return jnp.logical_and(origin >= 0, origin < n_z)

    def z_copy(w, d, t):
        j = z - step(d) * (t - 1)
        src = own_piece(w) if t == 1 else piece(w, j, s)
        return remote(src, piece(w, j, s), zs.at[w, d, t - 1], zr.at[w, d, t - 1], dp=z + step(d))

    def origin(d, t):
        return z - step(d) * t

    def x_copy(w, d, t):
        return remote(piece(w, origin(d, t), s), piece(w, origin(d, t), s), xs.at[w, d, t - 1], xr.at[w, d, t - 1], seq=s ^ 1)

    def y_copy(w, d, t):
        return remote(piece(w, origin(d, t), s), piece(w, origin(d, t), s), ys.at[w, d, t - 1], yr.at[w, d, t - 1], seq=s ^ 2)

    def fx_copy(w, d, t):
        ref = half(w, origin(d, t), s ^ 2, False)
        return remote(ref, ref, fxs.at[w, d, t - 1], fxr.at[w, d, t - 1], seq=s ^ 1)

    def fy_copy(w, d, t):
        ref = half(w, origin(d, t), s ^ 1, True)
        return remote(ref, ref, fys.at[w, d, t - 1], fyr.at[w, d, t - 1], seq=s ^ 2)

    def c_copy(w, d, t):
        if t == 0:
            return remote(own_shard(w), block(w, z), cs.at[w, 0, 3], cr.at[w, 0, 3], section=other)
        ref = block(w, origin(d, t))
        return remote(ref, ref, cs.at[w, d, t - 1], cr.at[w, d, t - 1], section=other)

    def own_copy(w):
        return pltpu.make_async_copy(own_shard(w), block(w, z), own.at[w])

    def start_own(w):
        for d in range(2):
            @pl.when(can_send(d, 1))
            def _():
                z_copy(w, d, 1).start()

    def take_z(w, t):
        for d in range(2):
            @pl.when(gets(d, t))
            def _():
                z_copy(w, d, t).wait_recv()
            if t < n_z - 1:
                @pl.when(can_send(d, t + 1))
                def _():
                    z_copy(w, d, t + 1).start()
            @pl.when(gets(d, t))
            def _():
                x_copy(w, d, t).start()
                y_copy(w, d, t).start()

    def take_xy(w, t):
        for d in range(2):
            @pl.when(gets(d, t))
            def _():
                x_copy(w, d, t).wait_recv()
                fy_copy(w, d, t).start()
                y_copy(w, d, t).wait_recv()
                fx_copy(w, d, t).start()

    def take_diagonal(w, t):
        for d in range(2):
            @pl.when(gets(d, t))
            def _():
                fy_copy(w, d, t).wait_recv()
                fx_copy(w, d, t).wait_recv()
                c_copy(w, d, t).start()

    ends_to_x = remote(held_ends.at[1], x_out, es, er, section=other)
    ends_to_c = remote(held_ends.at[0], c_out, es, er, section=other)
    ends_x = pltpu.make_async_copy(held_ends.at[0], x_out, own.at[n_w])
    ends_c = pltpu.make_async_copy(held_ends.at[1], c_out, own.at[n_w])

    for f in fetch:
        f.wait()
    start_own(0)
    @pl.when(core == 0)
    def _():
        ends_to_x.start()
        ends_x.start()

    @pl.when(core == 1)
    def _():
        ends_to_c.start()
        ends_c.start()

    def f1_copy(gap):
        return remote(
            held_f1, f1_out.at[core, z], f1s.at[gap], f1r.at[gap], dp=lax.rem(z + gap, n_z)
        )
    for gap in range(1, n_z):
        f1_copy(gap).start()
    f1_own = pltpu.make_async_copy(held_f1, f1_out.at[core, z], own.at[n_w + 1])
    f1_own.start()
    smalls = []
    for i, (a, b) in enumerate(zip(held_small, small_out)):
        mine = pltpu.make_async_copy(a, b.at[core], own.at[n_w + 2 + i])
        theirs = remote(a, b.at[core], ms.at[i], mr.at[i], section=other)
        mine.start()
        theirs.start()
        smalls.append((mine, theirs))
    for w in range(n_w):
        own_copy(w).start()
        c_copy(w, 0, 0).start()
    items = [(w, t) for w in range(n_w) for t in range(1, n_z)]
    f1_sends = [f1_copy(gap) for gap in range(1, n_z)]
    f1_cross = remote(f1_out.at[core], f1_out.at[core], f1c.at[0], f1c.at[1], section=other)
    for i in range(len(items) + 2):
        if i < len(items):
            w, t = items[i]
            if t == 1 and w + 1 < n_w:
                start_own(w + 1)
            take_z(w, t)
        if 0 <= i - 1 < len(items):
            take_xy(*items[i - 1])
        if 0 <= i - 2 < len(items):
            take_diagonal(*items[i - 2])
        if i == 1:
            f1_own.wait()
            for c in f1_sends:
                c.wait_recv()
            f1_cross.start()
    for w in range(n_w):
        own_copy(w).wait()
        c_copy(w, 0, 0).wait()
        for d in range(2):
            for t in range(1, n_z):
                @pl.when(can_send(d, t))
                def _():
                    z_copy(w, d, t).wait_send()
                @pl.when(gets(d, t))
                def _():
                    x_copy(w, d, t).wait_send()
                    y_copy(w, d, t).wait_send()
                    fx_copy(w, d, t).wait_send()
                    fy_copy(w, d, t).wait_send()
                    c_copy(w, d, t).wait()
    for mine, theirs in smalls:
        mine.wait()
        theirs.wait()
    for c in f1_sends:
        c.wait_send()
    f1_cross.wait()
    ends_x.wait()
    ends_to_x.wait()


def gather_all(shards, f1t, ends, small):
    n_w = 4
    shape = jax.ShapeDtypeStruct
    outs = [shape((2, 4 * w.shape[1], w.shape[2]), w.dtype) for w in shards]
    outs.append(shape((2, 4) + f1t.shape, f1t.dtype))
    outs += [shape(ends.shape[3:], ends.dtype)] * 2
    outs += [shape((2,) + a.shape[1:], a.dtype) for a in small]
    dma = pltpu.SemaphoreType.DMA
    per = [dma((n_w, 2, 3)) for _ in range(10)] + [dma((n_w, 2, 4)) for _ in range(2)]
    return pl.pallas_call(
        gather_kernel,
        out_shape=outs,
        in_specs=[ANY] * (n_w + 2 + len(small)),
        out_specs=[ANY] * len(outs),
        scratch_shapes=[pltpu.VMEM(w.shape[1:], w.dtype) for w in shards]
        + [pltpu.VMEM(a.shape[1:], a.dtype) for a in small]
        + [pltpu.VMEM((2,) + ends.shape[3:], ends.dtype), pltpu.VMEM(f1t.shape, f1t.dtype)]
        + [dma((n_w + len(small) + 2,))]
        + per
        + [dma((n_w + 2 + len(small),)), dma((len(small),)), dma((len(small),)), dma, dma, dma((4,)), dma((4,)), dma((2,))],
        compiler_params=pltpu.CompilerParams(collective_id=0, has_side_effects=True, vmem_limit_bytes=VMEM_LIMIT),
    )(*shards, f1t, ends, *small)


BF = jnp.bfloat16
F32 = jnp.float32


def nn(a, b):
    return lax.dot_general(a, b, (((1,), (0,)), ((), ())), preferred_element_type=F32)


def nt(a, b):
    return lax.dot_general(a, b, (((1,), (1,)), ((), ())), preferred_element_type=F32)


def tn(a, b):
    return lax.dot_general(a, b, (((0,), (0,)), ((), ())), preferred_element_type=F32)


def silu_parts(v):
    sig = lax.logistic(v)
    return v * sig, sig


def inverse_rms(v):
    return lax.rsqrt(jnp.mean(v * v, axis=-1, keepdims=True) + 1e-06)


def rms_back(v, grad):
    r = inverse_rms(v)
    n = v * r
    return r * (grad - n * jnp.mean(grad * n, axis=-1, keepdims=True))


def lanes(start, size):
    return pl.ds(pl.multiple_of(start, 128), size)


def rows(start, size):
    return pl.ds(pl.multiple_of(start, size if size <= 64 else 64), size)


def greet_peers(me):
    barrier = pltpu.get_barrier_semaphore()
    for d in range(1, HEADS):
        pl.semaphore_signal(barrier, inc=1, device_id={"seq": me ^ d}, device_id_type=MESH)
    pl.semaphore_wait(barrier, HEADS - 1)


def to_peer(src, dst, ssem, rsem, peer):
    return pltpu.make_async_remote_copy(
        src_ref=src, dst_ref=dst, send_sem=ssem, recv_sem=rsem,
        device_id={"seq": peer}, device_id_type=MESH,
    )


class Local:
    def __init__(self, sems):
        self.sems, self.used, self.open = sems, 0, []

    def start(self, src, dst, wait_at_end=False):
        copy = pltpu.make_async_copy(src, dst, self.sems.at[self.used])
        self.used += 1
        copy.start()
        if wait_at_end:
            self.open.append(copy)
        return copy

    def finish(self):
        for copy in self.open:
            copy.wait()


def picked(adapter, width):
    row = lax.broadcasted_iota(jnp.int32, (width, ADAPTER_RANK), 0)
    col = lax.broadcasted_iota(jnp.int32, (width, ADAPTER_RANK), 1)
    return (row == adapter * ADAPTER_RANK + col).astype(BF)


def column_mask(adapter):
    col = lax.broadcasted_iota(jnp.int32, (1, ADAPTER_COLUMNS), 1)
    low = adapter * ADAPTER_RANK
    return jnp.logical_and(col >= low, col < low + ADAPTER_RANK).astype(F32)


def lower_triangle(dtype):
    i = lax.broadcasted_iota(jnp.int32, (GROUP, GROUP), 0)
    j = lax.broadcasted_iota(jnp.int32, (GROUP, GROUP), 1)
    return (i >= j).astype(dtype)


DK = KEY // HEADS
DV = VALUE_WIDTH // HEADS
CHUNK = 2 * DK + DV
FROZEN = 2 * KEY + 2 * VALUE_WIDTH
TILE = 256
SCALE = DK ** (-0.5)

U_G = FROZEN
U_U = FROZEN + HIDDEN_UNITS
U_O = FROZEN + 2 * HIDDEN_UNITS
U_D = U_O + MODEL_WIDTH


def live_rows(n, length):
    at = lax.broadcasted_iota(jnp.int32, (GROUP, 1), 0) + n * GROUP
    return (at < length).astype(F32)


def forward_kernel(
    layer, n_blocks, meta, h_in, w_mi, w_mo, w_fi, w_fo, w_f1, w_f2, w_b, w_am, w_ah, w_au,
    y_out, o_ad, o_og, o_qkv, o_gl, o_st, o_mix, o_yh, o_rh, o_ao, o_mid, o_af, o_gu, o_dn,
    h, mi, mo, fi, fo, f1, f2, bias, am, ah, au,
    y, ad, og, qkv, gl, st, mix, yh, rh, ao, mid, af, gu, dn,
    normed, send, glsend, fg, state, gated, hidden,
    lsem, ssem, rsem,
):
    me = lax.axis_index("seq")
    T = h.shape[0]
    per = T // GROUP
    adapter = meta[2 * n_blocks]
    length = meta[2 * n_blocks + 1]
    loc = Local(lsem)
    l_h = loc.start(h_in, h)
    l_f1 = loc.start(w_f1.at[layer], f1)
    l_f2 = loc.start(w_f2.at[layer], f2)
    l_b = loc.start(w_b.at[layer], bias)
    l_am = loc.start(w_am.at[layer], am)
    l_au = loc.start(w_au.at[layer], au)
    l_mi = loc.start(w_mi.at[layer], mi)
    greet_peers(me)
    l_ah = loc.start(w_ah.at[layer], ah)
    l_mo = loc.start(w_mo.at[layer], mo)
    l_fi = loc.start(w_fi.at[layer], fi)
    l_fo = loc.start(w_fo.at[layer], fo)
    mask = column_mask(adapter)

    l_h.wait()
    hv = h[...].astype(F32)
    normed[...] = (hv * inverse_rms(hv)).astype(BF)
    l_f1.wait()
    z_w = f1.shape[2]
    low = nt(f1[0], normed[:, 0:z_w])
    for j in range(1, f1.shape[0]):
        low += nt(f1[j], normed[:, j * z_w : (j + 1) * z_w])
    glsend[...] = low.astype(BF)
    low_copies = [to_peer(glsend, gl.at[me], ssem.at[0, d], rsem.at[0, d], me ^ d) for d in range(1, HEADS)]
    for c in low_copies:
        c.start()
    gl[me] = glsend[...]
    l_am.wait()
    for p in range(4):
        cols = pl.ds(p * ADAPTER_COLUMNS, ADAPTER_COLUMNS)
        ad[:, cols] = (nn(normed[...], am[:, cols]) * mask).astype(BF)
    l_au.wait()
    l_mi.wait()

    def project(w_start, p, width):
        cols = lanes(w_start, width)
        return nn(normed[...], mi[:, cols]) + nn(ad[:, p * ADAPTER_COLUMNS : (p + 1) * ADAPTER_COLUMNS], au[:, cols])

    def chunk(head, ref):
        ref[:, 0:DK] = project(head * DK, 0, DK).astype(BF)
        ref[:, DK : 2 * DK] = project(KEY + head * DK, 1, DK).astype(BF)
        ref[:, 2 * DK : CHUNK] = project(2 * KEY + head * DV, 2, DV).astype(BF)

    qkv_copies = []
    for d in range(1, HEADS):
        chunk(me ^ d, send.at[d - 1])
        copy = to_peer(send.at[d - 1], qkv.at[rows(me * T, T)], ssem.at[1, d], rsem.at[1, d], me ^ d)
        copy.start()
        qkv_copies.append(copy)
    chunk(me, qkv.at[rows(me * T, T)])
    loc.start(ad, o_ad, True)
    for j in range(VALUE_WIDTH // TILE):
        og[:, j * TILE : (j + 1) * TILE] = project(2 * KEY + VALUE_WIDTH + j * TILE, 3, TILE)
    loc.start(og, o_og, True)
    l_f2.wait()
    l_b.wait()
    for c in low_copies:
        c.wait_recv()
    f2h = f2[:, lanes(me * DK, DK)]
    bh = bias[:, lanes(me * DK, DK)]
    for src in range(HEADS):
        logit = tn(gl[src], f2h) + bh
        fg[src * T : (src + 1) * T, :] = (jax.nn.log_sigmoid(logit) / 16.0).astype(BF)
    for c in qkv_copies:
        c.wait_recv()
    loc.start(gl, o_gl, True)
    loc.start(qkv, o_qkv, True)
    tri = lower_triangle(BF)
    causal = lower_triangle(F32)

    state[...] = jnp.zeros_like(state)

    def advance(n, carry):
        at = pl.ds(meta[n_blocks + n] * GROUP, GROUP)
        summed = nn(tri, fg[at, :])
        total = summed[GROUP - 1 : GROUP]
        k = qkv[at, DK : 2 * DK].astype(F32) * live_rows(n, length)
        ku = (k * jnp.exp(total - summed)).astype(BF)
        update = tn(qkv[at, 2 * DK : CHUNK], ku)
        now = state[...]
        st[n] = now.astype(BF)
        state[...] = jnp.exp(total) * now + update
        return carry

    lax.fori_loop(0, n_blocks, advance, 0, unroll=4)
    loc.start(st, o_st, True)

    def mix_block(p):
        n = meta[p]
        at = rows(p * GROUP, GROUP)
        summed = nn(tri, fg[at, :])
        middle = summed[GROUP // 2 : GROUP // 2 + 1]
        q = qkv[at, 0:DK].astype(F32) * SCALE
        k = qkv[at, DK : 2 * DK].astype(F32) * live_rows(n, length)
        qe = (q * jnp.exp(summed - middle)).astype(BF)
        ke = (k * jnp.exp(middle - summed)).astype(BF)
        scores = jnp.where(causal > 0, nt(qe, ke), 0.0).astype(BF)
        o = nn(scores, qkv[at, 2 * DK : CHUNK]) + nt((q * jnp.exp(summed)).astype(BF), st[n])
        r = lax.rsqrt(jnp.mean(o * o, axis=-1, keepdims=True) + 1.0)
        yh[at, :] = (o * r).astype(BF)
        rh[at, :] = jnp.broadcast_to(r, (GROUP, DK))

    mix_copies = []
    for d in range(1, HEADS):
        peer = me ^ d
        lax.fori_loop(0, per, lambda j, c, peer=peer: (mix_block(peer * per + j), c)[1], 0, unroll=True)
        copy = to_peer(yh.at[rows(peer * T, T)], mix.at[me], ssem.at[2, d], rsem.at[2, d], peer)
        copy.start()
        mix_copies.append(copy)
    lax.fori_loop(0, per, lambda j, c: (mix_block(me * per + j), c)[1], 0, unroll=True)
    mix[me] = yh[rows(me * T, T), :]
    loc.start(yh, o_yh, True)
    loc.start(rh, o_rh, True)
    for c in mix_copies:
        c.wait_recv()
    loc.start(mix, o_mix, True)
    for hd in range(HEADS):
        cols = slice(hd * DV, (hd + 1) * DV)
        gated[:, cols] = (mix[hd].astype(F32) * silu_parts(og[:, cols])[0]).astype(BF)
    l_ah.wait()
    l_mo.wait()
    ao[...] = (nn(gated[...], ah[0:VALUE_WIDTH, :]) * mask).astype(BF)
    for j in range(MODEL_WIDTH // TILE):
        cols = slice(j * TILE, (j + 1) * TILE)
        mid[:, cols] = (
            h[:, cols].astype(F32) + nn(gated[...], mo[:, cols]) + nn(ao[...], au[:, U_O + j * TILE : U_O + (j + 1) * TILE])
        )
    loc.start(ao, o_ao, True)
    loc.start(mid, o_mid, True)
    mv = mid[...]
    normed[...] = (mv * inverse_rms(mv)).astype(BF)
    for p in range(2):
        cols = slice(p * ADAPTER_COLUMNS, (p + 1) * ADAPTER_COLUMNS)
        wide = slice((4 + p) * ADAPTER_COLUMNS, (5 + p) * ADAPTER_COLUMNS)
        af[:, cols] = (nn(normed[...], am[:, wide]) * mask).astype(BF)
    loc.start(af, o_af, True)
    l_fi.wait()

    def up_tile(i, carry):
        a, b = lanes(i * TILE, TILE), lanes(HIDDEN_UNITS + i * TILE, TILE)
        gate = nn(normed[...], fi[:, a]) + nn(af[:, 0:ADAPTER_COLUMNS], au[:, lanes(U_G + i * TILE, TILE)])
        up = nn(normed[...], fi[:, b]) + nn(af[:, ADAPTER_COLUMNS:], au[:, lanes(U_U + i * TILE, TILE)])
        gu[:, a] = gate.astype(gu.dtype)
        gu[:, b] = up.astype(gu.dtype)
        hidden[:, a] = (silu_parts(gate)[0] * up).astype(BF)
        return carry

    lax.fori_loop(0, HIDDEN_UNITS // TILE, up_tile, 0)
    loc.start(gu, o_gu, True)
    l_fo.wait()
    dn[...] = (nn(hidden[...], ah[VALUE_WIDTH:, :]) * mask).astype(BF)
    loc.start(dn, o_dn, True)
    for j in range(MODEL_WIDTH // TILE):
        cols = slice(j * TILE, (j + 1) * TILE)
        y[:, cols] = (
            mid[:, cols] + nn(hidden[...], fo[:, cols]) + nn(dn[...], au[:, U_D + j * TILE : U_D + (j + 1) * TILE])
        ).astype(BF)
    loc.start(y, y_out, True)
    loc.finish()
    for c in low_copies + qkv_copies + mix_copies:
        c.wait_send()


def weight_scratch(weights):
    return [pltpu.VMEM(w.shape[1:], w.dtype) for w in weights]


def saved_shapes(T, L, n_blocks):
    s = lambda shape, dtype=BF: (shape, dtype)
    return [
        s((T, MODEL_WIDTH)),
        s((T, 4 * ADAPTER_COLUMNS)),
        s((T, VALUE_WIDTH), F32),
        s((L, CHUNK)),
        s((HEADS, FGATE_RANK, T)),
        s((n_blocks, DV, DK)),
        s((HEADS, T, DV)),
        s((L, DV)),
        s((L, DK), F32),
        s((T, ADAPTER_COLUMNS)),
        s((T, MODEL_WIDTH), F32),
        s((T, 2 * ADAPTER_COLUMNS)),
        s((T, 2 * HIDDEN_UNITS)),
        s((T, ADAPTER_COLUMNS)),
    ]


def forward(layer, meta, h, weights):
    T = h.shape[0]
    L = T * HEADS
    n_blocks = L // GROUP
    saved = saved_shapes(T, L, n_blocks)
    vm = pltpu.VMEM
    dma = pltpu.SemaphoreType.DMA
    return pl.pallas_call(
        functools.partial(forward_kernel, layer, n_blocks),
        out_shape=[jax.ShapeDtypeStruct(*s) for s in saved],
        in_specs=[pl.BlockSpec(memory_space=pltpu.SMEM)] + [ANY] * (1 + len(weights)),
        out_specs=[ANY] * len(saved),
        scratch_shapes=[vm(h.shape, h.dtype)]
        + weight_scratch(weights)
        + [vm(*s) for s in saved]
        + [
            vm((T, MODEL_WIDTH), BF),
            vm((HEADS - 1, T, CHUNK), BF),
            vm((FGATE_RANK, T), BF),
            vm((L, DK), BF),
            vm((DV, DK), F32),
            vm((T, VALUE_WIDTH), BF),
            vm((T, HIDDEN_UNITS), BF),
            dma((1 + len(weights) + len(saved),)),
            dma((3, HEADS)),
            dma((3, HEADS)),
        ],
        compiler_params=pltpu.CompilerParams(
            collective_id=1 + layer, has_side_effects=True, vmem_limit_bytes=VMEM_LIMIT
        ),
        cost_estimate=pl.CostEstimate(flops=2 * T * 13_000_000, bytes_accessed=40 << 20, transcendentals=T * 8192),
    )(meta, h, *weights)


def backward_kernel(
    layer, n_blocks, meta, d_in, h_in, w_mi, w_mo, w_fi, w_fo, w_f1, w_f2, w_b, w_am, w_ah, w_au,
    i_ad, i_og, i_qkv, i_gl, i_st, i_mix, i_yh, i_rh, i_ao, i_mid, i_af, i_gu, i_dn,
    e_out, gm_out, gh_out, gp_out,
    d, h, mi, mo, fi, fo, f1, f2, bias, am, ah, au,
    ad, og, qkv, gl, st, mix, yh, rh, ao, mid, af, gu, dn,
    e, gm, gh, gp,
    hidden, wide, gad, big, grad, dog, sendm, dmr, logit, fg, gstate, gt, dt, don, hidden_gated, sendq, dqkv, dlog, sendl, dlr, dproj,
    lsem, ssem, rsem,
):
    me = lax.axis_index("seq")
    T = h.shape[0]
    per = T // GROUP
    adapter = meta[2 * n_blocks]
    length = meta[2 * n_blocks + 1]
    loc = Local(lsem)
    l_d = loc.start(d_in, d)
    l_au = loc.start(w_au.at[layer], au)
    l_ah = loc.start(w_ah.at[layer], ah)
    l_fo = loc.start(w_fo.at[layer], fo)
    l_gu = loc.start(i_gu, gu)
    l_dn = loc.start(i_dn, dn)
    greet_peers(me)
    l_fi = loc.start(w_fi.at[layer], fi)
    l_am = loc.start(w_am.at[layer], am)
    l_mid = loc.start(i_mid, mid)
    l_af = loc.start(i_af, af)
    l_mo = loc.start(w_mo.at[layer], mo)
    l_og = loc.start(i_og, og)
    l_mix = loc.start(i_mix, mix)
    l_ao = loc.start(i_ao, ao)
    l_mixer = [
        loc.start(a, b)
        for a, b in (
            (w_f2.at[layer], f2), (w_b.at[layer], bias), (i_qkv, qkv), (i_gl, gl), (i_st, st), (i_yh, yh), (i_rh, rh),
        )
    ]
    l_last = [
        loc.start(a, b) for a, b in ((w_mi.at[layer], mi), (w_f1.at[layer], f1), (i_ad, ad), (h_in, h))
    ]
    mask = column_mask(adapter)
    pick = picked(adapter, ADAPTER_COLUMNS)

    def narrow(v):
        return nn(v, pick).astype(BF)

    l_d.wait()
    l_au.wait()
    gdown = (nt(d[...], au[:, U_D : U_D + MODEL_WIDTH]).astype(BF).astype(F32) * mask).astype(BF)
    gdown16 = narrow(gdown)
    l_dn.wait()
    gp[:, U_D : U_D + MODEL_WIDTH] = tn(narrow(dn[...]), d[...])
    gad[...] = gdown
    l_ah.wait()
    l_fo.wait()
    l_gu.wait()

    def down_tile(i, carry):
        a, b = lanes(i * TILE, TILE), lanes(HIDDEN_UNITS + i * TILE, TILE)
        at = pl.ds(pl.multiple_of(i * TILE, TILE), TILE)
        dh = nt(d[...], fo[at, :]) + nt(gad[...], ah[pl.ds(pl.multiple_of(VALUE_WIDTH + i * TILE, TILE), TILE), :])
        gate, up = gu[:, a].astype(F32), gu[:, b].astype(F32)
        act, sig = silu_parts(gate)
        hidden[:, a] = (act * up).astype(BF)
        wide[:, a] = (dh * up * sig * (1.0 + gate * (1.0 - sig))).astype(BF)
        wide[:, b] = (dh * act).astype(BF)
        return carry

    lax.fori_loop(0, HIDDEN_UNITS // TILE, down_tile, 0)
    gate_cols, up_cols = slice(0, HIDDEN_UNITS), slice(HIDDEN_UNITS, 2 * HIDDEN_UNITS)
    gg = (nt(wide[:, gate_cols], au[:, U_G : U_G + HIDDEN_UNITS]).astype(BF).astype(F32) * mask).astype(BF)
    gu2 = (nt(wide[:, up_cols], au[:, U_U : U_U + HIDDEN_UNITS]).astype(BF).astype(F32) * mask).astype(BF)
    gad2 = jnp.concatenate([gg, gu2], axis=1)
    big[:, 0 : 2 * ADAPTER_COLUMNS] = gad2
    l_fi.wait()
    l_am.wait()

    def wide_tile(i, carry):
        at = pl.ds(pl.multiple_of(i * TILE, TILE), TILE)
        grad[:, lanes(i * TILE, TILE)] = nt(wide[...], fi[at, :]) + nt(
            big[:, 0 : 2 * ADAPTER_COLUMNS], am[at, 4 * ADAPTER_COLUMNS :]
        )
        return carry

    lax.fori_loop(0, MODEL_WIDTH // TILE, wide_tile, 0)
    l_mid.wait()
    mv = mid[...]
    grad_mid = d[...].astype(F32) + rms_back(mv, grad[...])
    grad[...] = grad_mid
    attn = grad_mid.astype(BF)
    e[...] = attn
    gout = (nt(attn, au[:, U_O : U_O + MODEL_WIDTH]).astype(BF).astype(F32) * mask).astype(BF)
    gad[...] = gout
    l_mo.wait()
    l_og.wait()
    l_mix.wait()

    def gate_back(head, out):
        at = rows(head * DV, DV)
        cols = lanes(head * DV, DV)
        gg_ = nt(e[...], mo[at, :]) + nt(gad[...], ah[at, :])
        o = og[:, cols]
        act, sig = silu_parts(o)
        out[...] = (gg_ * act).astype(BF)
        m = mix[head].astype(F32)
        dog[:, cols] = (gg_ * m * sig * (1.0 + o * (1.0 - sig))).astype(BF)
        hidden_gated[:, cols] = (m * act).astype(BF)

    mix_copies = []
    for k in range(1, HEADS):
        peer = me ^ k
        gate_back(peer, sendm.at[k - 1])
        copy = to_peer(sendm.at[k - 1], dmr.at[rows(me * T, T)], ssem.at[0, k], rsem.at[0, k], peer)
        copy.start()
        mix_copies.append(copy)
    gate_back(me, dmr.at[rows(me * T, T)])

    l_af.wait()
    l_ao.wait()
    normed_mid = (mv * inverse_rms(mv)).astype(BF)
    gh[:, VALUE_WIDTH:] = tn(gdown16, hidden[...])
    gm[4 * ADAPTER_RANK : 5 * ADAPTER_RANK, :] = tn(narrow(gg), normed_mid)
    gm[5 * ADAPTER_RANK : 6 * ADAPTER_RANK, :] = tn(narrow(gu2), normed_mid)
    gp[:, U_G : U_G + HIDDEN_UNITS] = tn(narrow(af[:, 0:ADAPTER_COLUMNS]), wide[:, gate_cols])
    gp[:, U_U : U_U + HIDDEN_UNITS] = tn(narrow(af[:, ADAPTER_COLUMNS:]), wide[:, up_cols])
    gp[:, U_O : U_O + MODEL_WIDTH] = tn(narrow(ao[...]), e[...])
    gh[:, 0:VALUE_WIDTH] = tn(narrow(gad[...]), hidden_gated[...])

    for c in l_mixer:
        c.wait()
    f2h = f2[:, lanes(me * DK, DK)]
    bh = bias[:, lanes(me * DK, DK)]
    for src in range(HEADS):
        lg = tn(gl[src], f2h) + bh
        logit[src * T : (src + 1) * T, :] = lg
        fg[src * T : (src + 1) * T, :] = (jax.nn.log_sigmoid(lg) / 16.0).astype(BF)
    tri = lower_triangle(BF)
    causal = lower_triangle(F32)
    for c in mix_copies:
        c.wait_recv()
    gstate[...] = jnp.zeros_like(gstate)

    def retreat(i, carry):
        n = n_blocks - 1 - i
        at = pl.ds(meta[n_blocks + n] * GROUP, GROUP)
        here = rows(n * GROUP, GROUP)
        dm = dmr[at, :].astype(F32)
        yv = yh[at, :].astype(F32)
        r = rh[at, 0:1]
        do = (r * (dm - yv * jnp.mean(dm * yv, axis=-1, keepdims=True))).astype(BF)
        don[here, :] = do
        summed = nn(tri, fg[at, :])
        total = jnp.exp(summed[GROUP - 1 : GROUP])
        qs = (qkv[at, 0:DK].astype(F32) * SCALE * jnp.exp(summed)).astype(BF)
        now = gstate[...]
        gt[n] = now.astype(BF)
        decayed = total * now
        dt[n] = jnp.sum(decayed * st[n].astype(F32), axis=0, keepdims=True)
        gstate[...] = decayed + tn(do, qs)
        return carry

    lax.fori_loop(0, n_blocks, retreat, 0, unroll=4)

    def back_block(p, out, j):
        n = meta[p]
        at = rows(p * GROUP, GROUP)
        here = pl.ds(n * GROUP, GROUP)
        to = rows(j * GROUP, GROUP)
        live = live_rows(n, length)
        summed = nn(tri, fg[at, :])
        middle = summed[GROUP // 2 : GROUP // 2 + 1]
        total = summed[GROUP - 1 : GROUP]
        e1, e2 = jnp.exp(summed - middle), jnp.exp(middle - summed)
        es, eu = jnp.exp(summed), jnp.exp(total - summed)
        q = qkv[at, 0:DK].astype(F32) * SCALE
        k = qkv[at, DK : 2 * DK].astype(F32) * live
        v = qkv[at, 2 * DK : CHUNK]
        do, state_t, grad_t = don[here, :], st[n], gt[n]
        qe, ke, qs, ku = q * e1, k * e2, q * es, k * eu
        qeb, keb = qe.astype(BF), ke.astype(BF)
        scores = jnp.where(causal > 0, nt(qeb, keb), 0.0).astype(BF)
        dscores = jnp.where(causal > 0, nt(do, v), 0.0).astype(BF)
        dv = tn(scores, do) + nt(ku.astype(BF), grad_t)
        dqs = nn(do, state_t)
        dku = nn(v, grad_t)
        dqe = nn(dscores, keb)
        dke = tn(dscores, qeb)
        out[to, 0:DK] = (SCALE * (dqe * e1 + dqs * es)).astype(BF)
        out[to, DK : 2 * DK] = (live * (dke * e2 + dku * eu)).astype(BF)
        out[to, 2 * DK : CHUNK] = dv.astype(BF)
        kk = dku * ku
        dsum = dqe * qe + dqs * qs - dke * ke - kk
        dtotal = dt[n] + jnp.sum(kk, axis=0, keepdims=True)
        high = dsum.astype(BF)
        lowp = (dsum - high.astype(F32)).astype(BF)
        df = tn(tri, high) + tn(tri, lowp) + dtotal
        df = df.astype(BF).astype(F32)
        dlog[to, :] = (df * lax.logistic(-logit[at, :]) / 16.0).astype(BF)

    q_copies = []

    def back_rows(dest, out, low_out):
        lax.fori_loop(0, per, lambda j, c: (back_block(dest * per + j, out, j), c)[1], 0, unroll=2)
        low_out[...] = nt(f2h, dlog[...]).astype(BF)

    for k in range(1, HEADS):
        peer = me ^ k
        back_rows(peer, sendq.at[k - 1], sendl.at[k - 1])
        copies = (
            to_peer(sendq.at[k - 1], dqkv.at[me], ssem.at[1, k], rsem.at[1, k], peer),
            to_peer(sendl.at[k - 1], dlr.at[me], ssem.at[2, k], rsem.at[2, k], peer),
        )
        for copy in copies:
            copy.start()
        q_copies += copies
    back_rows(me, dqkv.at[me], dlr.at[me])

    for c in l_last:
        c.wait()
    hv = h[...].astype(F32)
    hr = inverse_rms(hv)
    big[...] = (hv * hr).astype(BF)
    for c in q_copies:
        c.wait_recv()
    for hd in range(HEADS):
        dproj[:, hd * DK : (hd + 1) * DK] = dqkv[hd, :, 0:DK]
        dproj[:, KEY + hd * DK : KEY + (hd + 1) * DK] = dqkv[hd, :, DK : 2 * DK]
        dproj[:, 2 * KEY + hd * DV : 2 * KEY + (hd + 1) * DV] = dqkv[hd, :, 2 * DK : CHUNK]
    dproj[:, 2 * KEY + VALUE_WIDTH :] = dog[...]
    dlow = dlr[0].astype(F32)
    for hd in range(1, HEADS):
        dlow += dlr[hd].astype(F32)
    dlowb = dlow.astype(BF)
    spans = ((0, KEY), (KEY, KEY), (2 * KEY, VALUE_WIDTH), (2 * KEY + VALUE_WIDTH, VALUE_WIDTH))
    for p, (start, width) in enumerate(spans):
        block = slice(p * ADAPTER_COLUMNS, (p + 1) * ADAPTER_COLUMNS)
        piece = dproj[:, start : start + width]
        ga = (nt(piece, au[:, start : start + width]).astype(BF).astype(F32) * mask).astype(BF)
        wide[:, block] = ga
        gm[p * ADAPTER_RANK : (p + 1) * ADAPTER_RANK, :] = tn(narrow(ga), big[...])
        gp[:, start : start + width] = tn(narrow(ad[:, block]), piece)
    z_w = f1.shape[2]
    tiles = f1.shape[0]
    back = []
    for j in range(tiles):
        at = slice(j * z_w, (j + 1) * z_w)
        back.append(
            nt(dproj[...], mi[at, :]) + nt(wide[:, 0 : 4 * ADAPTER_COLUMNS], am[at, 0 : 4 * ADAPTER_COLUMNS]) + tn(dlowb, f1[j])
        )
    dn_ = jnp.concatenate(back, axis=1)
    n = hv * hr
    e[...] = (grad[...] + hr * (dn_ - n * jnp.mean(dn_ * n, axis=-1, keepdims=True))).astype(BF)
    for a, b in ((e, e_out), (gm, gm_out), (gh, gh_out), (gp, gp_out)):
        loc.start(a, b, True)
    loc.finish()
    for c in mix_copies + q_copies:
        c.wait_send()


def backward(layer, meta, d, h, weights, saved):
    T = h.shape[0]
    L = T * HEADS
    n_blocks = L // GROUP
    outs = [
        ((T, MODEL_WIDTH), BF),
        ((6 * ADAPTER_RANK, MODEL_WIDTH), F32),
        ((ADAPTER_RANK, VALUE_WIDTH + HIDDEN_UNITS), F32),
        ((ADAPTER_RANK, U_D + MODEL_WIDTH), F32),
    ]
    vm = pltpu.VMEM
    dma = pltpu.SemaphoreType.DMA
    return pl.pallas_call(
        functools.partial(backward_kernel, layer, n_blocks),
        out_shape=[jax.ShapeDtypeStruct(*s) for s in outs],
        in_specs=[pl.BlockSpec(memory_space=pltpu.SMEM)] + [ANY] * (2 + len(weights) + len(saved)),
        out_specs=[ANY] * len(outs),
        scratch_shapes=[vm(d.shape, d.dtype), vm(h.shape, h.dtype)]
        + weight_scratch(weights)
        + [vm(s.shape, s.dtype) for s in saved]
        + [vm(*s) for s in outs]
        + [
            vm((T, HIDDEN_UNITS), BF),
            vm((T, 2 * HIDDEN_UNITS), BF),
            vm((T, ADAPTER_COLUMNS), BF),
            vm((T, MODEL_WIDTH), BF),
            vm((T, MODEL_WIDTH), F32),
            vm((T, VALUE_WIDTH), BF),
            vm((HEADS - 1, T, DV), BF),
            vm((L, DV), BF),
            vm((L, DK), F32),
            vm((L, DK), BF),
            vm((DV, DK), F32),
            vm((n_blocks, DV, DK), BF),
            vm((n_blocks, 1, DK), F32),
            vm((L, DV), BF),
            vm((T, VALUE_WIDTH), BF),
            vm((HEADS - 1, T, CHUNK), BF),
            vm((HEADS, T, CHUNK), BF),
            vm((T, DK), BF),
            vm((HEADS - 1, FGATE_RANK, T), BF),
            vm((HEADS, FGATE_RANK, T), BF),
            vm((T, FROZEN), BF),
            dma((2 + len(weights) + len(saved) + len(outs),)),
            dma((3, HEADS)),
            dma((3, HEADS)),
        ],
        compiler_params=pltpu.CompilerParams(
            collective_id=3 + layer, has_side_effects=True, vmem_limit_bytes=VMEM_LIMIT
        ),
        cost_estimate=pl.CostEstimate(flops=2 * T * 16_000_000, bytes_accessed=45 << 20, transcendentals=T * 8192),
    )(meta, d, h, *weights, *saved)


def swap_sections(v):
    return lax.ppermute(v, "section", [(0, 1), (1, 0)])


def plain_gather(shards, f1t, ends, small):
    first = lax.axis_index("section") == 0
    both = lambda a: lax.all_gather(a, "section", axis=0)
    outs = [both(lax.all_gather(w[0], "dp", axis=0, tiled=True)) for w in shards]
    low = lax.all_gather(f1t, "dp", axis=1, tiled=True)
    outs.append(both(jnp.stack(jnp.split(low, 4, axis=1))))
    sent = swap_sections(jnp.where(first, ends[0, 1, 0], ends[0, 0, 0]))
    outs.append(jnp.where(first, ends[0, 0, 0], sent))
    outs.append(jnp.where(first, sent, ends[0, 1, 0]))
    return outs + [both(a[0]) for a in small]


def spread(parts, chosen):
    hot = (chosen[:, None] == jnp.arange(ADAPTERS, dtype=jnp.int32)[None, :]).astype(F32)
    return sum(parts[n][:, None] * hot[n][None, :, None, None] for n in range(parts.shape[0]))


def reduce_gradients(early, late, chosen, first):
    n_dp, n_seq = lax.axis_size("dp"), lax.axis_size("seq")
    dp = lax.axis_index("dp")
    kept = [jnp.where(first, b, a) for a, b in zip(early, late)]
    got = [swap_sections(jnp.where(first, a, b)) for a, b in zip(early, late)]
    gm, gh, gp = [jnp.stack(pair) for pair in zip(kept, got)]
    wide = gp.shape[-1] // (n_dp * n_seq)
    gm = lax.psum_scatter(gm, "seq", scatter_dimension=2, tiled=True)
    gh = lax.psum_scatter(gh, "seq", scatter_dimension=2, tiled=True)
    gp = jnp.transpose(gp.reshape(2, ADAPTER_RANK, n_dp, n_seq, wide), (3, 2, 0, 1, 4))
    gp = lax.psum_scatter(gp, "seq", scatter_dimension=0, tiled=True)[0]
    gm = lax.all_gather(gm, "dp", axis=0)
    gh = lax.all_gather(gh, "dp", axis=0)
    gp = lax.all_to_all(gp, "dp", split_axis=0, concat_axis=0, tiled=True)
    chosen = chosen.reshape(-1)
    n = chosen.shape[0]
    gm = spread(gm.reshape(n, 6, ADAPTER_RANK, -1), chosen).reshape(6 * ADAPTER_COLUMNS, -1)
    gh = spread(gh.reshape(n, 1, ADAPTER_RANK, -1), chosen).reshape(ADAPTER_COLUMNS, -1)
    gp = spread(gp.reshape(n, 1, ADAPTER_RANK, -1), chosen).reshape(ADAPTER_COLUMNS, -1)

    def columns(v):
        size = v.shape[0] // n_dp
        v = lax.dynamic_slice_in_dim(v, dp * size, size, 0)
        return lax.all_to_all(v, "seq", split_axis=0, concat_axis=1, tiled=True).T

    return columns(gm), columns(gh), gp


def local(
    ends,
    mixer_input_weight,
    forget_first_map,
    forget_second_map,
    forget_logit_bias,
    mixer_output_weight,
    feedforward_input_weight,
    feedforward_output_weight,
    adapter_model_first,
    adapter_hidden_first,
    adapter_second_maps,
    lengths,
    dealt_block_order,
    adapter_choice_per_seq,
):
    first = lax.axis_index("section") == 0
    mine = lambda a: jnp.where(first, a[0], a[1])
    order = mine(dealt_block_order)[0]
    n_blocks = order.shape[0]
    at = jnp.arange(n_blocks, dtype=jnp.int32)
    inverse = jnp.sum(at[:, None] * (order[:, None] == at[None, :]).astype(jnp.int32), axis=0)
    meta = jnp.concatenate([order, inverse, mine(adapter_choice_per_seq), mine(lengths)])
    picks = lax.all_gather(adapter_choice_per_seq[:, 0], "dp", axis=0)
    picks = jnp.where(first, picks, picks[:, ::-1])
    shards = [mixer_input_weight, mixer_output_weight, feedforward_input_weight, feedforward_output_weight]
    small = [
        forget_second_map,
        forget_logit_bias[:, None],
        adapter_model_first,
        adapter_hidden_first,
        adapter_second_maps,
    ]
    gather = gather_all if lax.axis_size("dp") == 4 and lax.axis_size("seq") == 4 else plain_gather
    out = gather(shards, forget_first_map[0].T, ends, small)
    weights = list(out[:5]) + list(out[7:])
    x, cotangent = out[5], out[6]
    early = forward(0, meta, x, weights)
    late = forward(1, meta, early[0], weights)
    middle, *grads_late = backward(1, meta, cotangent, early[0], weights, late[1:])
    entry, *grads_early = backward(0, meta, middle, x, weights, early[1:])
    sent = swap_sections(jnp.where(first, late[0], entry))
    results = jnp.where(first, jnp.stack([entry, sent]), jnp.stack([sent, late[0]]))
    model, hidden, up = reduce_gradients(grads_late, grads_early, picks, first)
    return (results[None, :, None], model[None], hidden[None], up[None])


def solution(mesh):
    return jax.shard_map(
        local,
        mesh=mesh,
        in_specs=(
            P("section", None, "dp", "seq", None),
            P("section", "dp", None),
            P("section", "dp", None),
            P("section", None, None),
            P("section", None),
            P("section", "dp", None),
            P("section", "dp", None),
            P("section", "dp", None),
            P("section", None, None),
            P("section", None, None),
            P("section", None, None),
            P(None, "dp"),
            P(None, "dp", None),
            P(None, "dp"),
        ),
        out_specs=(
            P("section", None, "dp", "seq", None),
            P("section", None, ("dp", "seq")),
            P("section", None, ("dp", "seq")),
            P("section", None, ("dp", "seq")),
        ),
        check_vma=False,
    )
```

time: 2060 us -> 518 us (0.25)
  waiting for transfers between devices: 581 us -> 44 us
  other arithmetic: 460 us -> 8.55 us
  matrix products: 422 us -> 0 us
  local copies, waits for them, and re-layouts: 417 us -> 23.9 us
  Pallas kernels: 0 us -> 364 us
  starting transfers between devices: 126 us -> 11.2 us
  blocking collectives: 14.9 us -> 42.3 us
    dot_general x186 -> x0, matrix products: 422 us -> none  [the longest x51 128 us: times_trans(): lax.dot_general(left, right, (((1,), (1,)), ((), ())), preferred_element_...]
    pallas_call x0 -> x5, Pallas kernels: none -> 364 us  [the longest x1 192 us: gather_all(): pl.pallas_call(gather_kernel, out_shape=outs, in_specs=[ANY] * (n_w + 2 +...]
    all_gather x4 -> x0, waiting for transfers between devices: 301 us -> none  [the longest x1 146 us: local(): lax.all_gather(feedforward_input_weight[0], 'dp', axis=0, tiled=True)]
    reduce_scatter x1, waiting for transfers between devices: 134 us -> 7.6 us  [reduce_gradients(): gm = lax.psum_scatter(gm, 'seq', scatter_dimension=2, tiled=True)]
    add x116 -> x2, other arithmetic: 112 us -> 1.15 us  [spread(): sum((parts[n][:, None] * hot[n][None, :, None, None] for n in range(parts...]
    gather x27 -> x0, local copies, waits for them, and re-layouts: 110 us -> none  [the longest x6 27.3 us: head_mix(): values = jnp.take(values, source_tokens, axis=0)]
    all_to_all x30 -> x3, starting transfers between devices: 118 us -> 10.5 us  [the longest x2 6.69 us: columns(): return lax.all_to_all(v, 'seq', split_axis=0, concat_axis=1, tiled=True).T]
    scatter-add x15 -> x0, other arithmetic: 102 us -> none  [the longest x3 21.9 us: head_mix(): values = jnp.take(values, source_tokens, axis=0)]
  transfers between devices with their start and end apart: 41 -> 10, of which waited for: 19 -> 8; matrix products, arithmetic and copies ran while one was open for 36% -> 3% of each run, Pallas kernels for 0% -> 0%
where the time goes in v1:
time: 518 us; the launch traced here: 512 us
  Pallas kernels  364 us (70%)
  waiting for transfers between devices  44 us (8%)
  blocking collectives  42.3 us (8%)
  local copies, waits for them, and re-layouts  23.9 us (5%)
  between operations  18 us (3%)
  starting transfers between devices  11.2 us (2%)
  other arithmetic  8.55 us (2%)
    pallas_call x1, Pallas kernels, gather_all(): pl.pallas_call(gather_kernel, out_shape=outs, in_specs=[ANY] * (n_w + 2 +...  192 us
    pallas_call x2, Pallas kernels, backward(): pl.pallas_call(functools.partial(backward_kernel, layer, n_blocks), out_s...  90.6 us
    pallas_call x2, Pallas kernels, forward(): pl.pallas_call(functools.partial(forward_kernel, layer, n_blocks), out_sh...  81.2 us
    all_gather x1, blocking collectives, reduce_gradients(): gm = lax.all_gather(gm, 'dp', axis=0)  20.2 us
    unnamed x5, waiting for transfers between devices  16.8 us
    all_gather x1, blocking collectives, reduce_gradients(): gh = lax.all_gather(gh, 'dp', axis=0)  15.6 us
    unnamed x26, local copies, waits for them, and re-layouts  12.8 us
  transfers between devices with their start and end apart: 10, of which 8 were waited for; matrix products, arithmetic and copies ran while one was open for 3% of the time, Pallas kernels for 0%

profile of v1, /device:TPU:0, one launch (start us, length us, event | category | flops | bytes accessed | tf_op | source)
XLA Modules:
  0.0 511.6 jit_solution(6260734267987886914)
XLA Ops:
  7.2 1.3 fusion.24
  8.5 1.3 fusion.23
  13.8 191.9 %shard_map.165 = (bf16[2,1024,3072]{2,1,0:T(8,128)(2,1)}, bf16[2,1024,1024]{2,1,0:T(8,128)(2,1)}, bf16[2,1024,5632]{2,1,0:T(8,128)(2,1)}, bf16[2,2816,1024]{2,1,...) custom-call(bf16[1,256,3072]{2,1,0:T(8,128)(2,1)} %refs_0_.1, ...), custom_call_target="tpu_custom_call" | custom-call | tf_op jit(solution)/shard_map/pallas_call | solution.py:259
  205.7 42.2 %shard_map.166 = (bf16[256,1024]{1,0:T(8,128)(2,1)}, bf16[256,512]{1,0:T(8,128)(2,1)}, f32[256,1024]{1,0:T(8,128)}, bf16[1024,512]{1,0:T(8,128)(2,1)}, bf16[4,16...) custom-call(s32[34]{0:T(128)} %pad_add_fusion.meta, ...), custom_call_target="tpu_custom_call" | custom-call | flops 6656000000 | bytes 41943040 | tf_op jit(solution)/shard_map/pallas_call | solution.py:588
  247.9 39.0 %shard_map.167 = (bf16[256,1024]{1,0:T(8,128)(2,1)}, bf16[256,512]{1,0:T(8,128)(2,1)}, f32[256,1024]{1,0:T(8,128)}, bf16[1024,512]{1,0:T(8,128)(2,1)}, bf16[4,16...) custom-call(s32[34]{0:T(128)} %pad_add_fusion.meta, ...), custom_call_target="tpu_custom_call" | custom-call | flops 6656000000 | bytes 41943040 | tf_op jit(solution)/shard_map/pallas_call | solution.py:588
  286.9 46.0 %shard_map.168 = (bf16[256,1024]{1,0:T(8,128)(2,1)}, f32[96,1024]{1,0:T(8,128)}, f32[16,3840]{1,0:T(8,128)}, f32[16,10752]{1,0:T(8,128)}) custom-call(s32[34]{0:T(128)} %pad_add_fusion.meta, bf16[256,1024]{1,0:T(8,128)(2,1)} %get-tuple-element.52.d_in, bf16[256,1024]{1,0:T(8,128)(2,1)} %get-tuple-element.64.h_in, ...), custom_call_target="tpu_custom_call" | custom-call | flops 8192000000 | bytes 47185920 | tf_op jit(solution)/shard_map/pallas_call | solution.py:886
  332.9 44.7 %shard_map.169 = (bf16[256,1024]{1,0:T(8,128)(2,1)}, f32[96,1024]{1,0:T(8,128)}, f32[16,3840]{1,0:T(8,128)}, f32[16,10752]{1,0:T(8,128)}) custom-call(s32[34]{0:T(128)} %pad_add_fusion.meta, bf16[256,1024]{1,0:T(8,128)(2,1)} %get-tuple-element.78.d_in, bf16[256,1024]{1,0:T(8,128)(2,1)} %get-tuple-element.53.h_in, ...), custom_call_target="tpu_custom_call" | custom-call | flops 8192000000 | bytes 47185920 | tf_op jit(solution)/shard_map/pallas_call | solution.py:886
  377.6 1.0 select_bitcast_fusion.1
  378.7 1.5 collective-permute-done.2
  380.2 3.6 copy.36
  383.8 5.2 %reshape.582 = f32[3840,32]{1,0:T(8,128)} reshape(f32[3840,2,16]{2,1,0:T(2,128)} %bitcast.182) | data formatting | bytes 983040
  389.3 1.6 collective-permute-done.1
  390.9 0.9 pad_maximum_fusion
  395.6 1.3 maximum_bitcast_fusion
  398.3 6.5 %all-reduce = s32[8]{0:T(128)S(1)} all-reduce(s32[8]{0:T(128)S(1)} %bitcast_dynamic-update-slice_fusion), channel_id=3, replica_groups=mesh['section'=2,'dp'=4,'seq'=4] {'dp'}, use_global_device_ids=true, to_apply=%add | all-reduce | flops 8 | bytes 64
  408.4 13.7 %reduce-scatter.10.cloned.1.call-done = f32[960,32]{1,0:T(8,128)} async-done(((f32[3840,32]{1,0:T(8,128)}), f32[960,32]{1,0:T(8,128)}) %reduce-scatter.10.cloned.1.call-update) | async-done | bytes 122896
  422.1 1.6 reshape.583
  423.7 0.8 copy.37
  424.5 15.6 %all-gather.2 = f32[8,16,960]{2,1,0:T(8,128)S(1)} all-gather(f32[2,16,960]{2,1,0:T(8,128)S(1)} %copy.37), channel_id=4, replica_groups=mesh['section'=2,'dp'=4,'seq'=4] {'dp'}, dimensions={0}, use_global_device_ids=true | all-gather | bytes 614400 | tf_op jit(solution)/shard_map/all_gather | solution.py:961
  440.6 0.8 fusion.15
  441.4 3.3 all-to-all-start.1
  444.7 7.6 %reduce-scatter.8.cloned.1.call-done = f32[2,96,256]{2,1,0:T(8,128)} async-done(((f32[2,96,1024]{2,1,0:T(8,128)}), f32[2,96,256]{2,1,0:T(8,128)}) %reduce-scatter.8.cloned.1.call-update) | async-done | bytes 196624 | tf_op jit(solution)/shard_map/reduce_scatter | solution.py:956
  452.3 20.2 %all-gather = f32[8,96,256]{2,1,0:T(8,128)S(1)} all-gather(f32[2,96,256]{2,1,0:T(8,128)} %reduce-scatter.8.cloned.1.call-done), channel_id=2, replica_groups=mesh['section'=2,'dp'=4,'seq'=4] {'dp'}, dimensions={0}, use_global_device_ids=true | all-gather | bytes 983040 | tf_op jit(solution)/shard_map/all_gather | solution.py:960
  473.4 0.9 fusion.9
  474.3 3.4 all-to-all-start
  477.8 6.5 %all-to-all-done = f32[4,48,256]{2,1,0:T(8,128)S(1)} async-done(((f32[4,48,256]{2,1,0:T(8,128)}), f32[4,48,256]{2,1,0:T(8,128)S(1)}, u32[]{:S(2)}, u32[]{:S(2)}) %all-to-all-start) | async-done | bytes 196640 | tf_op jit(solution)/shard_map/all_to_all | solution.py:972
  484.4 3.0 reduce-scatter.12.cloned.1.call-done
  487.4 3.8 all-to-all-start.2
  491.2 1.1 maximum_select_fusion
  492.4 0.8 all_to_all.38
  494.0 9.2 %all-to-all-done.2 = f32[4,2,16,672]{3,2,1,0:T(8,128)S(1)} async-done(((f32[4,2,16,672]{3,2,1,0:T(8,128)}), f32[4,2,16,672]{3,2,1,0:T(8,128)S(1)}, u32[]{:S(2)}, u32[]{:S(2)}) %all-to-all-start.2) | async-done | bytes 344096 | tf_op jit(solution)/shard_map/all_to_all | solution.py:962
  503.7 0.9 copy.35
  (119 shorter events, 12.4 us)
Async XLA Ops:
  7.2 414.9 %reduce-scatter.10.cloned.1.call-start = ((), (), s32[]{:S(2)}) async-start(), calls=%async_computation.7 | async-start | bytes 2457600
  332.9 44.7 %copy-start.6 = (f32[16,3840]{1,0:T(8,128)S(1)}, f32[16,3840]{1,0:T(8,128)}, u32[]{:S(2)}) copy-start(f32[16,3840]{1,0:T(8,128)} %get-tuple-element.97) | copy-start | bytes 737284
  378.6 1.6 collective-permute-start.2
  383.8 5.3 %copy-start.4 = (f32[96,1024]{1,0:T(8,128)S(1)}, f32[96,1024]{1,0:T(8,128)}, u32[]{:S(2)}) copy-start(f32[96,1024]{1,0:T(8,128)} %get-tuple-element.95) | copy-start | bytes 1179652
  383.8 5.3 %copy-start.5 = (f32[96,1024]{1,0:T(8,128)S(1)}, f32[96,1024]{1,0:T(8,128)}, u32[]{:S(2)}) copy-start(f32[96,1024]{1,0:T(8,128)} %get-tuple-element.94) | copy-start | bytes 1179652
  389.0 3.0 copy-start.2
  389.0 3.0 copy-start.3
  389.0 63.3 %reduce-scatter.8.cloned.1.call-start = ((), (), s32[]{:S(2)}) async-start(), calls=%async_computation.6 | async-start | bytes 983040 | tf_op jit(solution)/shard_map/reduce_scatter | solution.py:956
  389.1 1.8 collective-permute-start.1
  391.9 95.5 %reduce-scatter.12.cloned.1.call-start = ((), (), s32[]{:S(2)}) async-start(), calls=%async_computation.8 | async-start | bytes 1966080
  392.1 2.2 collective-permute-start.3
  395.1 1.9 copy-start.8
  395.1 3.1 copy-start.7
  441.4 32.9 %all-to-all-start.1 = ((f32[4,8,960]{2,1,0:T(8,128)}), f32[4,8,960]{2,1,0:T(8,128)S(1)}, u32[]{:S(2)}, u32[]{:S(2)}) async-start(f32[4,8,960]{2,1,0:T(8,128)} %fusion.15), calls=%async_computation.2 | async-start | bytes 262144 | tf_op jit(solution)/shard_map/all_to_all | solution.py:972
  473.0 4.7 copy-start
  473.0 4.7 copy-start.1
  474.3 10.1 %all-to-all-start = ((f32[4,48,256]{2,1,0:T(8,128)}), f32[4,48,256]{2,1,0:T(8,128)S(1)}, u32[]{:S(2)}, u32[]{:S(2)}) async-start(f32[4,48,256]{2,1,0:T(8,128)} %bitcast.42), calls=%async_computation.1 | async-start | bytes 393216 | tf_op jit(solution)/shard_map/all_to_all | solution.py:972
  477.7 13.5 %collective-permute-start = (bf16[256,1024]{1,0:T(8,128)(2,1)S(1)}, bf16[256,1024]{1,0:T(8,128)(2,1)S(1)}, u32[]{:S(2)}, u32[]{:S(2)}) collective-permute-start(bf16[256,1024]{1,0:T(8,128)(2,1)S(1)} %broadcast_select_fusion), channel_id=1, source_target_pairs={{0,16},{16,0},{1,17},{17,1},{2,18},{18,2},{3,19},{19,3},{4,20},{20... | collective-permute-start | bytes 1572872 | tf_op jit(solution)/shard_map/ppermute | solution.py:929
  487.4 15.7 %all-to-all-start.2 = ((f32[4,2,16,672]{3,2,1,0:T(8,128)}), f32[4,2,16,672]{3,2,1,0:T(8,128)S(1)}, u32[]{:S(2)}, u32[]{:S(2)}) async-start(f32[4,2,16,672]{3,2,1,0:T(8,128)} %bitcast.216), calls=%async_computation.3 | async-start | bytes 786432 | tf_op jit(solution)/shard_map/all_to_all | solution.py:962
Sparse Core Ops, SparseCore 0:
  389.1 32.9 reduce-scatter.9
  425.6 26.6 reduce-scatter.7
  455.3 32.0 reduce-scatter.11

commit v2 on v1

--- a/solution.py
+++ b/solution.py
@@ -618,9 +618,9 @@
     e_out, gm_out, gh_out, gp_out,
     d, h, mi, mo, fi, fo, f1, f2, bias, am, ah, au,
     ad, og, qkv, gl, st, mix, yh, rh, ao, mid, af, gu, dn,
-    e, gm, gh, gp,
-    hidden, wide, gad, big, grad, dog, sendm, dmr, logit, fg, gstate, gt, dt, don, hidden_gated, sendq, dqkv, dlog, sendl, dlr, dproj,
-    lsem, ssem, rsem,
+    e, sgm, sgh, sgp,
+    gm, gh, gp, gps, rgm, rgh, rgp, hidden, wide, gad, big, grad, dog, sendm, dmr, logit, fg, gstate, gt, dt, don, hidden_gated, sendq, dqkv, dlog, sendl, dlr, dproj,
+    lsem, ssem, rsem, gssem, grsem,
 ):
     me = lax.axis_index("seq")
     T = h.shape[0]
@@ -658,12 +658,44 @@
     def narrow(v):
         return nn(v, pick).astype(BF)
 
+    def outer(u, v):
+        return tn(narrow(u), v).astype(BF)
+
+    n_dp, width, padded = gps.shape[1], gp.shape[1] // (HEADS * gps.shape[1]), gps.shape[3]
+    quarter, hidden_quarter = MODEL_WIDTH // HEADS, gh.shape[1] // HEADS
+    n_late = -(-FROZEN // (HEADS * width))
+    mix_rows = 4 * ADAPTER_RANK
+
+    def place(dps):
+        for i in dps:
+            for q in range(HEADS):
+                piece = gp[:, (i * HEADS + q) * width : (i * HEADS + q + 1) * width]
+                gps[q, i] = jnp.concatenate([piece, jnp.zeros((ADAPTER_RANK, padded - width), BF)], axis=1)
+
+    def grad_copies(late):
+        copies = []
+        at = slice(0, mix_rows) if late else slice(mix_rows, 6 * ADAPTER_RANK)
+        dps = slice(0, n_late) if late else slice(n_late, n_dp)
+        for k in range(1, HEADS):
+            peer = me ^ k
+            pairs = [
+                (gm.at[at, lanes(peer * quarter, quarter)], rgm.at[k - 1, at]),
+                (gps.at[peer, dps], rgp.at[k - 1, dps]),
+            ]
+            if not late:
+                pairs.append((gh.at[:, lanes(peer * hidden_quarter, hidden_quarter)], rgh.at[k - 1]))
+            for i, (a, b) in enumerate(pairs):
+                j = i if late else 2 + i
+                copies.append(to_peer(a, b, gssem.at[j, k], grsem.at[j, k], peer))
+        return copies
+
     l_d.wait()
     l_au.wait()
     gdown = (nt(d[...], au[:, U_D : U_D + MODEL_WIDTH]).astype(BF).astype(F32) * mask).astype(BF)
     gdown16 = narrow(gdown)
+    gh[:, VALUE_WIDTH + HIDDEN_UNITS :] = jnp.zeros((ADAPTER_RANK, gh.shape[1] - VALUE_WIDTH - HIDDEN_UNITS), BF)
     l_dn.wait()
-    gp[:, U_D : U_D + MODEL_WIDTH] = tn(narrow(dn[...]), d[...])
+    gp[:, U_D : U_D + MODEL_WIDTH] = outer(dn[...], d[...])
     gad[...] = gdown
     l_ah.wait()
     l_fo.wait()
@@ -732,13 +764,17 @@
     l_af.wait()
     l_ao.wait()
     normed_mid = (mv * inverse_rms(mv)).astype(BF)
-    gh[:, VALUE_WIDTH:] = tn(gdown16, hidden[...])
-    gm[4 * ADAPTER_RANK : 5 * ADAPTER_RANK, :] = tn(narrow(gg), normed_mid)
-    gm[5 * ADAPTER_RANK : 6 * ADAPTER_RANK, :] = tn(narrow(gu2), normed_mid)
-    gp[:, U_G : U_G + HIDDEN_UNITS] = tn(narrow(af[:, 0:ADAPTER_COLUMNS]), wide[:, gate_cols])
-    gp[:, U_U : U_U + HIDDEN_UNITS] = tn(narrow(af[:, ADAPTER_COLUMNS:]), wide[:, up_cols])
-    gp[:, U_O : U_O + MODEL_WIDTH] = tn(narrow(ao[...]), e[...])
-    gh[:, 0:VALUE_WIDTH] = tn(narrow(gad[...]), hidden_gated[...])
+    gh[:, VALUE_WIDTH : VALUE_WIDTH + HIDDEN_UNITS] = tn(gdown16, hidden[...]).astype(BF)
+    gm[4 * ADAPTER_RANK : 5 * ADAPTER_RANK, :] = outer(gg, normed_mid)
+    gm[5 * ADAPTER_RANK : 6 * ADAPTER_RANK, :] = outer(gu2, normed_mid)
+    gp[:, U_G : U_G + HIDDEN_UNITS] = outer(af[:, 0:ADAPTER_COLUMNS], wide[:, gate_cols])
+    gp[:, U_U : U_U + HIDDEN_UNITS] = outer(af[:, ADAPTER_COLUMNS:], wide[:, up_cols])
+    gp[:, U_O : U_O + MODEL_WIDTH] = outer(ao[...], e[...])
+    gh[:, 0:VALUE_WIDTH] = outer(gad[...], hidden_gated[...])
+    place(range(n_late, n_dp))
+    grads = grad_copies(False)
+    for c in grads:
+        c.start()
 
     for c in l_mixer:
         c.wait()
@@ -846,13 +882,17 @@
         dlow += dlr[hd].astype(F32)
     dlowb = dlow.astype(BF)
     spans = ((0, KEY), (KEY, KEY), (2 * KEY, VALUE_WIDTH), (2 * KEY + VALUE_WIDTH, VALUE_WIDTH))
-    for p, (start, width) in enumerate(spans):
+    for p, (start, span) in enumerate(spans):
         block = slice(p * ADAPTER_COLUMNS, (p + 1) * ADAPTER_COLUMNS)
-        piece = dproj[:, start : start + width]
-        ga = (nt(piece, au[:, start : start + width]).astype(BF).astype(F32) * mask).astype(BF)
+        piece = dproj[:, start : start + span]
+        ga = (nt(piece, au[:, start : start + span]).astype(BF).astype(F32) * mask).astype(BF)
         wide[:, block] = ga
-        gm[p * ADAPTER_RANK : (p + 1) * ADAPTER_RANK, :] = tn(narrow(ga), big[...])
-        gp[:, start : start + width] = tn(narrow(ad[:, block]), piece)
+        gm[p * ADAPTER_RANK : (p + 1) * ADAPTER_RANK, :] = outer(ga, big[...])
+        gp[:, start : start + span] = outer(ad[:, block], piece)
+    place(range(n_late))
+    late_grads = grad_copies(True)
+    for c in late_grads:
+        c.start()
     z_w = f1.shape[2]
     tiles = f1.shape[0]
     back = []
@@ -864,22 +904,45 @@
     dn_ = jnp.concatenate(back, axis=1)
     n = hv * hr
     e[...] = (grad[...] + hr * (dn_ - n * jnp.mean(dn_ * n, axis=-1, keepdims=True))).astype(BF)
-    for a, b in ((e, e_out), (gm, gm_out), (gh, gh_out), (gp, gp_out)):
+    loc.start(e, e_out, True)
+    grads += late_grads
+    for c in grads:
+        c.wait_recv()
+
+    def summed_over_seq(own, got):
+        total = own.astype(F32)
+        for k in range(HEADS - 1):
+            total += got[k].astype(F32)
+        return total.astype(BF)
+
+    sgm[...] = summed_over_seq(gm[:, lanes(me * quarter, quarter)], rgm)
+    sgh[...] = summed_over_seq(gh[:, lanes(me * hidden_quarter, hidden_quarter)], rgh)
+    spot = lax.broadcasted_iota(jnp.int32, (ADAPTER_RANK, padded), 1)
+    for i in range(n_dp):
+        total = gps[me, i].astype(F32)
+        for k in range(HEADS - 1):
+            total += rgp[k, i].astype(F32)
+        sgp[i] = jnp.where(spot == width, adapter.astype(F32), total).astype(BF)
+    for a, b in ((sgm, gm_out), (sgh, gh_out), (sgp, gp_out)):
         loc.start(a, b, True)
     loc.finish()
-    for c in mix_copies + q_copies:
+    for c in mix_copies + q_copies + grads:
         c.wait_send()
 
 
-def backward(layer, meta, d, h, weights, saved):
+def backward(layer, meta, d, h, weights, saved, n_dp):
     T = h.shape[0]
     L = T * HEADS
     n_blocks = L // GROUP
+    raised = U_D + MODEL_WIDTH
+    padded = (raised // (n_dp * HEADS) // 128 + 1) * 128
+    quarter = MODEL_WIDTH // HEADS
+    hidden_quarter = -(-(VALUE_WIDTH + HIDDEN_UNITS) // (HEADS * 128)) * 128
     outs = [
         ((T, MODEL_WIDTH), BF),
-        ((6 * ADAPTER_RANK, MODEL_WIDTH), F32),
-        ((ADAPTER_RANK, VALUE_WIDTH + HIDDEN_UNITS), F32),
-        ((ADAPTER_RANK, U_D + MODEL_WIDTH), F32),
+        ((6 * ADAPTER_RANK, quarter), BF),
+        ((ADAPTER_RANK, hidden_quarter), BF),
+        ((n_dp, ADAPTER_RANK, padded), BF),
     ]
     vm = pltpu.VMEM
     dma = pltpu.SemaphoreType.DMA
@@ -893,6 +956,13 @@
         + [vm(s.shape, s.dtype) for s in saved]
         + [vm(*s) for s in outs]
         + [
+            vm((6 * ADAPTER_RANK, MODEL_WIDTH), BF),
+            vm((ADAPTER_RANK, HEADS * hidden_quarter), BF),
+            vm((ADAPTER_RANK, raised), BF),
+            vm((HEADS, n_dp, ADAPTER_RANK, padded), BF),
+            vm((HEADS - 1, 6 * ADAPTER_RANK, quarter), BF),
+            vm((HEADS - 1, ADAPTER_RANK, hidden_quarter), BF),
+            vm((HEADS - 1, n_dp, ADAPTER_RANK, padded), BF),
             vm((T, HIDDEN_UNITS), BF),
             vm((T, 2 * HIDDEN_UNITS), BF),
             vm((T, ADAPTER_COLUMNS), BF),
@@ -917,6 +987,8 @@
             dma((2 + len(weights) + len(saved) + len(outs),)),
             dma((3, HEADS)),
             dma((3, HEADS)),
+            dma((5, HEADS)),
+            dma((5, HEADS)),
         ],
         compiler_params=pltpu.CompilerParams(
             collective_id=3 + layer, has_side_effects=True, vmem_limit_bytes=VMEM_LIMIT
@@ -946,32 +1018,165 @@
     return sum(parts[n][:, None] * hot[n][None, :, None, None] for n in range(parts.shape[0]))
 
 
-def reduce_gradients(early, late, chosen, first):
-    n_dp, n_seq = lax.axis_size("dp"), lax.axis_size("seq")
+def reduce_kernel(
+    gm0, gh0, gp0, gm1, gh1, gp1, m_out, h_out, u_out,
+    vm_, vh, vp, rm, rh, rp, am, ah, em, eh, ls, ss, rs, es, er,
+):
+    core, dp, me = lax.axis_index("section"), lax.axis_index("dp"), lax.axis_index("seq")
+    n_dp = vp.shape[1]
+    width = u_out.shape[1]
+    loads = [
+        pltpu.make_async_copy(a, b.at[l], ls.at[l, i])
+        for l, three in enumerate(((gm0, gh0, gp0), (gm1, gh1, gp1)))
+        for i, (a, b) in enumerate(zip(three, (vm_, vh, vp)))
+    ]
+    for c in loads:
+        c.start()
+    barrier = pltpu.get_barrier_semaphore()
+    places = [dict(section=1 - core)] + [dict(seq=me ^ k) for k in range(1, HEADS)]
+    for gap in range(1, n_dp):
+        to = lax.rem(dp + gap, n_dp)
+        places += [dict(dp=to), dict(section=1 - core, dp=to)]
+    for where in places:
+        pl.semaphore_signal(barrier, inc=1, device_id=where, device_id_type=MESH)
+    for c in loads:
+        c.wait()
+    pl.semaphore_wait(barrier, len(places))
+    slot = dp * 2 + core
+    size = 6 * ADAPTER_COLUMNS // n_dp
+
+    def first_projection(i):
+        return i * size // ADAPTER_COLUMNS
+
+    def parts(layer, to):
+        at = pl.ds(pl.multiple_of(first_projection(to) * ADAPTER_RANK, ADAPTER_RANK), 2 * ADAPTER_RANK)
+        return ((vm_.at[layer, at], rm.at[slot]), (vh.at[layer], rh.at[slot]), (vp.at[layer, to], rp.at[slot]))
+
+    copies = []
+    for gap in range(n_dp - 1, -1, -1):
+        to = lax.rem(dp + gap, n_dp)
+        for crossing in (0, 1):
+            if crossing == 0 and gap == 0:
+                continue
+            section = 1 - core if crossing else core
+            for i, (a, b) in enumerate(parts(section, to)):
+                c = pltpu.make_async_remote_copy(
+                    src_ref=a, dst_ref=b, send_sem=ss.at[crossing, gap, i], recv_sem=rs.at[crossing, gap, i],
+                    device_id=dict(section=section, dp=to), device_id_type=MESH,
+                )
+                c.start()
+                copies.append(c)
+    at = pl.ds(pl.multiple_of(first_projection(dp) * ADAPTER_RANK, ADAPTER_RANK), 2 * ADAPTER_RANK)
+    rm[slot] = vm_[core, at]
+    rh[slot] = vh[core]
+    rp[slot] = vp[core, dp]
+    for c in copies:
+        c.wait_recv()
+    n = rm.shape[0]
+    chosen = [rp[j, :, width : width + 1].astype(F32) for j in range(n)]
+    for a in range(ADAPTERS):
+        hot = [(c == float(a)).astype(F32) for c in chosen]
+        at = slice(a * ADAPTER_RANK, (a + 1) * ADAPTER_RANK)
+
+        def total(values):
+            out = hot[0] * values(0).astype(F32)
+            for j in range(1, n):
+                out += hot[j] * values(j).astype(F32)
+            return out
+
+        for p in range(2):
+            am[p * ADAPTER_COLUMNS + a * ADAPTER_RANK : p * ADAPTER_COLUMNS + (a + 1) * ADAPTER_RANK, :] = total(
+                lambda j, p=p: rm[j, p * ADAPTER_RANK : (p + 1) * ADAPTER_RANK]
+            )
+        ah[at, :] = total(lambda j: rh[j])
+        u_out[at, :] = total(lambda j: rp[j])[:, 0:width]
+    own_m, own_h = size // HEADS, ADAPTER_COLUMNS // n_dp // HEADS
+    base = dp * size - first_projection(dp) * ADAPTER_COLUMNS
+
+    def m_rows(q):
+        return am.at[pl.ds(pl.multiple_of(base + q * own_m, 16), own_m)]
+
+    def h_rows(q):
+        return ah.at[pl.ds(pl.multiple_of(dp * HEADS * own_h + q * own_h, 8), own_h)]
+
+    last = []
+    for k in range(1, HEADS):
+        for i, (a, b) in enumerate(((m_rows(me ^ k), em.at[me]), (h_rows(me ^ k), eh.at[me]))):
+            c = to_peer(a, b, es.at[i, k], er.at[i, k], me ^ k)
+            c.start()
+            last.append(c)
+    em[me] = m_rows(me)[...]
+    eh[me] = h_rows(me)[...]
+    for c in last:
+        c.wait_recv()
+    for q in range(HEADS):
+        m_out[:, q * em.shape[2] : (q + 1) * em.shape[2]] = em[q]
+        h_out[:, q * eh.shape[2] : (q + 1) * eh.shape[2]] = eh[q]
+    for c in copies + last:
+        c.wait_send()
+
+
+def reduce_gradients(early, late, n_dp):
+    gm, gh, gp = early
+    n = 2 * n_dp
+    width = (U_D + MODEL_WIDTH) // (n_dp * HEADS)
+    own_m, own_h = 6 * ADAPTER_COLUMNS // (n_dp * HEADS), ADAPTER_COLUMNS // (n_dp * HEADS)
+    vm, dma, VM = pltpu.VMEM, pltpu.SemaphoreType.DMA, pl.BlockSpec(memory_space=pltpu.VMEM)
+    shape = jax.ShapeDtypeStruct
+    model, hidden, up = pl.pallas_call(
+        reduce_kernel,
+        out_shape=[
+            shape((own_m, MODEL_WIDTH), F32),
+            shape((own_h, HEADS * gh.shape[1]), F32),
+            shape((ADAPTER_COLUMNS, width), F32),
+        ],
+        in_specs=[ANY] * 6,
+        out_specs=[VM] * 3,
+        scratch_shapes=[
+            vm((2,) + gm.shape, BF),
+            vm((2,) + gh.shape, BF),
+            vm((2,) + gp.shape, BF),
+            vm((n, 2 * ADAPTER_RANK, gm.shape[1]), BF),
+            vm((n,) + gh.shape, BF),
+            vm((n,) + gp.shape[1:], BF),
+            vm((2 * ADAPTER_COLUMNS, gm.shape[1]), F32),
+            vm((ADAPTER_COLUMNS, gh.shape[1]), F32),
+            vm((HEADS, own_m, gm.shape[1]), F32),
+            vm((HEADS, own_h, gh.shape[1]), F32),
+            dma((2, 3)),
+            dma((2, n_dp, 3)),
+            dma((2, n_dp, 3)),
+            dma((2, HEADS)),
+            dma((2, HEADS)),
+        ],
+        compiler_params=pltpu.CompilerParams(collective_id=5, has_side_effects=True, vmem_limit_bytes=32 << 20),
+    )(*early, *late)
+    return model.T, hidden[:, : VALUE_WIDTH + HIDDEN_UNITS].T, up
+
+
+def plain_reduce(early, late, n_dp):
+    first = lax.axis_index("section") == 0
     dp = lax.axis_index("dp")
-    kept = [jnp.where(first, b, a) for a, b in zip(early, late)]
-    got = [swap_sections(jnp.where(first, a, b)) for a, b in zip(early, late)]
+    kept = [jnp.where(first, a, b) for a, b in zip(early, late)]
+    got = [swap_sections(jnp.where(first, b, a)) for a, b in zip(early, late)]
     gm, gh, gp = [jnp.stack(pair) for pair in zip(kept, got)]
-    wide = gp.shape[-1] // (n_dp * n_seq)
-    gm = lax.psum_scatter(gm, "seq", scatter_dimension=2, tiled=True)
-    gh = lax.psum_scatter(gh, "seq", scatter_dimension=2, tiled=True)
-    gp = jnp.transpose(gp.reshape(2, ADAPTER_RANK, n_dp, n_seq, wide), (3, 2, 0, 1, 4))
-    gp = lax.psum_scatter(gp, "seq", scatter_dimension=0, tiled=True)[0]
+    width = (U_D + MODEL_WIDTH) // (n_dp * HEADS)
     gm = lax.all_gather(gm, "dp", axis=0)
     gh = lax.all_gather(gh, "dp", axis=0)
-    gp = lax.all_to_all(gp, "dp", split_axis=0, concat_axis=0, tiled=True)
-    chosen = chosen.reshape(-1)
-    n = chosen.shape[0]
-    gm = spread(gm.reshape(n, 6, ADAPTER_RANK, -1), chosen).reshape(6 * ADAPTER_COLUMNS, -1)
-    gh = spread(gh.reshape(n, 1, ADAPTER_RANK, -1), chosen).reshape(ADAPTER_COLUMNS, -1)
-    gp = spread(gp.reshape(n, 1, ADAPTER_RANK, -1), chosen).reshape(ADAPTER_COLUMNS, -1)
+    gp = lax.all_to_all(jnp.swapaxes(gp, 0, 1), "dp", split_axis=0, concat_axis=0, tiled=True)
+    gp = gp.reshape(2 * n_dp, 1, ADAPTER_RANK, -1)
+    n = gp.shape[0]
+    chosen = gp[:, 0, 0, width].astype(jnp.int32)
+    gm = spread(gm.reshape(n, 6, ADAPTER_RANK, -1).astype(F32), chosen).reshape(6 * ADAPTER_COLUMNS, -1)
+    gh = spread(gh.reshape(n, 1, ADAPTER_RANK, -1).astype(F32), chosen).reshape(ADAPTER_COLUMNS, -1)
+    gp = spread(gp.astype(F32), chosen).reshape(ADAPTER_COLUMNS, -1)
 
     def columns(v):
         size = v.shape[0] // n_dp
         v = lax.dynamic_slice_in_dim(v, dp * size, size, 0)
         return lax.all_to_all(v, "seq", split_axis=0, concat_axis=1, tiled=True).T
 
-    return columns(gm), columns(gh), gp
+    return columns(gm), columns(gh)[: VALUE_WIDTH + HIDDEN_UNITS], gp[:, :width]
 
 
 def local(
@@ -997,8 +1202,8 @@
     at = jnp.arange(n_blocks, dtype=jnp.int32)
     inverse = jnp.sum(at[:, None] * (order[:, None] == at[None, :]).astype(jnp.int32), axis=0)
     meta = jnp.concatenate([order, inverse, mine(adapter_choice_per_seq), mine(lengths)])
-    picks = lax.all_gather(adapter_choice_per_seq[:, 0], "dp", axis=0)
-    picks = jnp.where(first, picks, picks[:, ::-1])
+    n_dp = lax.axis_size("dp")
+    own_kernels = n_dp == 4 and lax.axis_size("seq") == 4
     shards = [mixer_input_weight, mixer_output_weight, feedforward_input_weight, feedforward_output_weight]
     small = [
         forget_second_map,
@@ -1007,17 +1212,18 @@
         adapter_hidden_first,
         adapter_second_maps,
     ]
-    gather = gather_all if lax.axis_size("dp") == 4 and lax.axis_size("seq") == 4 else plain_gather
+    gather = gather_all if own_kernels else plain_gather
     out = gather(shards, forget_first_map[0].T, ends, small)
     weights = list(out[:5]) + list(out[7:])
     x, cotangent = out[5], out[6]
     early = forward(0, meta, x, weights)
     late = forward(1, meta, early[0], weights)
-    middle, *grads_late = backward(1, meta, cotangent, early[0], weights, late[1:])
-    entry, *grads_early = backward(0, meta, middle, x, weights, early[1:])
+    middle, *grads_late = backward(1, meta, cotangent, early[0], weights, late[1:], n_dp)
+    entry, *grads_early = backward(0, meta, middle, x, weights, early[1:], n_dp)
     sent = swap_sections(jnp.where(first, late[0], entry))
     results = jnp.where(first, jnp.stack([entry, sent]), jnp.stack([sent, late[0]]))
-    model, hidden, up = reduce_gradients(grads_late, grads_early, picks, first)
+    reduce = reduce_gradients if own_kernels else plain_reduce
+    model, hidden, up = reduce(grads_early, grads_late, n_dp)
     return (results[None, :, None], model[None], hidden[None], up[None])
 
 

time: 518 us -> 415 us (0.80)
  waiting for transfers between devices: 44 us -> 0.01 us
  blocking collectives: 42.3 us -> 0 us
  Pallas kernels: 364 us -> 395 us
  local copies, waits for them, and re-layouts: 23.9 us -> 7.32 us
  between operations: 18 us -> 3.59 us
  starting transfers between devices: 11.2 us -> 0.07 us
  other arithmetic: 8.55 us -> 2.56 us
    all_gather x2 -> x0, blocking collectives: 35.8 us -> none  [the longest x1 20.2 us: reduce_gradients(): gm = lax.all_gather(gm, 'dp', axis=0)]
    pallas_call x0 -> x1, Pallas kernels: none -> 24.6 us  [reduce_gradients(): pl.pallas_call(reduce_kernel, out_shape=[shape((own_m, MODEL_WIDTH), F32)...]
    unnamed x5 -> x0, waiting for transfers between devices: 16.8 us -> none
    all_to_all x3 -> x0, waiting for transfers between devices: 15.7 us -> none  [the longest x1 9.16 us: reduce_gradients(): gp = lax.all_to_all(gp, 'dp', split_axis=0, concat_axis=0, tiled=True)]
    all_to_all x3 -> x0, starting transfers between devices: 10.5 us -> none  [the longest x2 6.69 us: columns(): return lax.all_to_all(v, 'seq', split_axis=0, concat_axis=1, tiled=True).T]
    unnamed x26 -> x18, local copies, waits for them, and re-layouts: 12.8 us -> 4.04 us
    reduce_scatter x1 -> x0, waiting for transfers between devices: 7.6 us -> none  [reduce_gradients(): gm = lax.psum_scatter(gm, 'seq', scatter_dimension=2, tiled=True)]
    pallas_call x2, Pallas kernels: 90.6 us -> 97.5 us  [backward(): pl.pallas_call(functools.partial(backward_kernel, layer, n_blocks), out_s...]
  transfers between devices with their start and end apart: 10 -> 1, of which waited for: 8 -> 0; matrix products, arithmetic and copies ran while one was open for 3% -> 0% of each run, Pallas kernels for 0% -> 6%
where the time goes in v2:
time: 415 us; the launch traced here: 409 us
  Pallas kernels  395 us (95%)
  local copies, waits for them, and re-layouts  7.32 us (2%)
    pallas_call x1, Pallas kernels, gather_all(): pl.pallas_call(gather_kernel, out_shape=outs, in_specs=[ANY] * (n_w + 2 +...  192 us
    pallas_call x2, Pallas kernels, backward(): pl.pallas_call(functools.partial(backward_kernel, layer, n_blocks), out_s...  97.5 us
    pallas_call x2, Pallas kernels, forward(): pl.pallas_call(functools.partial(forward_kernel, layer, n_blocks), out_sh...  81.3 us
    pallas_call x1, Pallas kernels, reduce_gradients(): pl.pallas_call(reduce_kernel, out_shape=[shape((own_m, MODEL_WIDTH), F32)...  24.6 us
  transfers between devices with their start and end apart: 1, of which 0 were waited for; matrix products, arithmetic and copies ran while one was open for 0% of the time, Pallas kernels for 6%

profile of v2, /device:TPU:0, one launch (start us, length us, event | category | flops | bytes accessed | tf_op | source)
XLA Modules:
  0.0 409.0 jit_solution(10639236733127845364)
XLA Ops:
  0.6 0.7 fusion
  1.3 0.1 select_reduce_fusion
  1.4 1.3 fusion.2
  2.7 1.3 fusion.1
  6.6 0.6 pad_add_fusion.meta
  7.2 192.1 %shard_map.165 = (bf16[2,1024,3072]{2,1,0:T(8,128)(2,1)}, bf16[2,1024,1024]{2,1,0:T(8,128)(2,1)}, bf16[2,1024,5632]{2,1,0:T(8,128)(2,1)}, bf16[2,2816,1024]{2,1,...) custom-call(bf16[1,256,3072]{2,1,0:T(8,128)(2,1)} %refs_0_.1, ...), custom_call_target="tpu_custom_call" | custom-call | tf_op jit(solution)/shard_map/pallas_call | solution.py:259
  199.3 42.0 %shard_map.166 = (bf16[256,1024]{1,0:T(8,128)(2,1)}, bf16[256,512]{1,0:T(8,128)(2,1)}, f32[256,1024]{1,0:T(8,128)}, bf16[1024,512]{1,0:T(8,128)(2,1)}, bf16[4,16...) custom-call(s32[34]{0:T(128)} %pad_add_fusion.meta, ...), custom_call_target="tpu_custom_call" | custom-call | flops 6656000000 | bytes 41943040 | tf_op jit(solution)/shard_map/pallas_call | solution.py:588
  241.2 39.4 %shard_map.167 = (bf16[256,1024]{1,0:T(8,128)(2,1)}, bf16[256,512]{1,0:T(8,128)(2,1)}, f32[256,1024]{1,0:T(8,128)}, bf16[1024,512]{1,0:T(8,128)(2,1)}, bf16[4,16...) custom-call(s32[34]{0:T(128)} %pad_add_fusion.meta, ...), custom_call_target="tpu_custom_call" | custom-call | flops 6656000000 | bytes 41943040 | tf_op jit(solution)/shard_map/pallas_call | solution.py:588
  280.6 48.9 %shard_map.168 = (bf16[256,1024]{1,0:T(8,128)(2,1)}, bf16[96,256]{1,0:T(8,128)(2,1)}, bf16[16,1024]{1,0:T(8,128)(2,1)}, bf16[4,16,768]{2,1,0:T(8,128)(2,1)}) custom-call(s32[34]{0:T(128)} %pad_add_fusion.meta, bf16[256,1024]{1,0:T(8,128)(2,1)} %get-tuple-element.55.d_in, bf16[256,1024]{1,0:T(8,128)(2,1)} %get-tuple-element.67.h_in, ...), custom_call_target="tpu_custom_call" | custom-call | flops 8192000000 | bytes 47185920 | tf_op jit(solution)/shard_map/pallas_call | solution.py:949
  329.6 0.0 copy-start.6
  329.6 0.0 copy-start
  329.6 0.0 copy-start.2
  329.6 0.0 copy-start.4
  329.6 48.5 %shard_map.169 = (bf16[256,1024]{1,0:T(8,128)(2,1)}, bf16[96,256]{1,0:T(8,128)(2,1)}, bf16[16,1024]{1,0:T(8,128)(2,1)}, bf16[4,16,768]{2,1,0:T(8,128)(2,1)}) custom-call(s32[34]{0:T(128)} %pad_add_fusion.meta, bf16[256,1024]{1,0:T(8,128)(2,1)} %get-tuple-element.81.d_in, bf16[256,1024]{1,0:T(8,128)(2,1)} %get-tuple-element.56.h_in, ...), custom_call_target="tpu_custom_call" | custom-call | flops 8192000000 | bytes 47185920 | tf_op jit(solution)/shard_map/pallas_call | solution.py:949
  378.1 0.0 copy-start.7
  378.2 0.0 copy-done.6
  378.2 0.1 broadcast_select_fusion
  378.2 0.1 collective-permute-start
  378.3 0.0 copy-done
  378.3 0.0 copy-done.2
  378.3 0.0 copy-done.4
  378.3 0.0 copy-start.1
  378.4 0.9 copy-done.1
  379.2 0.8 copy-done.3
  380.0 0.8 copy-done.5
  380.8 24.6 %shard_map.170 = (f32[48,1024]{1,0:T(8,128)S(1)}, f32[8,4096]{1,0:T(8,128)S(1)}, f32[128,672]{1,0:T(8,128)S(1)}) custom-call(bf16[96,256]{1,0:T(8,128)(2,1)S(1)} %copy-done.3, bf16[16,1024]{1,0:T(8,128)(2,1)S(1)} %copy-done.5, bf16[4,16,768]{2,1,0:T(8,128)(2,1)S(1)} %copy-done.1, bf16[96,256]{1,0:T(8,128)(2,1)S(1)} %copy-done.2, ...), custom_call_target="tpu_custom_call" | custom-call | tf_op jit(solution)/shard_map/pallas_call | solution.py:1126
  405.4 0.9 copy.19
  406.3 0.7 slice_bitcast_fusion
  407.0 0.0 collective-permute-done
  407.0 0.0 copy-done.7
  407.0 1.1 maximum_select_fusion
  408.1 0.7 copy.21
  (2 shorter events, 0.0 us)
Async XLA Ops:
  329.6 48.6 %copy-start.6 = (bf16[256,1024]{1,0:T(8,128)(2,1)S(1)}, bf16[256,1024]{1,0:T(8,128)(2,1)}, u32[]{:S(2)}) copy-start(bf16[256,1024]{1,0:T(8,128)(2,1)} %get-tuple-element.96) | copy-start | bytes 1572868
  329.6 48.7 %copy-start = (bf16[4,16,768]{2,1,0:T(8,128)(2,1)S(1)}, bf16[4,16,768]{2,1,0:T(8,128)(2,1)}, u32[]{:S(2)}) copy-start(bf16[4,16,768]{2,1,0:T(8,128)(2,1)} %get-tuple-element.102.gp1) | copy-start | bytes 294916
  329.6 48.7 %copy-start.2 = (bf16[96,256]{1,0:T(8,128)(2,1)S(1)}, bf16[96,256]{1,0:T(8,128)(2,1)}, u32[]{:S(2)}) copy-start(bf16[96,256]{1,0:T(8,128)(2,1)} %get-tuple-element.100.gm1) | copy-start | bytes 147460
  329.6 48.7 %copy-start.4 = (bf16[16,1024]{1,0:T(8,128)(2,1)S(1)}, bf16[16,1024]{1,0:T(8,128)(2,1)}, u32[]{:S(2)}) copy-start(bf16[16,1024]{1,0:T(8,128)(2,1)} %get-tuple-element.101.gh1) | copy-start | bytes 98308
  378.1 28.9 %copy-start.7 = (bf16[256,1024]{1,0:T(8,128)(2,1)S(1)}, bf16[256,1024]{1,0:T(8,128)(2,1)}, u32[]{:S(2)}) copy-start(bf16[256,1024]{1,0:T(8,128)(2,1)} %get-tuple-element.95) | copy-start | bytes 1572868
  378.2 28.8 %collective-permute-start = (bf16[256,1024]{1,0:T(8,128)(2,1)S(1)}, bf16[256,1024]{1,0:T(8,128)(2,1)S(1)}, u32[]{:S(2)}, u32[]{:S(2)}) collective-permute-start(bf16[256,1024]{1,0:T(8,128)(2,1)S(1)} %broadcast_select_fusion), channel_id=1, source_target_pairs={{0,16},{16,0},{1,17},{17,1},{2,18},{18,2},{3,19},{19,3},{4,20},{20... | collective-permute-start | bytes 1572872 | tf_op jit(solution)/shard_map/ppermute | solution.py:1001
  378.3 0.9 copy-start.1
  379.2 0.8 copy-start.3
  380.0 0.8 copy-start.5

commit v3 on v2

--- a/solution.py
+++ b/solution.py
@@ -18,257 +18,13 @@
 ADAPTERS = 8
 ADAPTER_COLUMNS = 128
 VMEM_LIMIT = 60 << 20
+LINK_BYTES_PER_US = 72e3
+SKEW = (2, 4)
+DELAYS = (8, 18, 12)
+STRIPS = (256, 128, 384, 128)
 
 MESH = pl.DeviceIdType.MESH
 ANY = pl.BlockSpec(memory_space=pl.ANY)
-
-
-def gather_kernel(*refs):
-    n_w, n_s = 4, 6
-    shards = refs[:n_w]
-    f1_ref, ends_ref = refs[n_w : n_w + 2]
-    small = refs[n_w + 2 : n_w + 2 + n_s - 1]
-    at = n_w + 2 + len(small)
-    outs = refs[at : at + n_w]
-    f1_out, x_out, c_out = refs[at + n_w : at + n_w + 3]
-    small_out = refs[at + n_w + 3 : at + n_w + 3 + len(small)]
-    at += n_w + 3 + len(small)
-    held, held_small, held_ends, held_f1 = refs[at : at + n_w], refs[at + n_w : at + n_w + len(small)], refs[-23], refs[-22]
-    ins = refs[-21]
-    (zs, zr, xs, xr, ys, yr, fxs, fxr, fys, fyr, cs, cr, own, ms, mr, es, er, f1s, f1r, f1c) = refs[-20:]
-    core, z, s = lax.axis_index("section"), lax.axis_index("dp"), lax.axis_index("seq")
-    other = 1 - core
-    n_z = 4
-    fetch = [pltpu.make_async_copy(shards[w].at[0], held[w], ins.at[w]) for w in range(n_w)]
-    fetch += [pltpu.make_async_copy(a.at[0], b, ins.at[n_w + i]) for i, (a, b) in enumerate(zip(small, held_small))]
-    fetch.append(pltpu.make_async_copy(ends_ref.at[0, :, 0], held_ends, ins.at[n_w + len(small)]))
-    fetch.append(pltpu.make_async_copy(f1_ref, held_f1, ins.at[n_w + len(small) + 1]))
-    for f in fetch:
-        f.start()
-    barrier = pltpu.get_barrier_semaphore()
-
-    def greet(**where):
-        pl.semaphore_signal(barrier, inc=1, device_id=where, device_id_type=MESH)
-
-    greet(section=other)
-    greet(seq=s ^ 1)
-    greet(seq=s ^ 2)
-    for gap in range(1, n_z):
-        greet(dp=lax.rem(z + gap, n_z))
-    pl.semaphore_wait(barrier, 3 + n_z - 1)
-
-    finals = []
-
-    def remote(src, dst, ssem, rsem, **where):
-        return pltpu.make_async_remote_copy(
-            src_ref=src, dst_ref=dst, send_sem=ssem, recv_sem=rsem, device_id=where, device_id_type=MESH
-        )
-
-    def rows_of(w, j):
-        return shards[w].shape[1] * j
-
-    def piece(w, j, q):
-        r = shards[w].shape[1]
-        return outs[w].at[core, pl.ds(pl.multiple_of(j * r + q * (r // 4), 16), r // 4)]
-
-    def half(w, j, q, low):
-        r = shards[w].shape[1]
-        cut = (r // 8 + 15) // 16 * 16
-        start, size = (0, cut) if low else (cut, r // 4 - cut)
-        return outs[w].at[core, pl.ds(pl.multiple_of(j * r + q * (r // 4) + start, 16), size)]
-
-    def block(w, j):
-        r = shards[w].shape[1]
-        return outs[w].at[core, pl.ds(pl.multiple_of(j * r, 16), r)]
-
-    def own_shard(w):
-        return held[w]
-
-    def own_piece(w):
-        r = shards[w].shape[1]
-        return held[w].at[pl.ds(pl.multiple_of(s * (r // 4), 16), r // 4)]
-
-    def step(d):
-        return 1 if d == 0 else -1
-
-    def can_send(d, t):
-        has_next = (z < n_z - 1) if d == 0 else (z > 0)
-        origin = z - step(d) * (t - 1)
-        return jnp.logical_and(has_next, jnp.logical_and(origin >= 0, origin < n_z))
-
-    def gets(d, t):
-        origin = z - step(d) * t
-        return jnp.logical_and(origin >= 0, origin < n_z)
-
-    def z_copy(w, d, t):
-        j = z - step(d) * (t - 1)
-        src = own_piece(w) if t == 1 else piece(w, j, s)
-        return remote(src, piece(w, j, s), zs.at[w, d, t - 1], zr.at[w, d, t - 1], dp=z + step(d))
-
-    def origin(d, t):
-        return z - step(d) * t
-
-    def x_copy(w, d, t):
-        return remote(piece(w, origin(d, t), s), piece(w, origin(d, t), s), xs.at[w, d, t - 1], xr.at[w, d, t - 1], seq=s ^ 1)
-
-    def y_copy(w, d, t):
-        return remote(piece(w, origin(d, t), s), piece(w, origin(d, t), s), ys.at[w, d, t - 1], yr.at[w, d, t - 1], seq=s ^ 2)
-
-    def fx_copy(w, d, t):
-        ref = half(w, origin(d, t), s ^ 2, False)
-        return remote(ref, ref, fxs.at[w, d, t - 1], fxr.at[w, d, t - 1], seq=s ^ 1)
-
-    def fy_copy(w, d, t):
-        ref = half(w, origin(d, t), s ^ 1, True)
-        return remote(ref, ref, fys.at[w, d, t - 1], fyr.at[w, d, t - 1], seq=s ^ 2)
-
-    def c_copy(w, d, t):
-        if t == 0:
-            return remote(own_shard(w), block(w, z), cs.at[w, 0, 3], cr.at[w, 0, 3], section=other)
-        ref = block(w, origin(d, t))
-        return remote(ref, ref, cs.at[w, d, t - 1], cr.at[w, d, t - 1], section=other)
-
-    def own_copy(w):
-        return pltpu.make_async_copy(own_shard(w), block(w, z), own.at[w])
-
-    def start_own(w):
-        for d in range(2):
-            @pl.when(can_send(d, 1))
-            def _():
-                z_copy(w, d, 1).start()
-
-    def take_z(w, t):
-        for d in range(2):
-            @pl.when(gets(d, t))
-            def _():
-                z_copy(w, d, t).wait_recv()
-            if t < n_z - 1:
-                @pl.when(can_send(d, t + 1))
-                def _():
-                    z_copy(w, d, t + 1).start()
-            @pl.when(gets(d, t))
-            def _():
-                x_copy(w, d, t).start()
-                y_copy(w, d, t).start()
-
-    def take_xy(w, t):
-        for d in range(2):
-            @pl.when(gets(d, t))
-            def _():
-                x_copy(w, d, t).wait_recv()
-                fy_copy(w, d, t).start()
-                y_copy(w, d, t).wait_recv()
-                fx_copy(w, d, t).start()
-
-    def take_diagonal(w, t):
-        for d in range(2):
-            @pl.when(gets(d, t))
-            def _():
-                fy_copy(w, d, t).wait_recv()
-                fx_copy(w, d, t).wait_recv()
-                c_copy(w, d, t).start()
-
-    ends_to_x = remote(held_ends.at[1], x_out, es, er, section=other)
-    ends_to_c = remote(held_ends.at[0], c_out, es, er, section=other)
-    ends_x = pltpu.make_async_copy(held_ends.at[0], x_out, own.at[n_w])
-    ends_c = pltpu.make_async_copy(held_ends.at[1], c_out, own.at[n_w])
-
-    for f in fetch:
-        f.wait()
-    start_own(0)
-    @pl.when(core == 0)
-    def _():
-        ends_to_x.start()
-        ends_x.start()
-
-    @pl.when(core == 1)
-    def _():
-        ends_to_c.start()
-        ends_c.start()
-
-    def f1_copy(gap):
-        return remote(
-            held_f1, f1_out.at[core, z], f1s.at[gap], f1r.at[gap], dp=lax.rem(z + gap, n_z)
-        )
-    for gap in range(1, n_z):
-        f1_copy(gap).start()
-    f1_own = pltpu.make_async_copy(held_f1, f1_out.at[core, z], own.at[n_w + 1])
-    f1_own.start()
-    smalls = []
-    for i, (a, b) in enumerate(zip(held_small, small_out)):
-        mine = pltpu.make_async_copy(a, b.at[core], own.at[n_w + 2 + i])
-        theirs = remote(a, b.at[core], ms.at[i], mr.at[i], section=other)
-        mine.start()
-        theirs.start()
-        smalls.append((mine, theirs))
-    for w in range(n_w):
-        own_copy(w).start()
-        c_copy(w, 0, 0).start()
-    items = [(w, t) for w in range(n_w) for t in range(1, n_z)]
-    f1_sends = [f1_copy(gap) for gap in range(1, n_z)]
-    f1_cross = remote(f1_out.at[core], f1_out.at[core], f1c.at[0], f1c.at[1], section=other)
-    for i in range(len(items) + 2):
-        if i < len(items):
-            w, t = items[i]
-            if t == 1 and w + 1 < n_w:
-                start_own(w + 1)
-            take_z(w, t)
-        if 0 <= i - 1 < len(items):
-            take_xy(*items[i - 1])
-        if 0 <= i - 2 < len(items):
-            take_diagonal(*items[i - 2])
-        if i == 1:
-            f1_own.wait()
-            for c in f1_sends:
-                c.wait_recv()
-            f1_cross.start()
-    for w in range(n_w):
-        own_copy(w).wait()
-        c_copy(w, 0, 0).wait()
-        for d in range(2):
-            for t in range(1, n_z):
-                @pl.when(can_send(d, t))
-                def _():
-                    z_copy(w, d, t).wait_send()
-                @pl.when(gets(d, t))
-                def _():
-                    x_copy(w, d, t).wait_send()
-                    y_copy(w, d, t).wait_send()
-                    fx_copy(w, d, t).wait_send()
-                    fy_copy(w, d, t).wait_send()
-                    c_copy(w, d, t).wait()
-    for mine, theirs in smalls:
-        mine.wait()
-        theirs.wait()
-    for c in f1_sends:
-        c.wait_send()
-    f1_cross.wait()
-    ends_x.wait()
-    ends_to_x.wait()
-
-
-def gather_all(shards, f1t, ends, small):
-    n_w = 4
-    shape = jax.ShapeDtypeStruct
-    outs = [shape((2, 4 * w.shape[1], w.shape[2]), w.dtype) for w in shards]
-    outs.append(shape((2, 4) + f1t.shape, f1t.dtype))
-    outs += [shape(ends.shape[3:], ends.dtype)] * 2
-    outs += [shape((2,) + a.shape[1:], a.dtype) for a in small]
-    dma = pltpu.SemaphoreType.DMA
-    per = [dma((n_w, 2, 3)) for _ in range(10)] + [dma((n_w, 2, 4)) for _ in range(2)]
-    return pl.pallas_call(
-        gather_kernel,
-        out_shape=outs,
-        in_specs=[ANY] * (n_w + 2 + len(small)),
-        out_specs=[ANY] * len(outs),
-        scratch_shapes=[pltpu.VMEM(w.shape[1:], w.dtype) for w in shards]
-        + [pltpu.VMEM(a.shape[1:], a.dtype) for a in small]
-        + [pltpu.VMEM((2,) + ends.shape[3:], ends.dtype), pltpu.VMEM(f1t.shape, f1t.dtype)]
-        + [dma((n_w + len(small) + 2,))]
-        + per
-        + [dma((n_w + 2 + len(small),)), dma((len(small),)), dma((len(small),)), dma, dma, dma((4,)), dma((4,)), dma((2,))],
-        compiler_params=pltpu.CompilerParams(collective_id=0, has_side_effects=True, vmem_limit_bytes=VMEM_LIMIT),
-    )(*shards, f1t, ends, *small)
 
 
 BF = jnp.bfloat16
@@ -339,6 +95,7 @@
     def finish(self):
         for copy in self.open:
             copy.wait()
+        self.open = []
 
 
 def picked(adapter, width):
@@ -377,38 +134,33 @@
     return (at < length).astype(F32)
 
 
-def forward_kernel(
-    layer, n_blocks, meta, h_in, w_mi, w_mo, w_fi, w_fo, w_f1, w_f2, w_b, w_am, w_ah, w_au,
-    y_out, o_ad, o_og, o_qkv, o_gl, o_st, o_mix, o_yh, o_rh, o_ao, o_mid, o_af, o_gu, o_dn,
-    h, mi, mo, fi, fo, f1, f2, bias, am, ah, au,
-    y, ad, og, qkv, gl, st, mix, yh, rh, ao, mid, af, gu, dn,
-    normed, send, glsend, fg, state, gated, hidden,
-    lsem, ssem, rsem,
-):
+def forward_steps(layer, n_blocks, meta, loc, weights, buffers, work, outs, sems):
+    w, v = weights, buffers
+    (h, y, ad, og, qkv, gl, st, mix, yh, rh, ao, mid, af, gu, dn, normed, send, glsend, fg, state, gated, hidden) = work
+    o_y, o_ad, o_og, o_qkv, o_gl, o_st, o_mix, o_yh, o_rh, o_ao, o_mid, o_af, o_gu, o_dn = outs
+    ssem, rsem = sems
     me = lax.axis_index("seq")
     T = h.shape[0]
     per = T // GROUP
     adapter = meta[2 * n_blocks]
     length = meta[2 * n_blocks + 1]
-    loc = Local(lsem)
-    l_h = loc.start(h_in, h)
-    l_f1 = loc.start(w_f1.at[layer], f1)
-    l_f2 = loc.start(w_f2.at[layer], f2)
-    l_b = loc.start(w_b.at[layer], bias)
-    l_am = loc.start(w_am.at[layer], am)
-    l_au = loc.start(w_au.at[layer], au)
-    l_mi = loc.start(w_mi.at[layer], mi)
-    greet_peers(me)
-    l_ah = loc.start(w_ah.at[layer], ah)
-    l_mo = loc.start(w_mo.at[layer], mo)
-    l_fi = loc.start(w_fi.at[layer], fi)
-    l_fo = loc.start(w_fo.at[layer], fo)
     mask = column_mask(adapter)
-
-    l_h.wait()
+    am, ah, au, mi, mo, fi, fo = [v[name] for name in ("am", "ah", "au", "mi", "mo", "fi", "fo")]
+
+    def load(*names):
+        return [loc.start(w[name], v[name]) for name in names]
+
+    def wait(copies):
+        for c in copies:
+            c.wait()
+
+    yield "small", 0
+    small = load("f1", "f2", "b", "am", "au", "ah")
+    yield None, 2
     hv = h[...].astype(F32)
     normed[...] = (hv * inverse_rms(hv)).astype(BF)
-    l_f1.wait()
+    wait(small)
+    f1, f2, bias = v["f1"], v["f2"], v["b"]
     z_w = f1.shape[2]
     low = nt(f1[0], normed[:, 0:z_w])
     for j in range(1, f1.shape[0]):
@@ -418,12 +170,21 @@
     for c in low_copies:
         c.start()
     gl[me] = glsend[...]
-    l_am.wait()
+    yield "delay", DELAYS[0]
     for p in range(4):
         cols = pl.ds(p * ADAPTER_COLUMNS, ADAPTER_COLUMNS)
         ad[:, cols] = (nn(normed[...], am[:, cols]) * mask).astype(BF)
-    l_au.wait()
-    l_mi.wait()
+    f2h = f2[:, lanes(me * DK, DK)]
+    bh = bias[:, lanes(me * DK, DK)]
+    for c in low_copies:
+        c.wait_recv()
+    for src in range(HEADS):
+        logit = tn(gl[src], f2h) + bh
+        fg[src * T : (src + 1) * T, :] = (jax.nn.log_sigmoid(logit) / 16.0).astype(BF)
+    loc.start(gl, o_gl, True)
+    loc.start(ad, o_ad, True)
+    yield "mi", 0
+    wait(load("mi"))
 
     def project(w_start, p, width):
         cols = lanes(w_start, width)
@@ -436,31 +197,23 @@
 
     qkv_copies = []
     for d in range(1, HEADS):
+        yield None, 1
         chunk(me ^ d, send.at[d - 1])
         copy = to_peer(send.at[d - 1], qkv.at[rows(me * T, T)], ssem.at[1, d], rsem.at[1, d], me ^ d)
         copy.start()
         qkv_copies.append(copy)
+    yield None, 1
     chunk(me, qkv.at[rows(me * T, T)])
-    loc.start(ad, o_ad, True)
+    yield None, 1
     for j in range(VALUE_WIDTH // TILE):
         og[:, j * TILE : (j + 1) * TILE] = project(2 * KEY + VALUE_WIDTH + j * TILE, 3, TILE)
     loc.start(og, o_og, True)
-    l_f2.wait()
-    l_b.wait()
-    for c in low_copies:
-        c.wait_recv()
-    f2h = f2[:, lanes(me * DK, DK)]
-    bh = bias[:, lanes(me * DK, DK)]
-    for src in range(HEADS):
-        logit = tn(gl[src], f2h) + bh
-        fg[src * T : (src + 1) * T, :] = (jax.nn.log_sigmoid(logit) / 16.0).astype(BF)
+    yield "delay", DELAYS[1]
     for c in qkv_copies:
         c.wait_recv()
-    loc.start(gl, o_gl, True)
     loc.start(qkv, o_qkv, True)
     tri = lower_triangle(BF)
     causal = lower_triangle(F32)
-
     state[...] = jnp.zeros_like(state)
 
     def advance(n, carry):
@@ -477,6 +230,7 @@
 
     lax.fori_loop(0, n_blocks, advance, 0, unroll=4)
     loc.start(st, o_st, True)
+    yield None, 4
 
     def mix_block(p):
         n = meta[p]
@@ -495,24 +249,28 @@
 
     mix_copies = []
     for d in range(1, HEADS):
+        yield None, 2
         peer = me ^ d
         lax.fori_loop(0, per, lambda j, c, peer=peer: (mix_block(peer * per + j), c)[1], 0, unroll=True)
         copy = to_peer(yh.at[rows(peer * T, T)], mix.at[me], ssem.at[2, d], rsem.at[2, d], peer)
         copy.start()
         mix_copies.append(copy)
+    yield None, 2
     lax.fori_loop(0, per, lambda j, c: (mix_block(me * per + j), c)[1], 0, unroll=True)
     mix[me] = yh[rows(me * T, T), :]
     loc.start(yh, o_yh, True)
     loc.start(rh, o_rh, True)
+    yield "mo", 0
+    l_mo = load("mo")
+    yield "delay", DELAYS[2]
     for c in mix_copies:
         c.wait_recv()
     loc.start(mix, o_mix, True)
     for hd in range(HEADS):
         cols = slice(hd * DV, (hd + 1) * DV)
         gated[:, cols] = (mix[hd].astype(F32) * silu_parts(og[:, cols])[0]).astype(BF)
-    l_ah.wait()
-    l_mo.wait()
     ao[...] = (nn(gated[...], ah[0:VALUE_WIDTH, :]) * mask).astype(BF)
+    wait(l_mo)
     for j in range(MODEL_WIDTH // TILE):
         cols = slice(j * TILE, (j + 1) * TILE)
         mid[:, cols] = (
@@ -520,6 +278,7 @@
         )
     loc.start(ao, o_ao, True)
     loc.start(mid, o_mid, True)
+    yield None, 1
     mv = mid[...]
     normed[...] = (mv * inverse_rms(mv)).astype(BF)
     for p in range(2):
@@ -527,7 +286,8 @@
         wide = slice((4 + p) * ADAPTER_COLUMNS, (5 + p) * ADAPTER_COLUMNS)
         af[:, cols] = (nn(normed[...], am[:, wide]) * mask).astype(BF)
     loc.start(af, o_af, True)
-    l_fi.wait()
+    yield "fi", 0
+    wait(load("fi"))
 
     def up_tile(i, carry):
         a, b = lanes(i * TILE, TILE), lanes(HIDDEN_UNITS + i * TILE, TILE)
@@ -538,20 +298,44 @@
         hidden[:, a] = (silu_parts(gate)[0] * up).astype(BF)
         return carry
 
-    lax.fori_loop(0, HIDDEN_UNITS // TILE, up_tile, 0)
+    tiles = HIDDEN_UNITS // TILE
+    yield None, 3
+    lax.fori_loop(0, tiles // 2, up_tile, 0)
+    yield None, 3
+    lax.fori_loop(tiles // 2, tiles, up_tile, 0)
     loc.start(gu, o_gu, True)
-    l_fo.wait()
     dn[...] = (nn(hidden[...], ah[VALUE_WIDTH:, :]) * mask).astype(BF)
     loc.start(dn, o_dn, True)
+    yield "fo", 0
+    wait(load("fo"))
+    yield None, 3
     for j in range(MODEL_WIDTH // TILE):
         cols = slice(j * TILE, (j + 1) * TILE)
         y[:, cols] = (
             mid[:, cols] + nn(hidden[...], fo[:, cols]) + nn(dn[...], au[:, U_D + j * TILE : U_D + (j + 1) * TILE])
         ).astype(BF)
-    loc.start(y, y_out, True)
+    loc.start(y, o_y, True)
     loc.finish()
     for c in low_copies + qkv_copies + mix_copies:
         c.wait_send()
+
+
+NAMES = ("mi", "mo", "fi", "fo", "f1", "f2", "b", "am", "ah", "au")
+
+
+def forward_kernel(layer, n_blocks, meta, h_in, *refs):
+    n_w, n_out = len(NAMES), 14
+    ins, outs = refs[:n_w], refs[n_w : n_w + n_out]
+    refs = refs[n_w + n_out :]
+    buffers, work = dict(zip(NAMES, refs[:n_w])), refs[n_w:-3]
+    lsem, ssem, rsem = refs[-3:]
+    loc = Local(lsem)
+    first = loc.start(h_in, work[0])
+    greet_peers(lax.axis_index("seq"))
+    first.wait()
+    weights = {name: ref.at[layer] for name, ref in zip(NAMES, ins)}
+    for _ in forward_steps(layer, n_blocks, meta, loc, weights, buffers, work, outs, (ssem, rsem)):
+        pass
 
 
 def weight_scratch(weights):
@@ -578,37 +362,36 @@
     ]
 
 
+def work_scratch(T, L, saved):
+    vm = pltpu.VMEM
+    return [vm((T, MODEL_WIDTH), BF)] + [vm(*s) for s in saved] + [
+        vm((T, MODEL_WIDTH), BF),
+        vm((HEADS - 1, T, CHUNK), BF),
+        vm((FGATE_RANK, T), BF),
+        vm((L, DK), BF),
+        vm((DV, DK), F32),
+        vm((T, VALUE_WIDTH), BF),
+        vm((T, HIDDEN_UNITS), BF),
+    ]
+
+
 def forward(layer, meta, h, weights):
     T = h.shape[0]
     L = T * HEADS
     n_blocks = L // GROUP
     saved = saved_shapes(T, L, n_blocks)
-    vm = pltpu.VMEM
     dma = pltpu.SemaphoreType.DMA
     return pl.pallas_call(
         functools.partial(forward_kernel, layer, n_blocks),
         out_shape=[jax.ShapeDtypeStruct(*s) for s in saved],
         in_specs=[pl.BlockSpec(memory_space=pltpu.SMEM)] + [ANY] * (1 + len(weights)),
         out_specs=[ANY] * len(saved),
-        scratch_shapes=[vm(h.shape, h.dtype)]
-        + weight_scratch(weights)
-        + [vm(*s) for s in saved]
-        + [
-            vm((T, MODEL_WIDTH), BF),
-            vm((HEADS - 1, T, CHUNK), BF),
-            vm((FGATE_RANK, T), BF),
-            vm((L, DK), BF),
-            vm((DV, DK), F32),
-            vm((T, VALUE_WIDTH), BF),
-            vm((T, HIDDEN_UNITS), BF),
-            dma((1 + len(weights) + len(saved),)),
-            dma((3, HEADS)),
-            dma((3, HEADS)),
-        ],
+        scratch_shapes=weight_scratch(weights)
+        + work_scratch(T, L, saved)
+        + [dma((1 + len(weights) + len(saved),)), dma((3, HEADS)), dma((3, HEADS))],
         compiler_params=pltpu.CompilerParams(
             collective_id=1 + layer, has_side_effects=True, vmem_limit_bytes=VMEM_LIMIT
         ),
-        cost_estimate=pl.CostEstimate(flops=2 * T * 13_000_000, bytes_accessed=40 << 20, transcendentals=T * 8192),
     )(meta, h, *weights)
 
 
@@ -997,6 +780,358 @@
     )(meta, d, h, *weights, *saved)
 
 
+UNITS = [(layer, w) for layer in range(2) for w in range(4)]
+
+
+def model_kernel(n_blocks, meta, *refs):
+    n_w, n_small, n_saved, n_z = 4, 5, 14, 4
+    refs = list(refs)
+
+    def take(n):
+        out = refs[:n]
+        del refs[:n]
+        return out
+
+    shards = take(n_w)
+    f1_ref, ends_ref = take(2)
+    small = take(n_small)
+    outs = take(n_w)
+    (f1_out,) = take(1)
+    (x_out, c_out) = take(2)
+    small_out = take(n_small)
+    saved = [take(n_saved), take(n_saved)]
+    held = take(n_w)
+    held_f1 = take(1)[0]
+    held_small = take(n_small)
+    work = take(1 + n_saved + 7)
+    qkv2, gl2, mix2, held_ends = take(4)
+    (ins, zs, zr, ts, tr, xs, xr, ys, yr, fxs, fxr, fys, fyr, cs, cr, own, ms, mr, es, er, f1s, f1r, f1c, lsem, ssem, rsem) = take(26)
+    core, z, s = lax.axis_index("section"), lax.axis_index("dp"), lax.axis_index("seq")
+    other = 1 - core
+
+    def remote(src, dst, send_sem, recv_sem, **where):
+        return pltpu.make_async_remote_copy(
+            src_ref=src, dst_ref=dst, send_sem=send_sem, recv_sem=recv_sem, device_id=where, device_id_type=MESH
+        )
+
+    def height(w):
+        return shards[w].shape[1]
+
+    def staged(w):
+        return held[w].at[pl.ds(pl.multiple_of(z * height(w), 16), height(w))]
+
+    fetch = [pltpu.make_async_copy(shards[w].at[0], staged(w), ins.at[w]) for w in range(n_w)]
+    fetch += [pltpu.make_async_copy(a.at[0], b, ins.at[n_w + i]) for i, (a, b) in enumerate(zip(small, held_small))]
+    fetch.append(pltpu.make_async_copy(ends_ref.at[0, :, 0], held_ends, ins.at[n_w + n_small]))
+    fetch.append(pltpu.make_async_copy(f1_ref, held_f1.at[z], ins.at[n_w + n_small + 1]))
+    for f in fetch:
+        f.start()
+
+    barrier = pltpu.get_barrier_semaphore()
+    greeted = [dict(section=other)] + [dict(seq=s ^ k) for k in range(1, HEADS)]
+    greeted += [dict(dp=lax.rem(z + gap, n_z)) for gap in range(1, n_z)]
+    for where in greeted:
+        pl.semaphore_signal(barrier, inc=1, device_id=where, device_id_type=MESH)
+    pl.semaphore_wait(barrier, len(greeted))
+
+    def part(u, j, start, size, strip=False):
+        layer, w = UNITS[u]
+        cols = shards[w].shape[2] // 2
+        at, wide = (cols - STRIPS[w], STRIPS[w]) if strip else (0, cols - STRIPS[w])
+        return outs[w].at[layer, pl.ds(pl.multiple_of(j * height(w) + start, 16), size), lanes(core * cols + at, wide)]
+
+    def piece(u, j, q):
+        r = height(UNITS[u][1])
+        return part(u, j, q * (r // 4), r // 4)
+
+    def half(u, j, q, low):
+        r = height(UNITS[u][1])
+        cut = (r // 8 + 15) // 16 * 16
+        start, size = (0, cut) if low else (cut, r // 4 - cut)
+        return part(u, j, q * (r // 4) + start, size)
+
+    def block(u, j):
+        layer, w = UNITS[u]
+        cols = shards[w].shape[2] // 2
+        return outs[w].at[layer, pl.ds(pl.multiple_of(j * height(w), 16), height(w)), lanes(core * cols, cols)]
+
+    def whole_block(layer, w):
+        return outs[w].at[layer, pl.ds(pl.multiple_of(z * height(w), 16), height(w))]
+
+    def step(d):
+        return 1 if d == 0 else -1
+
+    def can_send(d, t):
+        has_next = (z < n_z - 1) if d == 0 else (z > 0)
+        first = z - step(d) * (t - 1)
+        return jnp.logical_and(has_next, jnp.logical_and(first >= 0, first < n_z))
+
+    def gets(d, t):
+        first = z - step(d) * t
+        return jnp.logical_and(first >= 0, first < n_z)
+
+    def origin(d, t):
+        return z - step(d) * t
+
+    def z_copy(u, d, t):
+        ref = piece(u, z - step(d) * (t - 1), s)
+        return remote(ref, ref, zs.at[u, d, t - 1], zr.at[u, d, t - 1], dp=z + step(d))
+
+    def t_copy(u, d, t):
+        ref = part(u, z - step(d) * (t - 1), 0, height(UNITS[u][1]), True)
+        return remote(ref, ref, ts.at[u, d, t - 1], tr.at[u, d, t - 1], dp=z + step(d))
+
+    def x_copy(u, d, t):
+        ref = piece(u, origin(d, t), s)
+        return remote(ref, ref, xs.at[u, d, t - 1], xr.at[u, d, t - 1], seq=s ^ 1)
+
+    def y_copy(u, d, t):
+        ref = piece(u, origin(d, t), s)
+        return remote(ref, ref, ys.at[u, d, t - 1], yr.at[u, d, t - 1], seq=s ^ 2)
+
+    def fx_copy(u, d, t):
+        ref = half(u, origin(d, t), s ^ 2, False)
+        return remote(ref, ref, fxs.at[u, d, t - 1], fxr.at[u, d, t - 1], seq=s ^ 1)
+
+    def fy_copy(u, d, t):
+        ref = half(u, origin(d, t), s ^ 1, True)
+        return remote(ref, ref, fys.at[u, d, t - 1], fyr.at[u, d, t - 1], seq=s ^ 2)
+
+    def c_copy(u, d, t):
+        ref = block(u, origin(d, t))
+        return remote(ref, ref, cs.at[u, d, t - 1], cr.at[u, d, t - 1], section=other)
+
+    def own_copy(w):
+        return pltpu.make_async_copy(staged(w), whole_block(core, w), own.at[w])
+
+    def own_cross(w):
+        return remote(staged(w), whole_block(core, w), ms.at[n_small + w], mr.at[n_small + w], section=other)
+
+    def start_own(u):
+        layer, w = UNITS[u]
+
+        if layer == 0:
+            own_copy(w).wait()
+
+        @pl.when(core != layer)
+        def _():
+            own_cross(w).wait_recv()
+
+        for d in range(2):
+            @pl.when(can_send(d, 1))
+            def _():
+                z_copy(u, d, 1).start()
+                t_copy(u, d, 1).start()
+
+    def take_z(u, t):
+        for d in range(2):
+            @pl.when(gets(d, t))
+            def _():
+                z_copy(u, d, t).wait_recv()
+            if t < n_z - 1:
+                @pl.when(can_send(d, t + 1))
+                def _():
+                    z_copy(u, d, t + 1).start()
+            @pl.when(gets(d, t))
+            def _():
+                x_copy(u, d, t).start()
+                y_copy(u, d, t).start()
+                t_copy(u, d, t).wait_recv()
+            if t < n_z - 1:
+                @pl.when(can_send(d, t + 1))
+                def _():
+                    t_copy(u, d, t + 1).start()
+
+    def take_xy(u, t):
+        for d in range(2):
+            @pl.when(gets(d, t))
+            def _():
+                x_copy(u, d, t).wait_recv()
+                fy_copy(u, d, t).start()
+                y_copy(u, d, t).wait_recv()
+                fx_copy(u, d, t).start()
+
+    def take_diagonal(u, t):
+        for d in range(2):
+            @pl.when(gets(d, t))
+            def _():
+                fy_copy(u, d, t).wait_recv()
+                fx_copy(u, d, t).wait_recv()
+                c_copy(u, d, t).start()
+
+    def take_core(u):
+        for d in range(2):
+            for t in range(1, n_z):
+                @pl.when(gets(d, t))
+                def _():
+                    c_copy(u, d, t).wait_recv()
+
+    for f in fetch:
+        f.wait()
+    for w in range(n_w):
+        own_copy(w).start()
+        own_cross(w).start()
+
+    def f1_copy(gap):
+        return remote(held_f1.at[z], f1_out.at[core, z], f1s.at[gap], f1r.at[gap], dp=lax.rem(z + gap, n_z))
+
+    f1_sends = [f1_copy(gap) for gap in range(1, n_z)]
+    for c in f1_sends:
+        c.start()
+    f1_own = pltpu.make_async_copy(held_f1.at[z], f1_out.at[core, z], own.at[n_w])
+    f1_own.start()
+    smalls = []
+    for i, (a, b) in enumerate(zip(held_small, small_out)):
+        mine = pltpu.make_async_copy(a, b.at[core], own.at[n_w + 2 + i])
+        theirs = remote(a, b.at[core], ms.at[i], mr.at[i], section=other)
+        mine.start()
+        theirs.start()
+        smalls.append((mine, theirs))
+    ends_to_x = remote(held_ends.at[1], x_out, es, er, section=other)
+    ends_to_c = remote(held_ends.at[0], c_out, es, er, section=other)
+    ends_x = pltpu.make_async_copy(held_ends.at[0], x_out, own.at[n_w + 1])
+    ends_c = pltpu.make_async_copy(held_ends.at[1], c_out, own.at[n_w + 1])
+
+    @pl.when(core == 0)
+    def _():
+        ends_to_x.start()
+        ends_x.start()
+
+    @pl.when(core == 1)
+    def _():
+        ends_to_c.start()
+        ends_c.start()
+
+    f1_cross = remote(f1_out.at[core], f1_out.at[core], f1c.at[0], f1c.at[1], section=other)
+    start_own(0)
+    f1_own.wait()
+    for c in f1_sends:
+        c.wait_recv()
+    f1_cross.start()
+    for w in range(n_w):
+        own_cross(w).wait_send()
+    for mine, theirs in smalls:
+        mine.wait()
+        theirs.wait()
+    for c in f1_sends:
+        c.wait_send()
+    f1_cross.wait()
+    ends_x.wait()
+    ends_to_x.wait()
+
+    items = [(u, t) for u in range(len(UNITS)) for t in range(1, n_z)]
+    ready, clock = [], 8.0
+    for u, t in items:
+        r, c = shards[UNITS[u][1]].shape[1:]
+        clock += r // 4 * (c - 2 * STRIPS[UNITS[u][1]]) * 3 / LINK_BYTES_PER_US
+        ready.append(clock)
+
+    def gather_step(i):
+        if i < len(items):
+            u, t = items[i]
+            if t == 1 and u + 1 < len(UNITS):
+                start_own(u + 1)
+            take_z(u, t)
+        if 0 <= i - SKEW[0] < len(items):
+            take_xy(*items[i - SKEW[0]])
+        if 0 <= i - SKEW[1] < len(items):
+            take_diagonal(*items[i - SKEW[1]])
+
+    loc = Local(lsem)
+    loaded = loc.start(x_out, work[0])
+    loaded.wait()
+    n_steps = len(items) + SKEW[1]
+    works = [list(work), list(work)]
+    for at, ref in ((4, qkv2), (5, gl2), (7, mix2)):
+        works[1][at] = ref
+
+    def both_layers():
+        for layer in range(2):
+            sources = dict(zip(NAMES[:4], outs))
+            sources["f1"] = f1_out
+            sources.update(zip(NAMES[5:], small_out))
+            sources = {name: ref.at[layer] for name, ref in sources.items()}
+            buffers = dict(zip(NAMES, held + [held_f1] + held_small))
+            for what, us in forward_steps(
+                layer, n_blocks, meta, loc, sources, buffers, works[layer], saved[layer], (ssem.at[layer], rsem.at[layer])
+            ):
+                yield layer, what, us
+            if layer == 0:
+                work[0][...] = work[1][...]
+
+    steps, done, now, crossed, until = both_layers(), 0, 8.0, set(), None
+    pending = next(steps)
+    while pending is not None or done < n_steps:
+        due = ready[min(max(done - 2, 0), len(ready) - 1)]
+        blocked = False
+        if pending is not None and pending[1] in NAMES[:4]:
+            u = UNITS.index((pending[0], NAMES.index(pending[1])))
+            blocked = done < min(3 * u + 3 + SKEW[1], n_steps)
+            if not blocked:
+                take_core(u)
+                crossed.add(u)
+        elif pending is not None and pending[1] == "delay":
+            until = now + pending[2] if until is None else until
+            blocked = now < until and due < until
+        if done < n_steps and (pending is None or blocked or due <= now):
+            now = max(now, due)
+            gather_step(done)
+            done += 1
+            continue
+        now = now + pending[2] if until is None else max(now, until)
+        until = None
+        pending = next(steps, None)
+    for u in range(len(UNITS)):
+        if u not in crossed:
+            take_core(u)
+        for d in range(2):
+            for t in range(1, n_z):
+                @pl.when(can_send(d, t))
+                def _():
+                    z_copy(u, d, t).wait_send()
+                    t_copy(u, d, t).wait_send()
+                @pl.when(gets(d, t))
+                def _():
+                    x_copy(u, d, t).wait_send()
+                    y_copy(u, d, t).wait_send()
+                    fx_copy(u, d, t).wait_send()
+                    fy_copy(u, d, t).wait_send()
+                    c_copy(u, d, t).wait_send()
+
+
+def forward_model(meta, shards, f1t, ends, small):
+    shape, dma, vm = jax.ShapeDtypeStruct, pltpu.SemaphoreType.DMA, pltpu.VMEM
+    T = ends.shape[3]
+    L = T * HEADS
+    n_blocks = L // GROUP
+    saved = saved_shapes(T, L, n_blocks)
+    n_w, n_small, n_u = len(shards), len(small), len(UNITS)
+    outs = [shape((2, 4 * w.shape[1], w.shape[2]), w.dtype) for w in shards]
+    outs.append(shape((2, 4) + f1t.shape, f1t.dtype))
+    outs += [shape(ends.shape[3:], ends.dtype)] * 2
+    outs += [shape((2,) + a.shape[1:], a.dtype) for a in small]
+    outs += [shape(*s) for s in saved] * 2
+    full = [vm((4 * w.shape[1], w.shape[2]), w.dtype) for w in shards]
+    out = pl.pallas_call(
+        functools.partial(model_kernel, n_blocks),
+        out_shape=outs,
+        in_specs=[pl.BlockSpec(memory_space=pltpu.SMEM)] + [ANY] * (n_w + 2 + n_small),
+        out_specs=[ANY] * len(outs),
+        scratch_shapes=full
+        + [vm((4,) + f1t.shape, f1t.dtype)]
+        + [vm(a.shape[1:], a.dtype) for a in small]
+        + work_scratch(T, L, saved)
+        + [vm((L, CHUNK), BF), vm((HEADS, FGATE_RANK, T), BF), vm((HEADS, T, DV), BF), vm((2,) + ends.shape[3:], BF)]
+        + [dma((n_w + n_small + 2,))]
+        + [dma((n_u, 2, 3)) for _ in range(14)]
+        + [dma((n_w + n_small + 2,)), dma((n_small + n_w,)), dma((n_small + n_w,)), dma, dma, dma((4,)), dma((4,)), dma((2,))]
+        + [dma((1 + 2 * (len(NAMES) + len(saved)),)), dma((2, 3, HEADS)), dma((2, 3, HEADS))],
+        compiler_params=pltpu.CompilerParams(collective_id=0, has_side_effects=True, vmem_limit_bytes=VMEM_LIMIT),
+    )(meta, *shards, f1t, ends, *small)
+    weights = list(out[:5]) + list(out[7:12])
+    return weights, out[5], out[6], out[12 : 12 + len(saved)], out[12 + len(saved) :]
+
+
 def swap_sections(v):
     return lax.ppermute(v, "section", [(0, 1), (1, 0)])
 
@@ -1212,12 +1347,13 @@
         adapter_hidden_first,
         adapter_second_maps,
     ]
-    gather = gather_all if own_kernels else plain_gather
-    out = gather(shards, forget_first_map[0].T, ends, small)
-    weights = list(out[:5]) + list(out[7:])
-    x, cotangent = out[5], out[6]
-    early = forward(0, meta, x, weights)
-    late = forward(1, meta, early[0], weights)
+    if own_kernels:
+        weights, x, cotangent, early, late = forward_model(meta, shards, forget_first_map[0].T, ends, small)
+    else:
+        out = plain_gather(shards, forget_first_map[0].T, ends, small)
+        weights, x, cotangent = list(out[:5]) + list(out[7:]), out[5], out[6]
+        early = forward(0, meta, x, weights)
+        late = forward(1, meta, early[0], weights)
     middle, *grads_late = backward(1, meta, cotangent, early[0], weights, late[1:], n_dp)
     entry, *grads_early = backward(0, meta, middle, x, weights, early[1:], n_dp)
     sent = swap_sections(jnp.where(first, late[0], entry))

time: 415 us -> 391 us (0.942)
  Pallas kernels: 395 us -> 372 us
    pallas_call x3 -> x1, Pallas kernels: 273 us -> 249 us  [forward_model(): pl.pallas_call(functools.partial(model_kernel, n_blocks), out_shape=outs,...]
  transfers between devices with their start and end apart: 1 -> 1, of which waited for: 0 -> 0; matrix products, arithmetic and copies ran while one was open for 0% -> 0% of each run, Pallas kernels for 6% -> 7%
where the time goes in v3:
time: 391 us; the launch traced here: 386 us
  Pallas kernels  372 us (95%)
  local copies, waits for them, and re-layouts  7.32 us (2%)
    pallas_call x1, Pallas kernels, forward_model(): pl.pallas_call(functools.partial(model_kernel, n_blocks), out_shape=outs,...  249 us
    pallas_call x2, Pallas kernels, backward(): pl.pallas_call(functools.partial(backward_kernel, layer, n_blocks), out_s...  98 us
    pallas_call x1, Pallas kernels, reduce_gradients(): pl.pallas_call(reduce_kernel, out_shape=[shape((own_m, MODEL_WIDTH), F32)...  25.6 us
  transfers between devices with their start and end apart: 1, of which 0 were waited for; matrix products, arithmetic and copies ran while one was open for 0% of the time, Pallas kernels for 7%

profile of v3, /device:TPU:0, one launch (start us, length us, event | category | flops | bytes accessed | tf_op | source)
XLA Modules:
  0.0 386.0 jit_solution(6352311475995888025)
XLA Ops:
  0.6 0.7 fusion
  1.3 0.1 select_reduce_fusion
  1.4 1.3 fusion.2
  2.7 1.3 fusion.1
  6.6 0.6 pad_add_fusion.meta
  7.2 248.7 %shard_map.165 = (bf16[2,1024,3072]{2,1,0:T(8,128)(2,1)}, bf16[2,1024,1024]{2,1,0:T(8,128)(2,1)}, bf16[2,1024,5632]{2,1,0:T(8,128)(2,1)}, bf16[2,2816,1024]{2,1,...) custom-call(s32[34]{0:T(128)} %pad_add_fusion.meta, ...), custom_call_target="tpu_custom_call" | custom-call | tf_op jit(solution)/shard_map/pallas_call | solution.py:1115
  255.9 49.9 %shard_map.166 = (bf16[256,1024]{1,0:T(8,128)(2,1)}, bf16[96,256]{1,0:T(8,128)(2,1)}, bf16[16,1024]{1,0:T(8,128)(2,1)}, bf16[4,16,768]{2,1,0:T(8,128)(2,1)}) custom-call(s32[34]{0:T(128)} %pad_add_fusion.meta, bf16[256,1024]{1,0:T(8,128)(2,1)} %get-tuple-element.55.d_in, bf16[256,1024]{1,0:T(8,128)(2,1)} %get-tuple-element.56.h_in, ...), custom_call_target="tpu_custom_call" | custom-call | flops 8192000000 | bytes 47185920 | tf_op jit(solution)/shard_map/pallas_call | solution.py:732
  305.8 0.0 copy-start.6
  305.8 0.0 copy-start
  305.9 0.0 copy-start.2
  305.9 0.0 copy-start.4
  305.9 48.1 %shard_map.167 = (bf16[256,1024]{1,0:T(8,128)(2,1)}, bf16[96,256]{1,0:T(8,128)(2,1)}, bf16[16,1024]{1,0:T(8,128)(2,1)}, bf16[4,16,768]{2,1,0:T(8,128)(2,1)}) custom-call(s32[34]{0:T(128)} %pad_add_fusion.meta, bf16[256,1024]{1,0:T(8,128)(2,1)} %get-tuple-element.80.d_in, bf16[256,1024]{1,0:T(8,128)(2,1)} %get-tuple-element.81.h_in, ...), custom_call_target="tpu_custom_call" | custom-call | flops 8192000000 | bytes 47185920 | tf_op jit(solution)/shard_map/pallas_call | solution.py:732
  354.0 0.0 copy-start.7
  354.0 0.0 copy-done.6
  354.0 0.1 broadcast_select_fusion
  354.1 0.1 collective-permute-start
  354.1 0.0 copy-done
  354.2 0.0 copy-done.2
  354.2 0.0 copy-done.4
  354.2 0.0 copy-start.1
  354.2 0.9 copy-done.1
  355.1 0.0 copy-start.3
  355.1 0.8 copy-done.3
  355.9 0.0 copy-start.5
  355.9 0.8 copy-done.5
  356.6 25.6 %shard_map.168 = (f32[48,1024]{1,0:T(8,128)S(1)}, f32[8,4096]{1,0:T(8,128)S(1)}, f32[128,672]{1,0:T(8,128)S(1)}) custom-call(bf16[96,256]{1,0:T(8,128)(2,1)S(1)} %copy-done.3, bf16[16,1024]{1,0:T(8,128)(2,1)S(1)} %copy-done.5, bf16[4,16,768]{2,1,0:T(8,128)(2,1)S(1)} %copy-done.1, bf16[96,256]{1,0:T(8,128)(2,1)S(1)} %copy-done.2, ...), custom_call_target="tpu_custom_call" | custom-call | tf_op jit(solution)/shard_map/pallas_call | solution.py:1261
  382.2 0.9 copy.19
  383.1 0.7 slice_bitcast_fusion
  383.8 0.0 collective-permute-done
  383.8 0.0 copy-done.7
  383.8 1.1 maximum_select_fusion
  384.9 0.7 copy.21
Async XLA Ops:
  305.8 48.1 %copy-start.6 = (bf16[256,1024]{1,0:T(8,128)(2,1)S(1)}, bf16[256,1024]{1,0:T(8,128)(2,1)}, u32[]{:S(2)}) copy-start(bf16[256,1024]{1,0:T(8,128)(2,1)} %get-tuple-element.96) | copy-start | bytes 1572868
  305.8 48.3 %copy-start = (bf16[4,16,768]{2,1,0:T(8,128)(2,1)S(1)}, bf16[4,16,768]{2,1,0:T(8,128)(2,1)}, u32[]{:S(2)}) copy-start(bf16[4,16,768]{2,1,0:T(8,128)(2,1)} %get-tuple-element.102.gp1) | copy-start | bytes 294916
  305.9 48.3 %copy-start.2 = (bf16[96,256]{1,0:T(8,128)(2,1)S(1)}, bf16[96,256]{1,0:T(8,128)(2,1)}, u32[]{:S(2)}) copy-start(bf16[96,256]{1,0:T(8,128)(2,1)} %get-tuple-element.100.gm1) | copy-start | bytes 147460
  305.9 48.3 %copy-start.4 = (bf16[16,1024]{1,0:T(8,128)(2,1)S(1)}, bf16[16,1024]{1,0:T(8,128)(2,1)}, u32[]{:S(2)}) copy-start(bf16[16,1024]{1,0:T(8,128)(2,1)} %get-tuple-element.101.gh1) | copy-start | bytes 98308
  354.0 29.8 %copy-start.7 = (bf16[256,1024]{1,0:T(8,128)(2,1)S(1)}, bf16[256,1024]{1,0:T(8,128)(2,1)}, u32[]{:S(2)}) copy-start(bf16[256,1024]{1,0:T(8,128)(2,1)} %get-tuple-element.95) | copy-start | bytes 1572868
  354.1 29.7 %collective-permute-start = (bf16[256,1024]{1,0:T(8,128)(2,1)S(1)}, bf16[256,1024]{1,0:T(8,128)(2,1)S(1)}, u32[]{:S(2)}, u32[]{:S(2)}) collective-permute-start(bf16[256,1024]{1,0:T(8,128)(2,1)S(1)} %broadcast_select_fusion), channel_id=1, source_target_pairs={{0,16},{16,0},{1,17},{17,1},{2,18},{18,2},{3,19},{19,3},{4,20},{20... | collective-permute-start | bytes 1572872 | tf_op jit(solution)/shard_map/ppermute | solution.py:1136
  354.2 0.9 copy-start.1
  355.1 0.8 copy-start.3
  355.9 0.8 copy-start.5

commit v4 on v3

--- a/solution.py
+++ b/solution.py
@@ -966,58 +966,66 @@
                 def _():
                     c_copy(u, d, t).wait_recv()
 
-    for f in fetch:
-        f.wait()
-    for w in range(n_w):
+    def f1_copy(gap):
+        return remote(held_f1.at[z], f1_out.at[core, z], f1s.at[gap], f1r.at[gap], dp=lax.rem(z + gap, n_z))
+
+    def launch(w):
+        fetch[w].wait()
         own_copy(w).start()
         own_cross(w).start()
 
-    def f1_copy(gap):
-        return remote(held_f1.at[z], f1_out.at[core, z], f1s.at[gap], f1r.at[gap], dp=lax.rem(z + gap, n_z))
-
+    launch(0)
+    fetch[-1].wait()
     f1_sends = [f1_copy(gap) for gap in range(1, n_z)]
     for c in f1_sends:
         c.start()
     f1_own = pltpu.make_async_copy(held_f1.at[z], f1_out.at[core, z], own.at[n_w])
     f1_own.start()
-    smalls = []
-    for i, (a, b) in enumerate(zip(held_small, small_out)):
-        mine = pltpu.make_async_copy(a, b.at[core], own.at[n_w + 2 + i])
-        theirs = remote(a, b.at[core], ms.at[i], mr.at[i], section=other)
-        mine.start()
-        theirs.start()
-        smalls.append((mine, theirs))
     ends_to_x = remote(held_ends.at[1], x_out, es, er, section=other)
     ends_to_c = remote(held_ends.at[0], c_out, es, er, section=other)
     ends_x = pltpu.make_async_copy(held_ends.at[0], x_out, own.at[n_w + 1])
     ends_c = pltpu.make_async_copy(held_ends.at[1], c_out, own.at[n_w + 1])
-
-    @pl.when(core == 0)
-    def _():
-        ends_to_x.start()
-        ends_x.start()
-
-    @pl.when(core == 1)
-    def _():
-        ends_to_c.start()
-        ends_c.start()
-
     f1_cross = remote(f1_out.at[core], f1_out.at[core], f1c.at[0], f1c.at[1], section=other)
     start_own(0)
-    f1_own.wait()
-    for c in f1_sends:
-        c.wait_recv()
-    f1_cross.start()
-    for w in range(n_w):
-        own_cross(w).wait_send()
-    for mine, theirs in smalls:
-        mine.wait()
-        theirs.wait()
-    for c in f1_sends:
-        c.wait_send()
-    f1_cross.wait()
-    ends_x.wait()
-    ends_to_x.wait()
+    launch(1)
+    smalls = []
+
+    def launch_rest():
+        fetch[-2].wait()
+
+        @pl.when(core == 0)
+        def _():
+            ends_to_x.start()
+            ends_x.start()
+
+        @pl.when(core == 1)
+        def _():
+            ends_to_c.start()
+            ends_c.start()
+
+        for i, (a, b) in enumerate(zip(held_small, small_out)):
+            fetch[n_w + i].wait()
+            mine = pltpu.make_async_copy(a, b.at[core], own.at[n_w + 2 + i])
+            theirs = remote(a, b.at[core], ms.at[i], mr.at[i], section=other)
+            mine.start()
+            theirs.start()
+            smalls.append((mine, theirs))
+        for w in range(2, n_w):
+            launch(w)
+        f1_own.wait()
+        for c in f1_sends:
+            c.wait_recv()
+        f1_cross.start()
+
+    def settle_small():
+        for mine, theirs in smalls:
+            mine.wait()
+            theirs.wait()
+        for c in f1_sends:
+            c.wait_send()
+        f1_cross.wait()
+        ends_x.wait()
+        ends_to_x.wait()
 
     items = [(u, t) for u in range(len(UNITS)) for t in range(1, n_z)]
     ready, clock = [], 8.0
@@ -1027,6 +1035,8 @@
         ready.append(clock)
 
     def gather_step(i):
+        if i == 1:
+            launch_rest()
         if i < len(items):
             u, t = items[i]
             if t == 1 and u + 1 < len(UNITS):
@@ -1038,8 +1048,6 @@
             take_diagonal(*items[i - SKEW[1]])
 
     loc = Local(lsem)
-    loaded = loc.start(x_out, work[0])
-    loaded.wait()
     n_steps = len(items) + SKEW[1]
     works = [list(work), list(work)]
     for at, ref in ((4, qkv2), (5, gl2), (7, mix2)):
@@ -1070,6 +1078,13 @@
             if not blocked:
                 take_core(u)
                 crossed.add(u)
+                if pending[0] == 0:
+                    own_cross(UNITS[u][1]).wait_send()
+        elif pending is not None and pending[:2] == (0, "small"):
+            blocked = done < 3
+            if not blocked:
+                settle_small()
+                loc.start(x_out, work[0]).wait()
         elif pending is not None and pending[1] == "delay":
             until = now + pending[2] if until is None else until
             blocked = now < until and due < until

time: 391 us -> 383 us (0.980)
  Pallas kernels: 372 us -> 364 us
    pallas_call x1, Pallas kernels: 249 us -> 240 us  [forward_model(): pl.pallas_call(functools.partial(model_kernel, n_blocks), out_shape=outs,...]
  transfers between devices with their start and end apart: 1 -> 1, of which waited for: 0 -> 0; matrix products, arithmetic and copies ran while one was open for 0% -> 0% of each run, Pallas kernels for 7% -> 6%
where the time goes in v4:
time: 383 us; the launch traced here: 378 us
  Pallas kernels  364 us (95%)
  local copies, waits for them, and re-layouts  7.32 us (2%)
    pallas_call x1, Pallas kernels, forward_model(): pl.pallas_call(functools.partial(model_kernel, n_blocks), out_shape=outs,...  240 us
    pallas_call x2, Pallas kernels, backward(): pl.pallas_call(functools.partial(backward_kernel, layer, n_blocks), out_s...  101 us
    pallas_call x1, Pallas kernels, reduce_gradients(): pl.pallas_call(reduce_kernel, out_shape=[shape((own_m, MODEL_WIDTH), F32)...  23.8 us
  transfers between devices with their start and end apart: 1, of which 0 were waited for; matrix products, arithmetic and copies ran while one was open for 0% of the time, Pallas kernels for 6%

profile of v4, /device:TPU:0, one launch (start us, length us, event | category | flops | bytes accessed | tf_op | source)
XLA Modules:
  0.0 377.7 jit_solution(13999717619568630259)
XLA Ops:
  0.6 0.7 fusion
  1.3 0.1 select_reduce_fusion
  1.4 1.3 fusion.2
  2.7 1.3 fusion.1
  6.6 0.6 pad_add_fusion.meta
  7.2 239.6 %shard_map.165 = (bf16[2,1024,3072]{2,1,0:T(8,128)(2,1)}, bf16[2,1024,1024]{2,1,0:T(8,128)(2,1)}, bf16[2,1024,5632]{2,1,0:T(8,128)(2,1)}, bf16[2,2816,1024]{2,1,...) custom-call(s32[34]{0:T(128)} %pad_add_fusion.meta, ...), custom_call_target="tpu_custom_call" | custom-call | tf_op jit(solution)/shard_map/pallas_call | solution.py:1130
  246.8 48.7 %shard_map.166 = (bf16[256,1024]{1,0:T(8,128)(2,1)}, bf16[96,256]{1,0:T(8,128)(2,1)}, bf16[16,1024]{1,0:T(8,128)(2,1)}, bf16[4,16,768]{2,1,0:T(8,128)(2,1)}) custom-call(s32[34]{0:T(128)} %pad_add_fusion.meta, bf16[256,1024]{1,0:T(8,128)(2,1)} %get-tuple-element.55.d_in, bf16[256,1024]{1,0:T(8,128)(2,1)} %get-tuple-element.56.h_in, ...), custom_call_target="tpu_custom_call" | custom-call | flops 8192000000 | bytes 47185920 | tf_op jit(solution)/shard_map/pallas_call | solution.py:732
  295.5 0.0 copy-start.6
  295.5 0.0 copy-start
  295.5 0.0 copy-start.2
  295.5 0.0 copy-start.4
  295.6 51.9 %shard_map.167 = (bf16[256,1024]{1,0:T(8,128)(2,1)}, bf16[96,256]{1,0:T(8,128)(2,1)}, bf16[16,1024]{1,0:T(8,128)(2,1)}, bf16[4,16,768]{2,1,0:T(8,128)(2,1)}) custom-call(s32[34]{0:T(128)} %pad_add_fusion.meta, bf16[256,1024]{1,0:T(8,128)(2,1)} %get-tuple-element.80.d_in, bf16[256,1024]{1,0:T(8,128)(2,1)} %get-tuple-element.81.h_in, ...), custom_call_target="tpu_custom_call" | custom-call | flops 8192000000 | bytes 47185920 | tf_op jit(solution)/shard_map/pallas_call | solution.py:732
  347.4 0.0 copy-start.7
  347.4 0.0 copy-done.6
  347.4 0.1 broadcast_select_fusion
  347.5 0.1 collective-permute-start
  347.6 0.0 copy-done
  347.6 0.0 copy-done.2
  347.6 0.0 copy-done.4
  347.6 0.0 copy-start.1
  347.6 0.9 copy-done.1
  348.5 0.0 copy-start.3
  348.5 0.8 copy-done.3
  349.3 0.0 copy-start.5
  349.3 0.8 copy-done.5
  350.1 23.8 %shard_map.168 = (f32[48,1024]{1,0:T(8,128)S(1)}, f32[8,4096]{1,0:T(8,128)S(1)}, f32[128,672]{1,0:T(8,128)S(1)}) custom-call(bf16[96,256]{1,0:T(8,128)(2,1)S(1)} %copy-done.3, bf16[16,1024]{1,0:T(8,128)(2,1)S(1)} %copy-done.5, bf16[4,16,768]{2,1,0:T(8,128)(2,1)S(1)} %copy-done.1, bf16[96,256]{1,0:T(8,128)(2,1)S(1)} %copy-done.2, ...), custom_call_target="tpu_custom_call" | custom-call | tf_op jit(solution)/shard_map/pallas_call | solution.py:1276
  373.9 0.9 copy.19
  374.8 0.7 slice_bitcast_fusion
  375.5 0.0 collective-permute-done
  375.5 0.0 copy-done.7
  375.5 1.1 maximum_select_fusion
  376.6 0.7 copy.21
Async XLA Ops:
  295.5 51.9 %copy-start.6 = (bf16[256,1024]{1,0:T(8,128)(2,1)S(1)}, bf16[256,1024]{1,0:T(8,128)(2,1)}, u32[]{:S(2)}) copy-start(bf16[256,1024]{1,0:T(8,128)(2,1)} %get-tuple-element.96) | copy-start | bytes 1572868
  295.5 52.1 %copy-start = (bf16[4,16,768]{2,1,0:T(8,128)(2,1)S(1)}, bf16[4,16,768]{2,1,0:T(8,128)(2,1)}, u32[]{:S(2)}) copy-start(bf16[4,16,768]{2,1,0:T(8,128)(2,1)} %get-tuple-element.102.gp1) | copy-start | bytes 294916
  295.5 52.1 %copy-start.2 = (bf16[96,256]{1,0:T(8,128)(2,1)S(1)}, bf16[96,256]{1,0:T(8,128)(2,1)}, u32[]{:S(2)}) copy-start(bf16[96,256]{1,0:T(8,128)(2,1)} %get-tuple-element.100.gm1) | copy-start | bytes 147460
  295.5 52.1 %copy-start.4 = (bf16[16,1024]{1,0:T(8,128)(2,1)S(1)}, bf16[16,1024]{1,0:T(8,128)(2,1)}, u32[]{:S(2)}) copy-start(bf16[16,1024]{1,0:T(8,128)(2,1)} %get-tuple-element.101.gh1) | copy-start | bytes 98308
  347.4 28.0 %copy-start.7 = (bf16[256,1024]{1,0:T(8,128)(2,1)S(1)}, bf16[256,1024]{1,0:T(8,128)(2,1)}, u32[]{:S(2)}) copy-start(bf16[256,1024]{1,0:T(8,128)(2,1)} %get-tuple-element.95) | copy-start | bytes 1572868
  347.5 27.9 %collective-permute-start = (bf16[256,1024]{1,0:T(8,128)(2,1)S(1)}, bf16[256,1024]{1,0:T(8,128)(2,1)S(1)}, u32[]{:S(2)}, u32[]{:S(2)}) collective-permute-start(bf16[256,1024]{1,0:T(8,128)(2,1)S(1)} %broadcast_select_fusion), channel_id=1, source_target_pairs={{0,16},{16,0},{1,17},{17,1},{2,18},{18,2},{3,19},{19,3},{4,20},{20... | collective-permute-start | bytes 1572872 | tf_op jit(solution)/shard_map/ppermute | solution.py:1151
  347.6 0.9 copy-start.1
  348.5 0.8 copy-start.3
  349.3 0.8 copy-start.5

commit v5 on v4

--- a/solution.py
+++ b/solution.py
@@ -18,9 +18,9 @@
 ADAPTERS = 8
 ADAPTER_COLUMNS = 128
 VMEM_LIMIT = 60 << 20
-LINK_BYTES_PER_US = 72e3
+LINK_BYTES_PER_US = 60e3
 SKEW = (2, 4)
-DELAYS = (8, 18, 12)
+DELAYS = (8, 25, 20)
 STRIPS = (256, 128, 384, 128)
 
 MESH = pl.DeviceIdType.MESH
@@ -395,46 +395,84 @@
     )(meta, h, *weights)
 
 
-def backward_kernel(
-    layer, n_blocks, meta, d_in, h_in, w_mi, w_mo, w_fi, w_fo, w_f1, w_f2, w_b, w_am, w_ah, w_au,
-    i_ad, i_og, i_qkv, i_gl, i_st, i_mix, i_yh, i_rh, i_ao, i_mid, i_af, i_gu, i_dn,
-    e_out, gm_out, gh_out, gp_out,
+def backward_kernel(n_blocks, meta, d_in, *refs):
+    refs = list(refs)
+
+    def take(n):
+        out = refs[:n]
+        del refs[:n]
+        return out
+
+    n_w = len(NAMES)
+    inputs = take(2)
+    sources = take(n_w)
+    kept = [take(13), take(13)]
+    (e_out,) = take(1)
+    grad_outs = [take(3), take(3)]
+    d, h = take(2)
+    mi, mo, fi, fo, f1, f2, bias, am, ah, au = take(n_w)
+    ad, og, qkv, gl, st, mix, yh, rh, ao, mid, af, gu, dn = take(13)
+    (e,) = take(1)
+    grad_sums = [take(3), take(3)]
+    (gm, gh, gp, gps, rgm2, rgh2, rgp2, hidden, wide, gad, big, grad, dog, sendm, dmr, logit, fg, gstate, gt, dt, don,
+     hidden_gated, sendq, dqkv, dlog, sendl, dlr) = take(27)
+    dproj = wide.at[:, pl.ds(MODEL_WIDTH, FROZEN)]
+    lsem, ssem2, rsem2, gssem2, grsem2 = take(5)
+    me = lax.axis_index("seq")
+    loc = Local(lsem)
+    buffers = dict(zip(NAMES, (mi, mo, fi, fo, f1, f2, bias, am, ah, au)))
+    acts = dict(ad=ad, og=og, qkv=qkv, gl=gl, st=st, mix=mix, yh=yh, rh=rh, ao=ao, mid=mid, af=af, gu=gu, dn=dn)
+    on_the_way = [{}, {}]
+
+    def fetch(layer, *names):
+        for name in names:
+            if name == "d":
+                c = loc.start(d_in, d)
+            elif name == "h":
+                c = loc.start(inputs[layer], h)
+            elif name in buffers:
+                c = loc.start(sources[NAMES.index(name)].at[layer], buffers[name])
+            else:
+                c = loc.start(kept[layer][list(acts).index(name)], acts[name])
+            on_the_way[layer][name] = c
+
+    fetch(1, "d", "au", "dn", "ah", "fo", "gu")
+    greet_peers(me)
+    fetch(1, "fi", "am", "mid", "mo", "og", "mix", "f2", "b", "gl", "yh", "rh", "qkv", "st", "ao", "af", "mi", "f1", "ad", "h")
+    for layer in (1, 0):
+        def arrive(*names, layer=layer):
+            for name in names:
+                on_the_way[layer][name].wait()
+
+        backward_layer(
+            layer, n_blocks, meta, me, loc, arrive, fetch if layer == 1 else None,
+            d, h, mi, mo, fi, fo, f1, f2, bias, am, ah, au,
+            ad, og, qkv, gl, st, mix, yh, rh, ao, mid, af, gu, dn,
+            e, *grad_sums[layer], gm, gh, gp, gps, rgm2.at[layer], rgh2.at[layer], rgp2.at[layer],
+            hidden, wide, gad, big, grad, dog, sendm, dmr, logit, fg, gstate, gt, dt, don,
+            hidden_gated, sendq, dqkv, dlog, sendl, dlr, dproj,
+            ssem2.at[layer], rsem2.at[layer], gssem2.at[layer], grsem2.at[layer],
+        )
+        for x, y in zip(grad_sums[layer], grad_outs[layer]):
+            loc.start(x, y, True)
+    loc.start(e, e_out, True)
+    loc.finish()
+
+
+def backward_layer(
+    layer, n_blocks, meta, me, loc, arrive, fetch,
     d, h, mi, mo, fi, fo, f1, f2, bias, am, ah, au,
     ad, og, qkv, gl, st, mix, yh, rh, ao, mid, af, gu, dn,
-    e, sgm, sgh, sgp,
-    gm, gh, gp, gps, rgm, rgh, rgp, hidden, wide, gad, big, grad, dog, sendm, dmr, logit, fg, gstate, gt, dt, don, hidden_gated, sendq, dqkv, dlog, sendl, dlr, dproj,
-    lsem, ssem, rsem, gssem, grsem,
+    e, sgm, sgh, sgp, gm, gh, gp, gps, rgm, rgh, rgp,
+    hidden, wide, gad, big, grad, dog, sendm, dmr, logit, fg, gstate, gt, dt, don,
+    hidden_gated, sendq, dqkv, dlog, sendl, dlr, dproj,
+    ssem, rsem, gssem, grsem,
 ):
-    me = lax.axis_index("seq")
+    prefetch = (lambda *names: fetch(0, *names)) if fetch else (lambda *names: None)
     T = h.shape[0]
     per = T // GROUP
     adapter = meta[2 * n_blocks]
     length = meta[2 * n_blocks + 1]
-    loc = Local(lsem)
-    l_d = loc.start(d_in, d)
-    l_au = loc.start(w_au.at[layer], au)
-    l_ah = loc.start(w_ah.at[layer], ah)
-    l_fo = loc.start(w_fo.at[layer], fo)
-    l_gu = loc.start(i_gu, gu)
-    l_dn = loc.start(i_dn, dn)
-    greet_peers(me)
-    l_fi = loc.start(w_fi.at[layer], fi)
-    l_am = loc.start(w_am.at[layer], am)
-    l_mid = loc.start(i_mid, mid)
-    l_af = loc.start(i_af, af)
-    l_mo = loc.start(w_mo.at[layer], mo)
-    l_og = loc.start(i_og, og)
-    l_mix = loc.start(i_mix, mix)
-    l_ao = loc.start(i_ao, ao)
-    l_mixer = [
-        loc.start(a, b)
-        for a, b in (
-            (w_f2.at[layer], f2), (w_b.at[layer], bias), (i_qkv, qkv), (i_gl, gl), (i_st, st), (i_yh, yh), (i_rh, rh),
-        )
-    ]
-    l_last = [
-        loc.start(a, b) for a, b in ((w_mi.at[layer], mi), (w_f1.at[layer], f1), (i_ad, ad), (h_in, h))
-    ]
     mask = column_mask(adapter)
     pick = picked(adapter, ADAPTER_COLUMNS)
 
@@ -472,17 +510,13 @@
                 copies.append(to_peer(a, b, gssem.at[j, k], grsem.at[j, k], peer))
         return copies
 
-    l_d.wait()
-    l_au.wait()
+    arrive("au", "dn") if layer == 0 else arrive("d", "au", "dn")
     gdown = (nt(d[...], au[:, U_D : U_D + MODEL_WIDTH]).astype(BF).astype(F32) * mask).astype(BF)
     gdown16 = narrow(gdown)
     gh[:, VALUE_WIDTH + HIDDEN_UNITS :] = jnp.zeros((ADAPTER_RANK, gh.shape[1] - VALUE_WIDTH - HIDDEN_UNITS), BF)
-    l_dn.wait()
     gp[:, U_D : U_D + MODEL_WIDTH] = outer(dn[...], d[...])
     gad[...] = gdown
-    l_ah.wait()
-    l_fo.wait()
-    l_gu.wait()
+    arrive("ah", "fo", "gu")
 
     def down_tile(i, carry):
         a, b = lanes(i * TILE, TILE), lanes(HIDDEN_UNITS + i * TILE, TILE)
@@ -496,13 +530,13 @@
         return carry
 
     lax.fori_loop(0, HIDDEN_UNITS // TILE, down_tile, 0)
+    prefetch("dn", "fo", "gu")
     gate_cols, up_cols = slice(0, HIDDEN_UNITS), slice(HIDDEN_UNITS, 2 * HIDDEN_UNITS)
     gg = (nt(wide[:, gate_cols], au[:, U_G : U_G + HIDDEN_UNITS]).astype(BF).astype(F32) * mask).astype(BF)
     gu2 = (nt(wide[:, up_cols], au[:, U_U : U_U + HIDDEN_UNITS]).astype(BF).astype(F32) * mask).astype(BF)
     gad2 = jnp.concatenate([gg, gu2], axis=1)
     big[:, 0 : 2 * ADAPTER_COLUMNS] = gad2
-    l_fi.wait()
-    l_am.wait()
+    arrive("fi", "am")
 
     def wide_tile(i, carry):
         at = pl.ds(pl.multiple_of(i * TILE, TILE), TILE)
@@ -512,7 +546,8 @@
         return carry
 
     lax.fori_loop(0, MODEL_WIDTH // TILE, wide_tile, 0)
-    l_mid.wait()
+    prefetch("fi")
+    arrive("mid")
     mv = mid[...]
     grad_mid = d[...].astype(F32) + rms_back(mv, grad[...])
     grad[...] = grad_mid
@@ -520,9 +555,7 @@
     e[...] = attn
     gout = (nt(attn, au[:, U_O : U_O + MODEL_WIDTH]).astype(BF).astype(F32) * mask).astype(BF)
     gad[...] = gout
-    l_mo.wait()
-    l_og.wait()
-    l_mix.wait()
+    arrive("mo", "og", "mix")
 
     def gate_back(head, out):
         at = rows(head * DV, DV)
@@ -544,23 +577,8 @@
         mix_copies.append(copy)
     gate_back(me, dmr.at[rows(me * T, T)])
 
-    l_af.wait()
-    l_ao.wait()
-    normed_mid = (mv * inverse_rms(mv)).astype(BF)
-    gh[:, VALUE_WIDTH : VALUE_WIDTH + HIDDEN_UNITS] = tn(gdown16, hidden[...]).astype(BF)
-    gm[4 * ADAPTER_RANK : 5 * ADAPTER_RANK, :] = outer(gg, normed_mid)
-    gm[5 * ADAPTER_RANK : 6 * ADAPTER_RANK, :] = outer(gu2, normed_mid)
-    gp[:, U_G : U_G + HIDDEN_UNITS] = outer(af[:, 0:ADAPTER_COLUMNS], wide[:, gate_cols])
-    gp[:, U_U : U_U + HIDDEN_UNITS] = outer(af[:, ADAPTER_COLUMNS:], wide[:, up_cols])
-    gp[:, U_O : U_O + MODEL_WIDTH] = outer(ao[...], e[...])
-    gh[:, 0:VALUE_WIDTH] = outer(gad[...], hidden_gated[...])
-    place(range(n_late, n_dp))
-    grads = grad_copies(False)
-    for c in grads:
-        c.start()
-
-    for c in l_mixer:
-        c.wait()
+    prefetch("mo", "ah", "og", "mix")
+    arrive("f2", "b", "gl", "yh", "rh", "qkv", "st")
     f2h = f2[:, lanes(me * DK, DK)]
     bh = bias[:, lanes(me * DK, DK)]
     for src in range(HEADS):
@@ -648,8 +666,23 @@
         q_copies += copies
     back_rows(me, dqkv.at[me], dlr.at[me])
 
-    for c in l_last:
-        c.wait()
+    arrive("af", "ao")
+    mv = mid[...]
+    normed_mid = (mv * inverse_rms(mv)).astype(BF)
+    gh[:, VALUE_WIDTH : VALUE_WIDTH + HIDDEN_UNITS] = tn(gdown16, hidden[...]).astype(BF)
+    gm[4 * ADAPTER_RANK : 5 * ADAPTER_RANK, :] = outer(big[:, 0:ADAPTER_COLUMNS], normed_mid)
+    gm[5 * ADAPTER_RANK : 6 * ADAPTER_RANK, :] = outer(big[:, ADAPTER_COLUMNS : 2 * ADAPTER_COLUMNS], normed_mid)
+    gp[:, U_G : U_G + HIDDEN_UNITS] = outer(af[:, 0:ADAPTER_COLUMNS], wide[:, gate_cols])
+    gp[:, U_U : U_U + HIDDEN_UNITS] = outer(af[:, ADAPTER_COLUMNS:], wide[:, up_cols])
+    gp[:, U_O : U_O + MODEL_WIDTH] = outer(ao[...], e[...])
+    gh[:, 0:VALUE_WIDTH] = outer(gad[...], hidden_gated[...])
+    place(range(n_late, n_dp))
+    grads = grad_copies(False)
+    for c in grads:
+        c.start()
+    prefetch("mid", "af", "ao", "qkv", "gl", "st", "yh", "rh", "f2", "b")
+
+    arrive("mi", "f1", "ad", "h")
     hv = h[...].astype(F32)
     hr = inverse_rms(hv)
     big[...] = (hv * hr).astype(BF)
@@ -687,7 +720,9 @@
     dn_ = jnp.concatenate(back, axis=1)
     n = hv * hr
     e[...] = (grad[...] + hr * (dn_ - n * jnp.mean(dn_ * n, axis=-1, keepdims=True))).astype(BF)
-    loc.start(e, e_out, True)
+    if layer == 1:
+        d[...] = e[...]
+    prefetch("au", "am", "mi", "f1", "ad", "h")
     grads += late_grads
     for c in grads:
         c.wait_recv()
@@ -706,15 +741,12 @@
         for k in range(HEADS - 1):
             total += rgp[k, i].astype(F32)
         sgp[i] = jnp.where(spot == width, adapter.astype(F32), total).astype(BF)
-    for a, b in ((sgm, gm_out), (sgh, gh_out), (sgp, gp_out)):
-        loc.start(a, b, True)
-    loc.finish()
     for c in mix_copies + q_copies + grads:
         c.wait_send()
 
 
-def backward(layer, meta, d, h, weights, saved, n_dp):
-    T = h.shape[0]
+def backward(meta, d, x, h1, weights, early, late, n_dp):
+    T = x.shape[0]
     L = T * HEADS
     n_blocks = L // GROUP
     raised = U_D + MODEL_WIDTH
@@ -730,22 +762,22 @@
     vm = pltpu.VMEM
     dma = pltpu.SemaphoreType.DMA
     return pl.pallas_call(
-        functools.partial(backward_kernel, layer, n_blocks),
-        out_shape=[jax.ShapeDtypeStruct(*s) for s in outs],
-        in_specs=[pl.BlockSpec(memory_space=pltpu.SMEM)] + [ANY] * (2 + len(weights) + len(saved)),
-        out_specs=[ANY] * len(outs),
-        scratch_shapes=[vm(d.shape, d.dtype), vm(h.shape, h.dtype)]
+        functools.partial(backward_kernel, n_blocks),
+        out_shape=[jax.ShapeDtypeStruct(*s) for s in outs[:1] + 2 * outs[1:]],
+        in_specs=[pl.BlockSpec(memory_space=pltpu.SMEM)] + [ANY] * (3 + len(weights) + 2 * len(early)),
+        out_specs=[ANY] * (2 * len(outs) - 1),
+        scratch_shapes=[vm(d.shape, d.dtype), vm(x.shape, x.dtype)]
         + weight_scratch(weights)
-        + [vm(s.shape, s.dtype) for s in saved]
-        + [vm(*s) for s in outs]
+        + [vm(s.shape, s.dtype) for s in early]
+        + [vm(*s) for s in outs[:1] + 2 * outs[1:]]
         + [
             vm((6 * ADAPTER_RANK, MODEL_WIDTH), BF),
             vm((ADAPTER_RANK, HEADS * hidden_quarter), BF),
             vm((ADAPTER_RANK, raised), BF),
             vm((HEADS, n_dp, ADAPTER_RANK, padded), BF),
-            vm((HEADS - 1, 6 * ADAPTER_RANK, quarter), BF),
-            vm((HEADS - 1, ADAPTER_RANK, hidden_quarter), BF),
-            vm((HEADS - 1, n_dp, ADAPTER_RANK, padded), BF),
+            vm((2, HEADS - 1, 6 * ADAPTER_RANK, quarter), BF),
+            vm((2, HEADS - 1, ADAPTER_RANK, hidden_quarter), BF),
+            vm((2, HEADS - 1, n_dp, ADAPTER_RANK, padded), BF),
             vm((T, HIDDEN_UNITS), BF),
             vm((T, 2 * HIDDEN_UNITS), BF),
             vm((T, ADAPTER_COLUMNS), BF),
@@ -766,18 +798,17 @@
             vm((T, DK), BF),
             vm((HEADS - 1, FGATE_RANK, T), BF),
             vm((HEADS, FGATE_RANK, T), BF),
-            vm((T, FROZEN), BF),
-            dma((2 + len(weights) + len(saved) + len(outs),)),
-            dma((3, HEADS)),
-            dma((3, HEADS)),
-            dma((5, HEADS)),
-            dma((5, HEADS)),
+            dma((2 * (2 + len(weights) + len(early) + len(outs)),)),
+            dma((2, 3, HEADS)),
+            dma((2, 3, HEADS)),
+            dma((2, 5, HEADS)),
+            dma((2, 5, HEADS)),
         ],
         compiler_params=pltpu.CompilerParams(
-            collective_id=3 + layer, has_side_effects=True, vmem_limit_bytes=VMEM_LIMIT
+            collective_id=3, has_side_effects=True, vmem_limit_bytes=VMEM_LIMIT
         ),
-        cost_estimate=pl.CostEstimate(flops=2 * T * 16_000_000, bytes_accessed=45 << 20, transcendentals=T * 8192),
-    )(meta, d, h, *weights, *saved)
+        cost_estimate=pl.CostEstimate(flops=4 * T * 16_000_000, bytes_accessed=90 << 20, transcendentals=T * 16384),
+    )(meta, d, x, h1, *weights, *early, *late)
 
 
 UNITS = [(layer, w) for layer in range(2) for w in range(4)]
@@ -921,7 +952,8 @@
             @pl.when(can_send(d, 1))
             def _():
                 z_copy(u, d, 1).start()
-                t_copy(u, d, 1).start()
+                if STRIPS[w]:
+                    t_copy(u, d, 1).start()
 
     def take_z(u, t):
         for d in range(2):
@@ -936,8 +968,9 @@
             def _():
                 x_copy(u, d, t).start()
                 y_copy(u, d, t).start()
-                t_copy(u, d, t).wait_recv()
-            if t < n_z - 1:
+                if STRIPS[UNITS[u][1]]:
+                    t_copy(u, d, t).wait_recv()
+            if t < n_z - 1 and STRIPS[UNITS[u][1]]:
                 @pl.when(can_send(d, t + 1))
                 def _():
                     t_copy(u, d, t + 1).start()
@@ -1104,7 +1137,8 @@
                 @pl.when(can_send(d, t))
                 def _():
                     z_copy(u, d, t).wait_send()
-                    t_copy(u, d, t).wait_send()
+                    if STRIPS[UNITS[u][1]]:
+                        t_copy(u, d, t).wait_send()
                 @pl.when(gets(d, t))
                 def _():
                     x_copy(u, d, t).wait_send()
@@ -1369,8 +1403,8 @@
         weights, x, cotangent = list(out[:5]) + list(out[7:]), out[5], out[6]
         early = forward(0, meta, x, weights)
         late = forward(1, meta, early[0], weights)
-    middle, *grads_late = backward(1, meta, cotangent, early[0], weights, late[1:], n_dp)
-    entry, *grads_early = backward(0, meta, middle, x, weights, early[1:], n_dp)
+    entry, *grads = backward(meta, cotangent, x, early[0], weights, early[1:], late[1:], n_dp)
+    grads_early, grads_late = grads[:3], grads[3:]
     sent = swap_sections(jnp.where(first, late[0], entry))
     results = jnp.where(first, jnp.stack([entry, sent]), jnp.stack([sent, late[0]]))
     reduce = reduce_gradients if own_kernels else plain_reduce

time: 383 us -> 380 us (level)
  Pallas kernels: 364 us -> 359 us
    pallas_call x1, Pallas kernels: 240 us -> 233 us  [forward_model(): pl.pallas_call(functools.partial(model_kernel, n_blocks), out_shape=outs,...]
    pallas_call x2 -> x1, Pallas kernels: 101 us -> 101 us  [backward(): pl.pallas_call(functools.partial(backward_kernel, n_blocks), out_shape=[j...]
where the time goes in v5:
time: 380 us; the launch traced here: 375 us
  Pallas kernels  359 us (94%)
  local copies, waits for them, and re-layouts  9.75 us (3%)
    pallas_call x1, Pallas kernels, forward_model(): pl.pallas_call(functools.partial(model_kernel, n_blocks), out_shape=outs,...  233 us
    pallas_call x1, Pallas kernels, backward(): pl.pallas_call(functools.partial(backward_kernel, n_blocks), out_shape=[j...  101 us
    pallas_call x1, Pallas kernels, reduce_gradients(): pl.pallas_call(reduce_kernel, out_shape=[shape((own_m, MODEL_WIDTH), F32)...  23.8 us
  transfers between devices with their start and end apart: 1, of which 0 were waited for; matrix products, arithmetic and copies ran while one was open for 0% of the time, Pallas kernels for 6%

profile of v5, /device:TPU:0, one launch (start us, length us, event | category | flops | bytes accessed | tf_op | source)
XLA Modules:
  0.0 374.7 jit_solution(18177246538368081985)
XLA Ops:
  0.6 0.7 fusion
  1.3 0.1 select_reduce_fusion
  1.4 1.3 fusion.2
  2.7 1.3 fusion.1
  6.6 0.6 pad_add_fusion.meta
  7.2 233.4 %shard_map.165 = (bf16[2,1024,3072]{2,1,0:T(8,128)(2,1)}, bf16[2,1024,1024]{2,1,0:T(8,128)(2,1)}, bf16[2,1024,5632]{2,1,0:T(8,128)(2,1)}, bf16[2,2816,1024]{2,1,...) custom-call(s32[34]{0:T(128)} %pad_add_fusion.meta, ...), custom_call_target="tpu_custom_call" | custom-call | tf_op jit(solution)/shard_map/pallas_call | solution.py:1164
  240.6 0.0 copy-start.6
  240.6 101.4 %shard_map.166 = (bf16[256,1024]{1,0:T(8,128)(2,1)}, bf16[96,256]{1,0:T(8,128)(2,1)}, bf16[16,1024]{1,0:T(8,128)(2,1)}, bf16[4,16,768]{2,1,0:T(8,128)(2,1)}, bf1...) custom-call(s32[34]{0:T(128)} %pad_add_fusion.meta, ...), custom_call_target="tpu_custom_call" | custom-call | flops 16384000000 | bytes 94371840 | tf_op jit(solution)/shard_map/pallas_call | solution.py:764
  342.0 0.0 copy-start.7
  342.0 0.0 copy-done.6
  342.0 0.1 broadcast_select_fusion
  342.1 0.1 collective-permute-start
  342.2 0.0 copy-start
  342.2 0.9 copy-done
  343.1 0.0 copy-start.1
  343.1 0.9 copy-done.1
  343.9 0.0 copy-start.2
  343.9 0.8 copy-done.2
  344.7 0.0 copy-start.3
  344.7 0.8 copy-done.3
  345.5 0.0 copy-start.4
  345.5 0.8 copy-done.4
  346.3 0.0 copy-start.5
  346.3 0.8 copy-done.5
  347.1 23.8 %shard_map.167 = (f32[48,1024]{1,0:T(8,128)S(1)}, f32[8,4096]{1,0:T(8,128)S(1)}, f32[128,672]{1,0:T(8,128)S(1)}) custom-call(bf16[96,256]{1,0:T(8,128)(2,1)S(1)} %copy-done.2, bf16[16,1024]{1,0:T(8,128)(2,1)S(1)} %copy-done.4, bf16[4,16,768]{2,1,0:T(8,128)(2,1)S(1)} %copy-done, bf16[96,256]{1,0:T(8,128)(2,1)S(1)} %copy-done.3, ...), custom_call_target="tpu_custom_call" | custom-call | tf_op jit(solution)/shard_map/pallas_call | solution.py:1310
  370.9 0.9 copy.19
  371.8 0.7 slice_bitcast_fusion
  372.4 0.0 collective-permute-done
  372.4 0.0 copy-done.7
  372.4 1.1 maximum_select_fusion
  373.6 0.7 copy.21
Async XLA Ops:
  240.6 101.4 %copy-start.6 = (bf16[256,1024]{1,0:T(8,128)(2,1)S(1)}, bf16[256,1024]{1,0:T(8,128)(2,1)}, u32[]{:S(2)}) copy-start(bf16[256,1024]{1,0:T(8,128)(2,1)} %get-tuple-element.94) | copy-start | bytes 1572868
  342.0 30.4 %copy-start.7 = (bf16[256,1024]{1,0:T(8,128)(2,1)S(1)}, bf16[256,1024]{1,0:T(8,128)(2,1)}, u32[]{:S(2)}) copy-start(bf16[256,1024]{1,0:T(8,128)(2,1)} %get-tuple-element.93) | copy-start | bytes 1572868
  342.1 30.4 %collective-permute-start = (bf16[256,1024]{1,0:T(8,128)(2,1)S(1)}, bf16[256,1024]{1,0:T(8,128)(2,1)S(1)}, u32[]{:S(2)}, u32[]{:S(2)}) collective-permute-start(bf16[256,1024]{1,0:T(8,128)(2,1)S(1)} %broadcast_select_fusion), channel_id=1, source_target_pairs={{0,16},{16,0},{1,17},{17,1},{2,18},{18,2},{3,19},{19,3},{4,20},{20... | collective-permute-start | bytes 1572872 | tf_op jit(solution)/shard_map/ppermute | solution.py:1185
  342.2 0.9 copy-start
  343.1 0.9 copy-start.1
  343.9 0.8 copy-start.2
  344.7 0.8 copy-start.3
  345.5 0.8 copy-start.4
  346.3 0.8 copy-start.5

commit v6 on v5

--- a/solution.py
+++ b/solution.py
@@ -196,7 +196,7 @@
         ref[:, 2 * DK : CHUNK] = project(2 * KEY + head * DV, 2, DV).astype(BF)
 
     qkv_copies = []
-    for d in range(1, HEADS):
+    for d in (3, 1, 2):
         yield None, 1
         chunk(me ^ d, send.at[d - 1])
         copy = to_peer(send.at[d - 1], qkv.at[rows(me * T, T)], ssem.at[1, d], rsem.at[1, d], me ^ d)
@@ -228,7 +228,7 @@
         state[...] = jnp.exp(total) * now + update
         return carry
 
-    lax.fori_loop(0, n_blocks, advance, 0, unroll=4)
+    lax.fori_loop(0, n_blocks, advance, 0, unroll=8)
     loc.start(st, o_st, True)
     yield None, 4
 
@@ -248,7 +248,7 @@
         rh[at, :] = jnp.broadcast_to(r, (GROUP, DK))
 
     mix_copies = []
-    for d in range(1, HEADS):
+    for d in (3, 1, 2):
         yield None, 2
         peer = me ^ d
         lax.fori_loop(0, per, lambda j, c, peer=peer: (mix_block(peer * per + j), c)[1], 0, unroll=True)
@@ -439,13 +439,14 @@
     fetch(1, "d", "au", "dn", "ah", "fo", "gu")
     greet_peers(me)
     fetch(1, "fi", "am", "mid", "mo", "og", "mix", "f2", "b", "gl", "yh", "rh", "qkv", "st", "ao", "af", "mi", "f1", "ad", "h")
+    finish = None
     for layer in (1, 0):
         def arrive(*names, layer=layer):
             for name in names:
                 on_the_way[layer][name].wait()
 
-        backward_layer(
-            layer, n_blocks, meta, me, loc, arrive, fetch if layer == 1 else None,
+        finish = backward_layer(
+            layer, n_blocks, meta, me, loc, arrive, fetch if layer == 1 else None, finish, grad_outs[layer],
             d, h, mi, mo, fi, fo, f1, f2, bias, am, ah, au,
             ad, og, qkv, gl, st, mix, yh, rh, ao, mid, af, gu, dn,
             e, *grad_sums[layer], gm, gh, gp, gps, rgm2.at[layer], rgh2.at[layer], rgp2.at[layer],
@@ -453,14 +454,13 @@
             hidden_gated, sendq, dqkv, dlog, sendl, dlr, dproj,
             ssem2.at[layer], rsem2.at[layer], gssem2.at[layer], grsem2.at[layer],
         )
-        for x, y in zip(grad_sums[layer], grad_outs[layer]):
-            loc.start(x, y, True)
     loc.start(e, e_out, True)
+    finish()
     loc.finish()
 
 
 def backward_layer(
-    layer, n_blocks, meta, me, loc, arrive, fetch,
+    layer, n_blocks, meta, me, loc, arrive, fetch, window, grad_outs,
     d, h, mi, mo, fi, fo, f1, f2, bias, am, ah, au,
     ad, og, qkv, gl, st, mix, yh, rh, ao, mid, af, gu, dn,
     e, sgm, sgh, sgp, gm, gh, gp, gps, rgm, rgh, rgp,
@@ -513,7 +513,8 @@
     arrive("au", "dn") if layer == 0 else arrive("d", "au", "dn")
     gdown = (nt(d[...], au[:, U_D : U_D + MODEL_WIDTH]).astype(BF).astype(F32) * mask).astype(BF)
     gdown16 = narrow(gdown)
-    gh[:, VALUE_WIDTH + HIDDEN_UNITS :] = jnp.zeros((ADAPTER_RANK, gh.shape[1] - VALUE_WIDTH - HIDDEN_UNITS), BF)
+    if layer == 1:
+        gh[:, VALUE_WIDTH + HIDDEN_UNITS :] = jnp.zeros((ADAPTER_RANK, gh.shape[1] - VALUE_WIDTH - HIDDEN_UNITS), BF)
     gp[:, U_D : U_D + MODEL_WIDTH] = outer(dn[...], d[...])
     gad[...] = gdown
     arrive("ah", "fo", "gu")
@@ -569,7 +570,7 @@
         hidden_gated[:, cols] = (m * act).astype(BF)
 
     mix_copies = []
-    for k in range(1, HEADS):
+    for k in (3, 1, 2):
         peer = me ^ k
         gate_back(peer, sendm.at[k - 1])
         copy = to_peer(sendm.at[k - 1], dmr.at[rows(me * T, T)], ssem.at[0, k], rsem.at[0, k], peer)
@@ -578,6 +579,15 @@
     gate_back(me, dmr.at[rows(me * T, T)])
 
     prefetch("mo", "ah", "og", "mix")
+    if window:
+        window()
+    arrive("af")
+    mv = mid[...]
+    normed_mid = (mv * inverse_rms(mv)).astype(BF)
+    gm[4 * ADAPTER_RANK : 5 * ADAPTER_RANK, :] = outer(big[:, 0:ADAPTER_COLUMNS], normed_mid)
+    gm[5 * ADAPTER_RANK : 6 * ADAPTER_RANK, :] = outer(big[:, ADAPTER_COLUMNS : 2 * ADAPTER_COLUMNS], normed_mid)
+    gp[:, U_G : U_G + HIDDEN_UNITS] = outer(af[:, 0:ADAPTER_COLUMNS], wide[:, gate_cols])
+    gp[:, U_U : U_U + HIDDEN_UNITS] = outer(af[:, ADAPTER_COLUMNS:], wide[:, up_cols])
     arrive("f2", "b", "gl", "yh", "rh", "qkv", "st")
     f2h = f2[:, lanes(me * DK, DK)]
     bh = bias[:, lanes(me * DK, DK)]
@@ -610,7 +620,7 @@
         gstate[...] = decayed + tn(do, qs)
         return carry
 
-    lax.fori_loop(0, n_blocks, retreat, 0, unroll=4)
+    lax.fori_loop(0, n_blocks, retreat, 0, unroll=8)
 
     def back_block(p, out, j):
         n = meta[p]
@@ -651,10 +661,10 @@
     q_copies = []
 
     def back_rows(dest, out, low_out):
-        lax.fori_loop(0, per, lambda j, c: (back_block(dest * per + j, out, j), c)[1], 0, unroll=2)
+        lax.fori_loop(0, per, lambda j, c: (back_block(dest * per + j, out, j), c)[1], 0, unroll=True)
         low_out[...] = nt(f2h, dlog[...]).astype(BF)
 
-    for k in range(1, HEADS):
+    for k in (3, 1, 2):
         peer = me ^ k
         back_rows(peer, sendq.at[k - 1], sendl.at[k - 1])
         copies = (
@@ -666,14 +676,8 @@
         q_copies += copies
     back_rows(me, dqkv.at[me], dlr.at[me])
 
-    arrive("af", "ao")
-    mv = mid[...]
-    normed_mid = (mv * inverse_rms(mv)).astype(BF)
+    arrive("ao")
     gh[:, VALUE_WIDTH : VALUE_WIDTH + HIDDEN_UNITS] = tn(gdown16, hidden[...]).astype(BF)
-    gm[4 * ADAPTER_RANK : 5 * ADAPTER_RANK, :] = outer(big[:, 0:ADAPTER_COLUMNS], normed_mid)
-    gm[5 * ADAPTER_RANK : 6 * ADAPTER_RANK, :] = outer(big[:, ADAPTER_COLUMNS : 2 * ADAPTER_COLUMNS], normed_mid)
-    gp[:, U_G : U_G + HIDDEN_UNITS] = outer(af[:, 0:ADAPTER_COLUMNS], wide[:, gate_cols])
-    gp[:, U_U : U_U + HIDDEN_UNITS] = outer(af[:, ADAPTER_COLUMNS:], wide[:, up_cols])
     gp[:, U_O : U_O + MODEL_WIDTH] = outer(ao[...], e[...])
     gh[:, 0:VALUE_WIDTH] = outer(gad[...], hidden_gated[...])
     place(range(n_late, n_dp))
@@ -724,25 +728,33 @@
         d[...] = e[...]
     prefetch("au", "am", "mi", "f1", "ad", "h")
     grads += late_grads
-    for c in grads:
-        c.wait_recv()
-
-    def summed_over_seq(own, got):
-        total = own.astype(F32)
-        for k in range(HEADS - 1):
-            total += got[k].astype(F32)
-        return total.astype(BF)
-
-    sgm[...] = summed_over_seq(gm[:, lanes(me * quarter, quarter)], rgm)
-    sgh[...] = summed_over_seq(gh[:, lanes(me * hidden_quarter, hidden_quarter)], rgh)
-    spot = lax.broadcasted_iota(jnp.int32, (ADAPTER_RANK, padded), 1)
-    for i in range(n_dp):
-        total = gps[me, i].astype(F32)
-        for k in range(HEADS - 1):
-            total += rgp[k, i].astype(F32)
-        sgp[i] = jnp.where(spot == width, adapter.astype(F32), total).astype(BF)
-    for c in mix_copies + q_copies + grads:
+    for c in mix_copies + q_copies:
         c.wait_send()
+
+    def finish():
+        for c in grads:
+            c.wait_recv()
+
+        def summed_over_seq(own, got):
+            total = own.astype(F32)
+            for k in range(HEADS - 1):
+                total += got[k].astype(F32)
+            return total.astype(BF)
+
+        sgm[...] = summed_over_seq(gm[:, lanes(me * quarter, quarter)], rgm)
+        sgh[...] = summed_over_seq(gh[:, lanes(me * hidden_quarter, hidden_quarter)], rgh)
+        spot = lax.broadcasted_iota(jnp.int32, (ADAPTER_RANK, padded), 1)
+        for i in range(n_dp):
+            total = gps[me, i].astype(F32)
+            for k in range(HEADS - 1):
+                total += rgp[k, i].astype(F32)
+            sgp[i] = jnp.where(spot == width, adapter.astype(F32), total).astype(BF)
+        for c in grads:
+            c.wait_send()
+        for a, b in zip((sgm, sgh, sgp), grad_outs):
+            loc.start(a, b, True)
+
+    return finish
 
 
 def backward(meta, d, x, h1, weights, early, late, n_dp):
@@ -1203,8 +1215,8 @@
 
 
 def reduce_kernel(
-    gm0, gh0, gp0, gm1, gh1, gp1, m_out, h_out, u_out,
-    vm_, vh, vp, rm, rh, rp, am, ah, em, eh, ls, ss, rs, es, er,
+    gm0, gh0, gp0, gm1, gh1, gp1, entry, last_y, m_out, h_out, u_out, ends_out,
+    vm_, vh, vp, rm, rh, rp, am, ah, em, eh, ends, ls, ss, rs, es, er, xl, xo, xs, xr,
 ):
     core, dp, me = lax.axis_index("section"), lax.axis_index("dp"), lax.axis_index("seq")
     n_dp = vp.shape[1]
@@ -1215,6 +1227,9 @@
         for i, (a, b) in enumerate(zip(three, (vm_, vh, vp)))
     ]
     for c in loads:
+        c.start()
+    ends_in = [pltpu.make_async_copy(a, ends.at[i], xl.at[i]) for i, a in enumerate((entry, last_y))]
+    for c in ends_in:
         c.start()
     barrier = pltpu.get_barrier_semaphore()
     places = [dict(section=1 - core)] + [dict(seq=me ^ k) for k in range(1, HEADS)]
@@ -1250,6 +1265,15 @@
                 )
                 c.start()
                 copies.append(c)
+    for c in ends_in:
+        c.wait()
+    ends_own = pltpu.make_async_copy(ends.at[core], ends_out.at[core], xo)
+    ends_cross = pltpu.make_async_remote_copy(
+        src_ref=ends.at[1 - core], dst_ref=ends_out.at[core], send_sem=xs, recv_sem=xr,
+        device_id=dict(section=1 - core), device_id_type=MESH,
+    )
+    ends_own.start()
+    ends_cross.start()
     at = pl.ds(pl.multiple_of(first_projection(dp) * ADAPTER_RANK, ADAPTER_RANK), 2 * ADAPTER_RANK)
     rm[slot] = vm_[core, at]
     rh[slot] = vh[core]
@@ -1298,24 +1322,27 @@
         h_out[:, q * eh.shape[2] : (q + 1) * eh.shape[2]] = eh[q]
     for c in copies + last:
         c.wait_send()
-
-
-def reduce_gradients(early, late, n_dp):
+    ends_own.wait()
+    ends_cross.wait()
+
+
+def reduce_gradients(early, late, entry, y, n_dp):
     gm, gh, gp = early
     n = 2 * n_dp
     width = (U_D + MODEL_WIDTH) // (n_dp * HEADS)
     own_m, own_h = 6 * ADAPTER_COLUMNS // (n_dp * HEADS), ADAPTER_COLUMNS // (n_dp * HEADS)
     vm, dma, VM = pltpu.VMEM, pltpu.SemaphoreType.DMA, pl.BlockSpec(memory_space=pltpu.VMEM)
     shape = jax.ShapeDtypeStruct
-    model, hidden, up = pl.pallas_call(
+    model, hidden, up, ends = pl.pallas_call(
         reduce_kernel,
         out_shape=[
             shape((own_m, MODEL_WIDTH), F32),
             shape((own_h, HEADS * gh.shape[1]), F32),
             shape((ADAPTER_COLUMNS, width), F32),
+            shape((2,) + y.shape, y.dtype),
         ],
-        in_specs=[ANY] * 6,
-        out_specs=[VM] * 3,
+        in_specs=[ANY] * 8,
+        out_specs=[VM] * 3 + [ANY],
         scratch_shapes=[
             vm((2,) + gm.shape, BF),
             vm((2,) + gh.shape, BF),
@@ -1327,15 +1354,20 @@
             vm((ADAPTER_COLUMNS, gh.shape[1]), F32),
             vm((HEADS, own_m, gm.shape[1]), F32),
             vm((HEADS, own_h, gh.shape[1]), F32),
+            vm((2,) + y.shape, y.dtype),
             dma((2, 3)),
             dma((2, n_dp, 3)),
             dma((2, n_dp, 3)),
             dma((2, HEADS)),
             dma((2, HEADS)),
+            dma((2,)),
+            dma,
+            dma,
+            dma,
         ],
-        compiler_params=pltpu.CompilerParams(collective_id=5, has_side_effects=True, vmem_limit_bytes=32 << 20),
-    )(*early, *late)
-    return model.T, hidden[:, : VALUE_WIDTH + HIDDEN_UNITS].T, up
+        compiler_params=pltpu.CompilerParams(collective_id=5, has_side_effects=True, vmem_limit_bytes=VMEM_LIMIT),
+    )(*early, *late, entry, y)
+    return model.T, hidden[:, : VALUE_WIDTH + HIDDEN_UNITS].T, up, ends
 
 
 def plain_reduce(early, late, n_dp):
@@ -1405,10 +1437,12 @@
         late = forward(1, meta, early[0], weights)
     entry, *grads = backward(meta, cotangent, x, early[0], weights, early[1:], late[1:], n_dp)
     grads_early, grads_late = grads[:3], grads[3:]
-    sent = swap_sections(jnp.where(first, late[0], entry))
-    results = jnp.where(first, jnp.stack([entry, sent]), jnp.stack([sent, late[0]]))
-    reduce = reduce_gradients if own_kernels else plain_reduce
-    model, hidden, up = reduce(grads_early, grads_late, n_dp)
+    if own_kernels:
+        model, hidden, up, results = reduce_gradients(grads_early, grads_late, entry, late[0], n_dp)
+    else:
+        sent = swap_sections(jnp.where(first, late[0], entry))
+        results = jnp.where(first, jnp.stack([entry, sent]), jnp.stack([sent, late[0]]))
+        model, hidden, up = plain_reduce(grads_early, grads_late, n_dp)
     return (results[None, :, None], model[None], hidden[None], up[None])
 
 

time: 380 us -> 375 us (0.987)
    pallas_call x1, Pallas kernels: 101 us -> 96.5 us  [backward(): pl.pallas_call(functools.partial(backward_kernel, n_blocks), out_shape=[j...]
  transfers between devices with their start and end apart: 1 -> 0, of which waited for: 0 -> 0; matrix products, arithmetic and copies ran while one was open for 0% -> 0% of each run, Pallas kernels for 6% -> 0%
where the time goes in v6:
time: 375 us; the launch traced here: 370 us
  Pallas kernels  356 us (95%)
  local copies, waits for them, and re-layouts  9.06 us (2%)
    pallas_call x1, Pallas kernels, forward_model(): pl.pallas_call(functools.partial(model_kernel, n_blocks), out_shape=outs,...  234 us
    pallas_call x1, Pallas kernels, backward(): pl.pallas_call(functools.partial(backward_kernel, n_blocks), out_shape=[j...  96.5 us
    pallas_call x1, Pallas kernels, reduce_gradients(): pl.pallas_call(reduce_kernel, out_shape=[shape((own_m, MODEL_WIDTH), F32)...  25.4 us

profile of v6, /device:TPU:0, one launch (start us, length us, event | category | flops | bytes accessed | tf_op | source)
XLA Modules:
  0.0 370.0 jit_solution(12879143726461063903)
XLA Ops:
  0.6 0.7 fusion
  1.3 0.1 select_reduce_fusion
  1.4 1.3 fusion.2
  4.0 1.3 fusion.1
  6.6 0.6 pad_add_fusion.meta
  7.2 234.1 %shard_map.165 = (bf16[2,1024,3072]{2,1,0:T(8,128)(2,1)}, bf16[2,1024,1024]{2,1,0:T(8,128)(2,1)}, bf16[2,1024,5632]{2,1,0:T(8,128)(2,1)}, bf16[2,2816,1024]{2,1,...) custom-call(s32[34]{0:T(128)} %pad_add_fusion.meta, ...), custom_call_target="tpu_custom_call" | custom-call | tf_op jit(solution)/shard_map/pallas_call | solution.py:1176
  241.4 96.5 %shard_map.166 = (bf16[256,1024]{1,0:T(8,128)(2,1)}, bf16[96,256]{1,0:T(8,128)(2,1)}, bf16[16,1024]{1,0:T(8,128)(2,1)}, bf16[4,16,768]{2,1,0:T(8,128)(2,1)}, bf1...) custom-call(s32[34]{0:T(128)} %pad_add_fusion.meta, ...), custom_call_target="tpu_custom_call" | custom-call | flops 16384000000 | bytes 94371840 | tf_op jit(solution)/shard_map/pallas_call | solution.py:776
  337.9 25.4 %shard_map.167 = (f32[48,1024]{1,0:T(8,128)}, f32[8,4096]{1,0:T(8,128)}, f32[128,672]{1,0:T(8,128)}, bf16[2,256,1024]{2,1,0:T(8,128)(2,1)}) custom-call(bf16[96,256]{1,0:T(8,128)(2,1)} %get-tuple-element.94.gm0, bf16[16,1024]{1,0:T(8,128)(2,1)} %get-tuple-element.95.gh0, bf16[4,16,768]{2,1,0:T(8,128)(2,1)} %get-tuple-element.96.gp0, ...), custom_call_target="tpu_custom_call" | custom-call | tf_op jit(solution)/shard_map/pallas_call | solution.py:1336
  363.3 0.0 copy-start
  363.3 1.6 slice_bitcast_fusion
  364.9 1.9 copy.21
  366.8 2.3 copy.24
  369.1 0.0 copy-done
  369.1 0.7 copy.25
Async XLA Ops:
  363.3 5.8 %copy-start = (f32[48,1024]{1,0:T(8,128)S(1)}, f32[48,1024]{1,0:T(8,128)}, u32[]{:S(2)}) copy-start(f32[48,1024]{1,0:T(8,128)} %get-tuple-element.103) | copy-start | bytes 589828

commit v7 on v6

--- a/solution.py
+++ b/solution.py
@@ -1412,12 +1412,13 @@
     adapter_choice_per_seq,
 ):
     first = lax.axis_index("section") == 0
-    mine = lambda a: jnp.where(first, a[0], a[1])
-    order = mine(dealt_block_order)[0]
+    told = jnp.concatenate([dealt_block_order[:, 0], adapter_choice_per_seq, lengths], axis=1)
+    told = jnp.where(first, told[0], told[1])
+    order = told[:-2]
     n_blocks = order.shape[0]
     at = jnp.arange(n_blocks, dtype=jnp.int32)
     inverse = jnp.sum(at[:, None] * (order[:, None] == at[None, :]).astype(jnp.int32), axis=0)
-    meta = jnp.concatenate([order, inverse, mine(adapter_choice_per_seq), mine(lengths)])
+    meta = jnp.concatenate([order, inverse, told[-2:]])
     n_dp = lax.axis_size("dp")
     own_kernels = n_dp == 4 and lax.axis_size("seq") == 4
     shards = [mixer_input_weight, mixer_output_weight, feedforward_input_weight, feedforward_output_weight]

time: 375 us -> 372 us (level)
  no operation moved by 1% of the time
where the time goes in v7:
time: 372 us; the launch traced here: 366 us
  Pallas kernels  356 us (96%)
  local copies, waits for them, and re-layouts  7.99 us (2%)
    pallas_call x1, Pallas kernels, forward_model(): pl.pallas_call(functools.partial(model_kernel, n_blocks), out_shape=outs,...  234 us
    pallas_call x1, Pallas kernels, backward(): pl.pallas_call(functools.partial(backward_kernel, n_blocks), out_shape=[j...  96.5 us
    pallas_call x1, Pallas kernels, reduce_gradients(): pl.pallas_call(reduce_kernel, out_shape=[shape((own_m, MODEL_WIDTH), F32)...  25.4 us

profile of v7, /device:TPU:0, one launch (start us, length us, event | category | flops | bytes accessed | tf_op | source)
XLA Modules:
  0.0 366.3 jit_solution(4479708971665554930)
XLA Ops:
  0.6 0.7 copy.23
  1.4 0.7 copy.22
  2.1 0.8 pad_add_fusion
  2.9 0.1 slice_bitcast_fusion.1
  3.0 0.1 select_reduce_fusion
  3.0 0.6 pad_add_fusion.1.meta
  3.6 234.1 %shard_map.165 = (bf16[2,1024,3072]{2,1,0:T(8,128)(2,1)}, bf16[2,1024,1024]{2,1,0:T(8,128)(2,1)}, bf16[2,1024,5632]{2,1,0:T(8,128)(2,1)}, bf16[2,2816,1024]{2,1,...) custom-call(s32[34]{0:T(128)} %pad_add_fusion.1.meta, ...), custom_call_target="tpu_custom_call" | custom-call | tf_op jit(solution)/shard_map/pallas_call | solution.py:1176
  237.8 96.5 %shard_map.166 = (bf16[256,1024]{1,0:T(8,128)(2,1)}, bf16[96,256]{1,0:T(8,128)(2,1)}, bf16[16,1024]{1,0:T(8,128)(2,1)}, bf16[4,16,768]{2,1,0:T(8,128)(2,1)}, bf1...) custom-call(s32[34]{0:T(128)} %pad_add_fusion.1.meta, ...), custom_call_target="tpu_custom_call" | custom-call | flops 16384000000 | bytes 94371840 | tf_op jit(solution)/shard_map/pallas_call | solution.py:776
  334.3 25.4 %shard_map.167 = (f32[48,1024]{1,0:T(8,128)}, f32[8,4096]{1,0:T(8,128)}, f32[128,672]{1,0:T(8,128)}, bf16[2,256,1024]{2,1,0:T(8,128)(2,1)}) custom-call(bf16[96,256]{1,0:T(8,128)(2,1)} %get-tuple-element.94.gm0, bf16[16,1024]{1,0:T(8,128)(2,1)} %get-tuple-element.95.gh0, bf16[4,16,768]{2,1,0:T(8,128)(2,1)} %get-tuple-element.96.gp0, ...), custom_call_target="tpu_custom_call" | custom-call | tf_op jit(solution)/shard_map/pallas_call | solution.py:1336
  359.7 0.0 copy-start
  359.7 1.6 slice_bitcast_fusion
  361.3 1.9 copy.25
  363.2 2.3 copy.28
  365.5 0.0 copy-done
  365.5 0.7 copy.29
  (2 shorter events, 0.0 us)
Async XLA Ops:
  359.7 5.8 %copy-start = (f32[48,1024]{1,0:T(8,128)S(1)}, f32[48,1024]{1,0:T(8,128)}, u32[]{:S(2)}) copy-start(f32[48,1024]{1,0:T(8,128)} %get-tuple-element.103) | copy-start | bytes 589828

commit v8 on v7

--- a/solution.py
+++ b/solution.py
@@ -436,9 +436,12 @@
                 c = loc.start(kept[layer][list(acts).index(name)], acts[name])
             on_the_way[layer][name] = c
 
+    barrier = pltpu.get_barrier_semaphore()
+    for k in range(1, HEADS):
+        pl.semaphore_signal(barrier, inc=1, device_id={"seq": me ^ k}, device_id_type=MESH)
     fetch(1, "d", "au", "dn", "ah", "fo", "gu")
-    greet_peers(me)
     fetch(1, "fi", "am", "mid", "mo", "og", "mix", "f2", "b", "gl", "yh", "rh", "qkv", "st", "ao", "af", "mi", "f1", "ad", "h")
+    pl.semaphore_wait(barrier, HEADS - 1)
     finish = None
     for layer in (1, 0):
         def arrive(*names, layer=layer):
@@ -1319,7 +1322,9 @@
         c.wait_recv()
     for q in range(HEADS):
         m_out[:, q * em.shape[2] : (q + 1) * em.shape[2]] = em[q]
-        h_out[:, q * eh.shape[2] : (q + 1) * eh.shape[2]] = eh[q]
+        start = q * eh.shape[2]
+        wide = min(eh.shape[2], h_out.shape[1] - start)
+        h_out[:, start : start + wide] = eh[q, :, 0:wide]
     for c in copies + last:
         c.wait_send()
     ends_own.wait()
@@ -1337,7 +1342,7 @@
         reduce_kernel,
         out_shape=[
             shape((own_m, MODEL_WIDTH), F32),
-            shape((own_h, HEADS * gh.shape[1]), F32),
+            shape((own_h, VALUE_WIDTH + HIDDEN_UNITS), F32),
             shape((ADAPTER_COLUMNS, width), F32),
             shape((2,) + y.shape, y.dtype),
         ],
@@ -1367,7 +1372,7 @@
         ],
         compiler_params=pltpu.CompilerParams(collective_id=5, has_side_effects=True, vmem_limit_bytes=VMEM_LIMIT),
     )(*early, *late, entry, y)
-    return model.T, hidden[:, : VALUE_WIDTH + HIDDEN_UNITS].T, up, ends
+    return model.T, hidden.T, up, ends
 
 
 def plain_reduce(early, late, n_dp):

time: 372 us -> 371 us (level)
  no operation moved by 1% of the time
where the time goes in v8:
time: 371 us; the launch traced here: 366 us
  Pallas kernels  356 us (96%)
  local copies, waits for them, and re-layouts  7.09 us (2%)
    pallas_call x1, Pallas kernels, forward_model(): pl.pallas_call(functools.partial(model_kernel, n_blocks), out_shape=outs,...  234 us
    pallas_call x1, Pallas kernels, backward(): pl.pallas_call(functools.partial(backward_kernel, n_blocks), out_shape=[j...  96.5 us
    pallas_call x1, Pallas kernels, reduce_gradients(): pl.pallas_call(reduce_kernel, out_shape=[shape((own_m, MODEL_WIDTH), F32)...  25.4 us

profile of v8, /device:TPU:0, one launch (start us, length us, event | category | flops | bytes accessed | tf_op | source)
XLA Modules:
  0.0 365.5 jit_solution(14751579777800805932)
XLA Ops:
  0.6 0.7 copy.23
  1.4 0.7 copy.22
  2.1 0.8 pad_add_fusion
  2.9 0.1 slice_bitcast_fusion
  3.0 0.1 select_reduce_fusion
  3.0 0.6 pad_add_fusion.1.meta
  3.6 234.2 %shard_map.165 = (bf16[2,1024,3072]{2,1,0:T(8,128)(2,1)}, bf16[2,1024,1024]{2,1,0:T(8,128)(2,1)}, bf16[2,1024,5632]{2,1,0:T(8,128)(2,1)}, bf16[2,2816,1024]{2,1,...) custom-call(s32[34]{0:T(128)} %pad_add_fusion.1.meta, ...), custom_call_target="tpu_custom_call" | custom-call | tf_op jit(solution)/shard_map/pallas_call | solution.py:1179
  237.8 96.5 %shard_map.166 = (bf16[256,1024]{1,0:T(8,128)(2,1)}, bf16[96,256]{1,0:T(8,128)(2,1)}, bf16[16,1024]{1,0:T(8,128)(2,1)}, bf16[4,16,768]{2,1,0:T(8,128)(2,1)}, bf1...) custom-call(s32[34]{0:T(128)} %pad_add_fusion.1.meta, ...), custom_call_target="tpu_custom_call" | custom-call | flops 16384000000 | bytes 94371840 | tf_op jit(solution)/shard_map/pallas_call | solution.py:779
  334.3 25.4 %shard_map.167 = (f32[48,1024]{1,0:T(8,128)}, f32[8,3840]{1,0:T(8,128)}, f32[128,672]{1,0:T(8,128)}, bf16[2,256,1024]{2,1,0:T(8,128)(2,1)}) custom-call(bf16[96,256]{1,0:T(8,128)(2,1)} %get-tuple-element.94.gm0, bf16[16,1024]{1,0:T(8,128)(2,1)} %get-tuple-element.95.gh0, bf16[4,16,768]{2,1,0:T(8,128)(2,1)} %get-tuple-element.96.gp0, ...), custom_call_target="tpu_custom_call" | custom-call | tf_op jit(solution)/shard_map/pallas_call | solution.py:1341
  359.8 0.0 copy-start
  359.8 0.0 copy-start.1
  359.8 1.9 copy.25
  361.8 2.3 copy.29
  364.0 0.0 copy-done
  364.0 0.7 copy.30
  364.7 0.0 copy-done.1
  364.7 0.6 copy.31
  (2 shorter events, 0.0 us)
Async XLA Ops:
  359.8 4.2 %copy-start = (f32[48,1024]{1,0:T(8,128)S(1)}, f32[48,1024]{1,0:T(8,128)}, u32[]{:S(2)}) copy-start(f32[48,1024]{1,0:T(8,128)} %get-tuple-element.103) | copy-start | bytes 589828
  359.8 4.9 %copy-start.1 = (f32[8,3840]{1,0:T(8,128)S(1)}, f32[8,3840]{1,0:T(8,128)}, u32[]{:S(2)}) copy-start(f32[8,3840]{1,0:T(8,128)} %get-tuple-element.104) | copy-start | bytes 368644
